TPU v7x, 32 devices: a whole 2x2x4 slice. The times are simulated.
32 devices in a mesh: space: 8 (over y, x, core), filt: 4 (over z).
Axes of the slice: x: 2, y: 2, z: 4, core: 2. Of those that a mesh axis runs over, the one named last changes fastest.
Arguments:
- volume: bfloat16 [4, 32, 64, 512], P(None, 'space', 'filt'), may hold values from -6 to 6
- stem_weight: bfloat16 [27, 4, 32], replicated, may hold values from -0.625 to 0.625
- middle_weight: bfloat16 [27, 32, 64], P(None, None, 'filt'), may hold values from -0.21875 to 0.21875
- cotangent: bfloat16 [64, 8, 16, 128], P('filt', 'space'), may hold values from -6 to 6
Outputs:
- features: bfloat16 [64, 8, 16, 128], P('filt', 'space')
- middle_gradient: float32 [27, 32, 64], P(None, None, 'filt')
- stem_gradient: float32 [27, 4, 32], replicated
All inputs are finite; a program needn't handle non-finite values.
Results may differ from a plain program's by a relative error of at most 0.019.
Values may be sent and summed in bfloat16 or wider, within the bound.
No kernel may reach another device: no remote copies, remote signals or barrier semaphores. Data moves between devices by JAX's collectives and lax.ppermute only.
A program may use at most 64 MiB of HBM per device.

v0:
```python
import functools
import math

import jax
import jax.numpy as jnp
import numpy as np
from jax import lax
from jax.experimental import pallas as pl
from jax.experimental.pallas import tpu as pltpu
from jax.sharding import PartitionSpec as P

F32 = jnp.float32
BF16 = jnp.bfloat16
LANES = 128
STEM_ROWS = 288


def nn(a, b):
    return lax.dot_general(a, b, (((1,), (0,)), ((), ())), preferred_element_type=F32)


def nt(a, b):
    return lax.dot_general(a, b, (((1,), (1,)), ((), ())), preferred_element_type=F32)


def place_table():
    table = np.zeros((2, LANES, STEM_ROWS), np.float32)
    for even_odd in range(2):
        for a in range(3):
            for b in range(3):
                for d in range(3):
                    q = 2 * even_odd + d - 1
                    shifted, phase = (1, 3) if q < 0 else (0, q)
                    for c in range(4):
                        column = 96 * a + 48 * shifted + 16 * b + 4 * phase + c
                        table[even_odd, 4 * (9 * a + 3 * b + d) + c, column] = 1.0
    return table


def rows_lanes(shape):
    return lax.broadcasted_iota(jnp.int32, shape, 0), lax.broadcasted_iota(jnp.int32, shape, 1)


def regroup_kernel(volume, own, slab_x, slab_y, corner):
    channels, planes, width, depth = volume.shape
    z, column = rows_lanes((depth, depth))
    select = (z == 4 * (column & (LANES - 1)) + (column // LANES)).astype(F32).astype(BF16)
    row, column = rows_lanes((16 * width, 16 * width))
    turn = ((row & 15) * 16 + (row // 16) == column).astype(F32).astype(BF16)
    picked = nn(volume[...].reshape(channels * planes * width, depth), select).astype(BF16)
    for x in range(planes):
        parts = []
        for phase in range(4):
            for c in range(channels):
                start = (c * planes + x) * width
                parts.append(picked[start : start + width, phase * LANES : (phase + 1) * LANES])
        plane = nn(turn, jnp.concatenate(parts, axis=0)).astype(BF16)
        own[x] = plane
        slab_y[x] = plane[-48:]
        if x > 0:
            slab_x[x - 1] = plane
            corner[x - 1] = plane[-48:]


def softplus_sigmoid(values):
    small = jnp.exp(-jnp.abs(values))
    inverse = 1.0 / (1.0 + small)
    soft = jnp.maximum(values, 0.0) + jnp.log(1.0 + small)
    return soft, jnp.where(values >= 0.0, inverse, small * inverse)


def roll_lanes(values, amount):
    lane = lax.broadcasted_iota(jnp.int32, values.shape, 1)
    edge = 0 if amount == 1 else LANES - 1
    rolled = pltpu.roll(values, amount % LANES, 1)
    return jnp.where(lane == edge, 0.0, rolled)


def main_kernel(
    own, slab_x, slab_y, corner, stem_w, place, gathered, features, slots, cols, mid_cols, slope, stem_back, odd_cols,
):
    blocks = gathered.shape[0]
    keep_x = jnp.where(lax.axis_index("space") > 0, 1.0, 0.0).astype(F32)
    keep_y = jnp.where(lax.axis_index("filt") > 0, 1.0, 0.0).astype(F32)

    for x in range(7):
        low = corner[x] if x < 3 else slab_y[x - 3]
        high = slab_x[x] if x < 3 else own[x - 3]
        plane = jnp.concatenate([low, high], axis=0)
        shifted = roll_lanes(plane.astype(F32), 1).astype(BF16)
        for j in range(9):
            lanes = pl.ds(j * LANES, LANES)
            cols[x, 0:48, lanes] = plane[32 * j : 32 * j + 48]
            cols[x, 48:96, lanes] = shifted[32 * j : 32 * j + 48]

    weights = jnp.concatenate([nn(stem_w[...], place[0]), nn(stem_w[...], place[1])], axis=0).astype(BF16)
    for i in range(3):
        pre = nn(weights, cols[2 * i : 2 * i + 3].reshape(STEM_ROWS, 9 * LANES))
        soft, sig = softplus_sigmoid(pre)
        act = 0.3 * pre + 0.7 * soft
        lean = 0.3 + 0.7 * sig
        keep = jnp.where(lax.broadcasted_iota(jnp.int32, pre.shape, 1) < LANES, keep_y, 1.0)
        if i == 0:
            keep = keep * keep_x
        slope[i] = lean * keep
        act = act * keep
        for j in range(9):
            even = act[0:32, j * LANES : (j + 1) * LANES]
            odd = act[32:64, j * LANES : (j + 1) * LANES]
            for d, part in ((0, roll_lanes(odd, 1)), (1, even), (2, odd)):
                part = part.astype(BF16)
                for b in range(3):
                    if (j - b) % 2 == 0 and 0 <= (j - b) // 2 < 4:
                        row = 32 * (9 * i + 3 * b + d)
                        mid_cols[row : row + 32, pl.ds((j - b) // 2 * LANES, LANES)] = part

    mid_w = gathered[:, :, 0:896].reshape(blocks * 16, 896)
    cotangent = gathered[:, :, 896:1408].reshape(blocks * 16, 512)
    pre = nn(mid_w[:, 0:864], mid_cols[...])
    soft, sig = softplus_sigmoid(pre)
    features[...] = (0.3 * pre + 0.7 * soft).astype(BF16).reshape(features.shape)
    delta = cotangent.astype(F32) * (0.3 + 0.7 * sig)
    delta_low = delta.astype(BF16)
    mid_grad = nt(delta_low, mid_cols[...])

    turned = jnp.concatenate(
        [mid_w[:, t * LANES : (t + 1) * LANES].astype(F32).T for t in range(7)], axis=0
    ).astype(BF16)
    zero = jnp.zeros((32, blocks * 16), BF16)

    def block(a, b, d):
        row = 32 * (9 * a + 3 * b + d)
        return turned[row : row + 32]

    def wide(a, b):
        even = jnp.concatenate([block(a, b, 1), zero], axis=1)
        odd = jnp.concatenate([block(a, b, 2), block(a, b, 0)], axis=1)
        return jnp.concatenate([even, odd], axis=0)

    both = jnp.concatenate(
        [delta_low]
        + [
            jnp.concatenate(
                [roll_lanes(delta[:, j * LANES : (j + 1) * LANES], -1) for j in range(4)], axis=1
            ).astype(BF16)
        ],
        axis=0,
    )
    nothing = jnp.zeros((2 * blocks * 16, LANES), BF16)
    pair = jnp.concatenate(
        [jnp.concatenate([both, nothing], axis=1), jnp.concatenate([nothing, both], axis=1)], axis=0
    )
    stem_grad = jnp.zeros((64, STEM_ROWS), F32)
    for i in range(3):
        odd_back = nn(wide(i, 1), both)
        even_back = nn(jnp.concatenate([wide(i, 0), wide(i, 2)], axis=1), pair)
        for j in range(9):
            source = even_back if j % 2 == 0 else odd_back
            part = source[:, (j // 2) * LANES : (j // 2 + 1) * LANES]
            lanes = pl.ds(j * LANES, LANES)
            stem_back[i, :, lanes] = (part * slope[i, :, lanes]).astype(BF16)
        stem_grad += nt(stem_back[i], cols[2 * i : 2 * i + 3].reshape(STEM_ROWS, 9 * LANES))
    high = stem_grad.astype(BF16)
    low = (stem_grad - high.astype(F32)).astype(BF16)
    taken = sum(
        nt(part[32 * e : 32 * e + 32], place[e]) for part in (high, low) for e in range(2)
    )
    high = taken.astype(BF16)
    low = (taken - high.astype(F32)).astype(BF16)

    mid_low = mid_grad.astype(BF16)
    mid_low = jnp.concatenate([mid_low, jnp.zeros((blocks * 16, 32), BF16)], axis=1)
    per = slots.shape[2]
    pieces = 11
    for f in range(blocks):
        for u in range(slots.shape[0] * per):
            if u < 7:
                value = mid_low[16 * f : 16 * f + 16, u * LANES : (u + 1) * LANES]
            elif u < pieces:
                value = (high, low)[(u - 7) // 2][16 * ((u - 7) % 2) : 16 * ((u - 7) % 2) + 16]
            else:
                value = jnp.zeros((16, LANES), BF16)
            slots[u // per, f, u % per] = value


def whole(count):
    return [pl.BlockSpec(memory_space=pltpu.VMEM)] * count


def body(volume, stem_weight, middle_weight, cotangent):
    spaces, filts = lax.axis_size("space"), lax.axis_size("filt")
    channels, planes, width, depth = volume.shape
    stem_cells = (planes // 2) * spaces * (width // 2) * filts * (depth // 2)
    middle_cells = stem_cells // 8
    limit = pltpu.CompilerParams(vmem_limit_bytes=48 * 1024 * 1024)

    mid_w = middle_weight.transpose(2, 0, 1).reshape(16, 864)
    mid_w = jnp.pad(mid_w, ((0, 0), (0, 32)))
    cot = cotangent.reshape(16, filts, 512).transpose(1, 0, 2)
    packed = jnp.concatenate([jnp.broadcast_to(mid_w[None], (filts, 16, 896)), cot], axis=2)
    gathered = lax.all_to_all(packed, "filt", 0, 0, tiled=True)

    own, slab_x, slab_y, corner = pl.pallas_call(
        regroup_kernel,
        out_shape=[
            jax.ShapeDtypeStruct((planes, 16 * width, LANES), BF16),
            jax.ShapeDtypeStruct((planes - 1, 16 * width, LANES), BF16),
            jax.ShapeDtypeStruct((planes, 48, LANES), BF16),
            jax.ShapeDtypeStruct((planes - 1, 48, LANES), BF16),
        ],
        in_specs=whole(1),
        out_specs=whole(4),
        compiler_params=limit,
        name="regroup",
    )(volume)
    route_x = [(s - 1, s) for s in range(1, spaces)]
    route_y = [(f - 1, f) for f in range(1, filts)]
    route_xy = [
        ((s - 1) * filts + f - 1, s * filts + f) for s in range(1, spaces) for f in range(1, filts)
    ]
    slab_x = lax.ppermute(slab_x, "space", route_x)
    slab_y = lax.ppermute(slab_y, "filt", route_y)
    corner = lax.ppermute(corner, ("space", "filt"), route_xy)

    stem_w = jnp.pad(stem_weight.reshape(108, 32).T, ((0, 0), (0, 20)))
    place = jnp.asarray(place_table(), BF16)
    per = -(-11 // spaces)
    features, slots = pl.pallas_call(
        main_kernel,
        out_shape=[
            jax.ShapeDtypeStruct((filts, 16, 512), BF16),
            jax.ShapeDtypeStruct((spaces, filts, per, 16, LANES), BF16),
        ],
        in_specs=whole(7),
        out_specs=whole(2),
        scratch_shapes=[
            pltpu.VMEM((7, 96, 9 * LANES), BF16),
            pltpu.VMEM((864, 512), BF16),
            pltpu.VMEM((3, 64, 9 * LANES), F32),
            pltpu.VMEM((3, 64, 9 * LANES), BF16),
            pltpu.VMEM((8, LANES), F32),
        ],
        compiler_params=limit,
        name="sections",
    )(own, slab_x, slab_y, corner, stem_w, place, gathered)

    features = lax.all_to_all(features, "filt", 0, 0, tiled=True)
    features = features.transpose(1, 0, 2).reshape(16, 1, 4 * filts, LANES)

    slots = slots.reshape(spaces * filts, per, 16, LANES)
    parts = lax.all_to_all(slots, ("space", "filt"), 0, 0, tiled=True)
    total = parts.astype(F32).sum(0)
    total = lax.all_to_all(
        jnp.broadcast_to(total[None], (spaces, per, 16, LANES)), "space", 0, 0, tiled=True
    ).reshape(spaces * per, 16, LANES)
    middle = total[:7].transpose(1, 0, 2).reshape(16, 896)[:, :864] / math.sqrt(middle_cells)
    middle = middle.reshape(16, 27, 32).transpose(1, 2, 0)
    stem = (total[7:9] + total[9:11]).reshape(32, LANES)[:, :108] / math.sqrt(stem_cells)
    stem = stem.T.reshape(27, 4, 32)
    return features, middle, stem


def solution(mesh):
    in_specs = (
        P(None, "space", "filt", None),
        P(),
        P(None, None, "filt"),
        P("filt", "space", None, None),
    )
    out_specs = (P("filt", "space", None, None), P(None, None, "filt"), P())
    return jax.shard_map(body, mesh=mesh, in_specs=in_specs, out_specs=out_specs, check_vma=False)
```

profile of v0, /device:TPU:0, one launch (start us, length us, event | category | flops | bytes accessed | tf_op | source)
XLA Modules:
  0.0 60.0 jit_solution(12179508233618535437)
XLA Ops:
  0.6 0.0 copy-start.2
  0.6 0.9 %reshape.40 = bf16[16,4,512]{2,1,0:T(4,128)(2,1)S(1)} reshape(bf16[16,1,16,128]{3,2,1,0:T(8,128)(2,1)} %param.8) | data formatting | bytes 131072 | tf_op jit(solution)/shard_map/reshape | solution.py:199
  1.6 0.0 copy-done.2
  1.6 0.2 reshape.39
  1.8 0.7 %pad_maximum_fusion = bf16[4,16,1408]{2,1,0:T(8,128)(2,1)} fusion(bf16[4,16,512]{2,1,0:T(8,128)(2,1)S(1)} %bitcast.26, bf16[4,16,896]{2,1,0:T(8,128)(2,1)S(1)} %broadcast_in_dim.4), kind=kLoop, calls=%fused_computation.1 | loop fusion | flops 360448 | bytes 360448 | tf_op jit(solution)/shard_map/concatenate | solution.py:200
  2.5 0.0 copy-start
  2.5 6.4 %all-to-all-start = ((bf16[4,16,1408]{2,1,0:T(8,128)(2,1)}), bf16[4,16,1408]{2,1,0:T(8,128)(2,1)S(1)}, u32[]{:S(2)}, u32[]{:S(2)}) async-start(bf16[4,16,1408]{2,1,0:T(8,128)(2,1)} %pad_maximum_fusion), calls=%async_computation | async-start | bytes 360448 | tf_op jit(solution)/shard_map/all_to_all | solution.py:201
  9.0 0.0 copy-done
  9.0 0.0 copy-start.3
  9.0 0.0 copy-start.1
  9.0 0.6 regroup.1
  9.6 1.5 %collective-permute-start = (bf16[3,256,128]{2,1,0:T(8,128)(2,1)S(1)}, bf16[3,256,128]{2,1,0:T(8,128)(2,1)S(1)}, u32[]{:S(2)}, u32[]{:S(2)}) collective-permute-start(bf16[3,256,128]{2,1,0:T(8,128)(2,1)S(1)} %get-tuple-element.10), channel_id=1, source_target_pairs={{0,4},{4,8},{8,12},{12,16},{16,20},{20,24},{24,28},{1,5},{5,9},{9,... | collective-permute-start | bytes 589832 | tf_op jit(solution)/shard_map/ppermute | solution.py:221
  11.0 3.8 %collective-permute-start.1 = (bf16[4,48,128]{2,1,0:T(8,128)(2,1)S(1)}, bf16[4,48,128]{2,1,0:T(8,128)(2,1)S(1)}, u32[]{:S(2)}, u32[]{:S(2)}) collective-permute-start(bf16[4,48,128]{2,1,0:T(8,128)(2,1)S(1)} %get-tuple-element.11), channel_id=1, source_target_pairs={{0,1},{1,2},{2,3},{4,5},{5,6},{6,7},{8,9},{9,10},{10,11},{12,13},{... | collective-permute-start | bytes 147464 | tf_op jit(solution)/shard_map/ppermute | solution.py:222
  14.8 4.9 %collective-permute-start.2 = (bf16[3,48,128]{2,1,0:T(8,128)(2,1)S(1)}, bf16[3,48,128]{2,1,0:T(8,128)(2,1)S(1)}, u32[]{:S(2)}, u32[]{:S(2)}) collective-permute-start(bf16[3,48,128]{2,1,0:T(8,128)(2,1)S(1)} %get-tuple-element.12), channel_id=1, source_target_pairs={{0,5},{1,6},{2,7},{4,9},{5,10},{6,11},{8,13},{9,14},{10,15},{12,17... | collective-permute-start | bytes 110600 | tf_op jit(solution)/shard_map/ppermute | solution.py:223
  19.7 0.0 copy-done.3
  19.8 0.1 copy.9
  19.8 1.5 %collective-permute-done.2.corner = bf16[3,48,128]{2,1,0:T(8,128)(2,1)S(1)} collective-permute-done((bf16[3,48,128]{2,1,0:T(8,128)(2,1)S(1)}, bf16[3,48,128]{2,1,0:T(8,128)(2,1)S(1)}, u32[]{:S(2)}, u32[]{:S(2)}) %collective-permute-start.2) | collective-permute-done | bytes 36896 | tf_op jit(solution)/shard_map/ppermute | solution.py:223
  21.3 0.0 collective-permute-done.1.slab_y
  21.3 0.0 collective-permute-done.slab_x
  21.3 0.0 all-to-all-done.gathered
  21.3 0.0 copy-done.1
  21.4 3.5 %sections.1 = (bf16[4,16,512]{2,1,0:T(8,128)(2,1)}, bf16[8,4,2,16,128]{4,3,2,1,0:T(8,128)(2,1)S(1)}) custom-call(bf16[4,256,128]{2,1,0:T(8,128)(2,1)S(1)} %get-tuple-element.9.own, bf16[3,256,128]{2,1,0:T(8,128)(2,1)S(1)} %collective-permute-done.slab_x, bf16[4,48,128]{2,1,0:T(8,128)(2,1)S(1)} %collective-permute-done.1.slab_y, ...), custom_call_target="tpu_custom_call" | custom-call | tf_op jit(solution)/shard_map/sections/pallas_call | solution.py:228
  24.8 14.9 %all_to_all.20 = bf16[32,2,16,128]{3,2,1,0:T(8,128)(2,1)S(1)} all-to-all(bf16[32,2,16,128]{3,2,1,0:T(8,128)(2,1)S(1)} %bitcast.21), channel_id=1, replica_groups=mesh['space'=8,'filt'=4] {'space','filt'}, dimensions={0} | all-to-all | bytes 524288 | tf_op jit(solution)/shard_map/all_to_all | solution.py:251
  39.8 3.3 %all-to-all-start.1 = ((bf16[4,16,512]{2,1,0:T(8,128)(2,1)}), bf16[4,16,512]{2,1,0:T(8,128)(2,1)S(1)}, u32[]{:S(2)}, u32[]{:S(2)}) async-start(bf16[4,16,512]{2,1,0:T(8,128)(2,1)} %get-tuple-element.13), calls=%async_computation.1 | async-start | bytes 131072 | tf_op jit(solution)/shard_map/all_to_all | solution.py:247
  43.1 5.7 %all-to-all-done.1 = bf16[4,16,512]{2,1,0:T(8,128)(2,1)S(1)} async-done(((bf16[4,16,512]{2,1,0:T(8,128)(2,1)}), bf16[4,16,512]{2,1,0:T(8,128)(2,1)S(1)}, u32[]{:S(2)}, u32[]{:S(2)}) %all-to-all-start.1) | async-done | bytes 65568 | tf_op jit(solution)/shard_map/all_to_all | solution.py:247
  48.8 0.7 %broadcast_in_dim.5 = f32[8,2,16,128]{3,2,1,0:T(8,128)} broadcast(f32[2,16,128]{2,1,0:T(8,128)S(1)} %convert_reduce_fusion), dimensions={1,2,3} | broadcast | bytes 147456 | tf_op jit(solution)/shard_map/broadcast_in_dim | solution.py:254
  49.4 3.4 %all-to-all-start.3 = ((f32[8,2,16,128]{3,2,1,0:T(8,128)}), f32[8,2,16,128]{3,2,1,0:T(8,128)S(1)}, u32[]{:S(2)}, u32[]{:S(2)}) async-start(f32[8,2,16,128]{3,2,1,0:T(8,128)} %broadcast_in_dim.5), calls=%async_computation.3 | async-start | bytes 262144 | tf_op jit(solution)/shard_map/all_to_all | solution.py:253
  52.8 0.1 copy.12
  52.9 0.7 %reshape.41 = bf16[16,1,16,128]{3,2,0,1:T(8,128)(2,1)} reshape(bf16[16,4,512]{2,1,0:T(4,128)(2,1)S(1)} %copy.12) | data formatting | bytes 131072 | tf_op jit(solution)/shard_map/reshape | solution.py:248
  53.5 4.7 %all-to-all-done.3 = f32[8,2,16,128]{3,2,1,0:T(8,128)S(1)} async-done(((f32[8,2,16,128]{3,2,1,0:T(8,128)}), f32[8,2,16,128]{3,2,1,0:T(8,128)S(1)}, u32[]{:S(2)}, u32[]{:S(2)}) %all-to-all-start.3) | async-done | bytes 131104 | tf_op jit(solution)/shard_map/all_to_all | solution.py:253
  58.3 0.1 copy.14
  58.4 0.6 %reshape.47 = f32[27,4,32]{2,1,0:T(4,128)} reshape(f32[108,32]{1,0:T(8,128)S(1)} %copy.14) | data formatting | bytes 27648 | tf_op jit(solution)/shard_map/reshape | solution.py:259
  59.1 0.1 reshape.45
  59.2 0.8 %copy.16 = f32[27,32,16]{1,2,0:T(8,128)} copy(f32[27,32,16]{1,0,2:T(8,128)S(1)} %bitcast.22) | data formatting | bytes 110592
  (11 shorter events, 0.2 us)
Async XLA Ops:
  0.6 0.9 %copy-start.2 = (bf16[27,32,16]{1,2,0:T(8,128)(2,1)S(1)}, bf16[27,32,16]{1,2,0:T(8,128)(2,1)}, u32[]{:S(2)}) copy-start(bf16[27,32,16]{1,2,0:T(8,128)(2,1)} %param.7) | copy-start | bytes 82948
  2.5 6.5 %copy-start = (bf16[4,4,16,512]{3,2,1,0:T(8,128)(2,1)S(1)}, bf16[4,4,16,512]{3,2,1,0:T(8,128)(2,1)}, u32[]{:S(2)}) copy-start(bf16[4,4,16,512]{3,2,1,0:T(8,128)(2,1)} %volume.1) | copy-start | bytes 786436
  2.5 18.8 %all-to-all-start = ((bf16[4,16,1408]{2,1,0:T(8,128)(2,1)}), bf16[4,16,1408]{2,1,0:T(8,128)(2,1)S(1)}, u32[]{:S(2)}, u32[]{:S(2)}) async-start(bf16[4,16,1408]{2,1,0:T(8,128)(2,1)} %pad_maximum_fusion), calls=%async_computation | async-start | bytes 360448 | tf_op jit(solution)/shard_map/all_to_all | solution.py:201
  9.0 10.8 %copy-start.3 = (bf16[27,4,32]{2,1,0:T(4,128)(2,1)S(1)}, bf16[27,4,32]{2,1,0:T(4,128)(2,1)}, u32[]{:S(2)}) copy-start(bf16[27,4,32]{2,1,0:T(4,128)(2,1)} %param.6) | copy-start | bytes 20740
  9.0 12.4 %copy-start.1 = (bf16[2,128,288]{2,1,0:T(8,128)(2,1)S(1)}, bf16[2,128,288]{2,1,0:T(8,128)(2,1)}, u32[]{:S(2)}) copy-start(bf16[2,128,288]{2,1,0:T(8,128)(2,1)} %constant.13.clone.place) | copy-start | bytes 442372
  9.6 11.8 %collective-permute-start = (bf16[3,256,128]{2,1,0:T(8,128)(2,1)S(1)}, bf16[3,256,128]{2,1,0:T(8,128)(2,1)S(1)}, u32[]{:S(2)}, u32[]{:S(2)}) collective-permute-start(bf16[3,256,128]{2,1,0:T(8,128)(2,1)S(1)} %get-tuple-element.10), channel_id=1, source_target_pairs={{0,4},{4,8},{8,12},{12,16},{16,20},{20,24},{24,28},{1,5},{5,9},{9,... | collective-permute-start | bytes 589832 | tf_op jit(solution)/shard_map/ppermute | solution.py:221
  11.0 10.3 %collective-permute-start.1 = (bf16[4,48,128]{2,1,0:T(8,128)(2,1)S(1)}, bf16[4,48,128]{2,1,0:T(8,128)(2,1)S(1)}, u32[]{:S(2)}, u32[]{:S(2)}) collective-permute-start(bf16[4,48,128]{2,1,0:T(8,128)(2,1)S(1)} %get-tuple-element.11), channel_id=1, source_target_pairs={{0,1},{1,2},{2,3},{4,5},{5,6},{6,7},{8,9},{9,10},{10,11},{12,13},{... | collective-permute-start | bytes 147464 | tf_op jit(solution)/shard_map/ppermute | solution.py:222
  14.8 6.5 %collective-permute-start.2 = (bf16[3,48,128]{2,1,0:T(8,128)(2,1)S(1)}, bf16[3,48,128]{2,1,0:T(8,128)(2,1)S(1)}, u32[]{:S(2)}, u32[]{:S(2)}) collective-permute-start(bf16[3,48,128]{2,1,0:T(8,128)(2,1)S(1)} %get-tuple-element.12), channel_id=1, source_target_pairs={{0,5},{1,6},{2,7},{4,9},{5,10},{6,11},{8,13},{9,14},{10,15},{12,17... | collective-permute-start | bytes 110600 | tf_op jit(solution)/shard_map/ppermute | solution.py:223
  39.8 9.0 %all-to-all-start.1 = ((bf16[4,16,512]{2,1,0:T(8,128)(2,1)}), bf16[4,16,512]{2,1,0:T(8,128)(2,1)S(1)}, u32[]{:S(2)}, u32[]{:S(2)}) async-start(bf16[4,16,512]{2,1,0:T(8,128)(2,1)} %get-tuple-element.13), calls=%async_computation.1 | async-start | bytes 131072 | tf_op jit(solution)/shard_map/all_to_all | solution.py:247
  49.4 8.8 %all-to-all-start.3 = ((f32[8,2,16,128]{3,2,1,0:T(8,128)}), f32[8,2,16,128]{3,2,1,0:T(8,128)S(1)}, u32[]{:S(2)}, u32[]{:S(2)}) async-start(f32[8,2,16,128]{3,2,1,0:T(8,128)} %broadcast_in_dim.5), calls=%async_computation.3 | async-start | bytes 262144 | tf_op jit(solution)/shard_map/all_to_all | solution.py:253
where the time goes:
time: 60.5 us; the launch traced here: 60 us
  starting transfers between devices  23.2 us (38%)
  blocking collectives  14.9 us (25%)
  waiting for transfers between devices  11.9 us (20%)
  local copies, waits for them, and re-layouts  4.33 us (7%)
  Pallas kernels  4.04 us (7%)
  between operations  0.8 us (1%)
  other arithmetic  0.75 us (1%)
    all_to_all x1, blocking collectives, body(): parts = lax.all_to_all(slots, ('space', 'filt'), 0, 0, tiled=True)  14.9 us
    all_to_all x1, starting transfers between devices, body(): gathered = lax.all_to_all(packed, 'filt', 0, 0, tiled=True)  6.45 us
    all_to_all x1, waiting for transfers between devices, body(): features = lax.all_to_all(features, 'filt', 0, 0, tiled=True)  5.66 us
    ppermute x1, starting transfers between devices, body(): corner = lax.ppermute(corner, ('space', 'filt'), route_xy)  4.91 us
    all_to_all x1, waiting for transfers between devices, body(): lax.all_to_all(jnp.broadcast_to(total[None], (spaces, per, 16, LANES)), '...  4.74 us
    ppermute x1, starting transfers between devices, body(): slab_y = lax.ppermute(slab_y, 'filt', route_y)  3.75 us
    pallas_call x1, Pallas kernels, body(): pl.pallas_call(main_kernel, out_shape=[jax.ShapeDtypeStruct((filts, 16, 5...  3.46 us
    all_to_all x1, starting transfers between devices, body(): lax.all_to_all(jnp.broadcast_to(total[None], (spaces, per, 16, LANES)), '...  3.37 us
  transfers between devices with their start and end apart: 6, of which 3 were waited for; matrix products, arithmetic and copies ran while one was open for 1% of the time, Pallas kernels for 1%

commit v1 on v0

--- a/solution.py
+++ b/solution.py
@@ -1,5 +1,4 @@
 import functools
-import math
 
 import jax
 import jax.numpy as jnp
@@ -41,12 +40,16 @@
     return lax.broadcasted_iota(jnp.int32, shape, 0), lax.broadcasted_iota(jnp.int32, shape, 1)
 
 
-def regroup_kernel(volume, own, slab_x, slab_y, corner):
+def turn_matrix(count):
+    row, column = rows_lanes((count * count, count * count))
+    return ((row % count) * count + (row // count) == column).astype(F32).astype(BF16)
+
+
+def regroup_kernel(volume, weight, cotangent, own, slab_x, packed):
     channels, planes, width, depth = volume.shape
     z, column = rows_lanes((depth, depth))
-    select = (z == 4 * (column & (LANES - 1)) + (column // LANES)).astype(F32).astype(BF16)
-    row, column = rows_lanes((16 * width, 16 * width))
-    turn = ((row & 15) * 16 + (row // 16) == column).astype(F32).astype(BF16)
+    select = (z == 4 * (column % LANES) + (column // LANES)).astype(F32).astype(BF16)
+    turn = turn_matrix(16)
     picked = nn(volume[...].reshape(channels * planes * width, depth), select).astype(BF16)
     for x in range(planes):
         parts = []
@@ -56,10 +59,27 @@
                 parts.append(picked[start : start + width, phase * LANES : (phase + 1) * LANES])
         plane = nn(turn, jnp.concatenate(parts, axis=0)).astype(BF16)
         own[x] = plane
-        slab_y[x] = plane[-48:]
         if x > 0:
             slab_x[x - 1] = plane
-            corner[x - 1] = plane[-48:]
+
+    blank = jnp.zeros((16, 32), BF16)
+    taps = [weight[t] if t < 27 else blank for t in range(28)]
+    turned = nn(turn, cotangent[...].reshape(256, LANES)).astype(BF16)
+    for t in range(7):
+        tile = jnp.concatenate(taps[4 * t : 4 * t + 4], axis=1)
+        for f in range(packed.shape[0]):
+            packed[f, t] = tile
+    for f in range(packed.shape[0]):
+        for j in range(4):
+            row = 16 * (4 * f + j)
+            packed[f, 7 + j] = turned[row : row + 16]
+
+
+def border_kernel(slab_x, own, border):
+    for x in range(3):
+        border[x] = slab_x[x, -48:]
+    for x in range(4):
+        border[3 + x] = own[x, -48:]
 
 
 def softplus_sigmoid(values):
@@ -76,17 +96,28 @@
     return jnp.where(lane == edge, 0.0, rolled)
 
 
-def main_kernel(
-    own, slab_x, slab_y, corner, stem_w, place, gathered, features, slots, cols, mid_cols, slope, stem_back, odd_cols,
-):
+def slot_kinds(spaces):
+    kinds = [("middle", u) for u in range(7)] + [("none", 0)]
+    kinds += [("stem", u) for u in range(4)] + [("features", u) for u in range(4)]
+    return kinds + [("none", 0)] * (-len(kinds) % spaces)
+
+
+def slot_widths(spaces):
+    kinds = [kind for kind, _ in slot_kinds(spaces)]
+    widths = []
+    for t in range(len(kinds) // spaces):
+        mine = kinds[t * spaces : (t + 1) * spaces]
+        widths.append(4 if "features" in mine else 2 if "stem" in mine else 1)
+    return widths
+
+
+def main_kernel(own, slab_x, border, stem_w, place, gathered, slots, cols, mid_w, mid_cols, slope, stem_back):
     blocks = gathered.shape[0]
     keep_x = jnp.where(lax.axis_index("space") > 0, 1.0, 0.0).astype(F32)
     keep_y = jnp.where(lax.axis_index("filt") > 0, 1.0, 0.0).astype(F32)
 
     for x in range(7):
-        low = corner[x] if x < 3 else slab_y[x - 3]
-        high = slab_x[x] if x < 3 else own[x - 3]
-        plane = jnp.concatenate([low, high], axis=0)
+        plane = jnp.concatenate([border[x], slab_x[x] if x < 3 else own[x - 3]], axis=0)
         shifted = roll_lanes(plane.astype(F32), 1).astype(BF16)
         for j in range(9):
             lanes = pl.ds(j * LANES, LANES)
@@ -114,11 +145,19 @@
                         row = 32 * (9 * i + 3 * b + d)
                         mid_cols[row : row + 32, pl.ds((j - b) // 2 * LANES, LANES)] = part
 
-    mid_w = gathered[:, :, 0:896].reshape(blocks * 16, 896)
-    cotangent = gathered[:, :, 896:1408].reshape(blocks * 16, 512)
+    for f in range(blocks):
+        for t in range(7):
+            mid_w[16 * f : 16 * f + 16, t * LANES : (t + 1) * LANES] = gathered[f, t]
+    cotangent = jnp.concatenate(
+        [
+            jnp.concatenate([gathered[f, 7 + j] for j in range(4)], axis=1)
+            for f in range(blocks)
+        ],
+        axis=0,
+    )
     pre = nn(mid_w[:, 0:864], mid_cols[...])
     soft, sig = softplus_sigmoid(pre)
-    features[...] = (0.3 * pre + 0.7 * soft).astype(BF16).reshape(features.shape)
+    features = (0.3 * pre + 0.7 * soft).astype(BF16)
     delta = cotangent.astype(F32) * (0.3 + 0.7 * sig)
     delta_low = delta.astype(BF16)
     mid_grad = nt(delta_low, mid_cols[...])
@@ -170,17 +209,71 @@
 
     mid_low = mid_grad.astype(BF16)
     mid_low = jnp.concatenate([mid_low, jnp.zeros((blocks * 16, 32), BF16)], axis=1)
-    per = slots.shape[2]
-    pieces = 11
+    blank = jnp.zeros((16, LANES), BF16)
+    spaces = slots.shape[0]
     for f in range(blocks):
-        for u in range(slots.shape[0] * per):
-            if u < 7:
-                value = mid_low[16 * f : 16 * f + 16, u * LANES : (u + 1) * LANES]
-            elif u < pieces:
-                value = (high, low)[(u - 7) // 2][16 * ((u - 7) % 2) : 16 * ((u - 7) % 2) + 16]
+        rows = slice(16 * f, 16 * f + 16)
+        for u, (kind, which) in enumerate(slot_kinds(spaces)):
+            lanes = slice(which * LANES, (which + 1) * LANES)
+            if kind == "middle":
+                value = mid_low[rows, lanes]
+            elif kind == "stem":
+                value = (high, low)[which // 2][16 * (which % 2) : 16 * (which % 2) + 16]
+            elif kind == "features":
+                value = features[rows, lanes]
             else:
-                value = jnp.zeros((16, LANES), BF16)
-            slots[u // per, f, u % per] = value
+                value = blank
+            slots[u % spaces, f, u // spaces] = value
+
+
+def sum_kernel(parts, chunks):
+    spaces = chunks.shape[0]
+    filts = parts.shape[0] // spaces
+    me = lax.axis_index("space")
+    kinds = [kind for kind, _ in slot_kinds(spaces)]
+    base = 0
+    for t, width in enumerate(slot_widths(spaces)):
+        total = jnp.sum(parts[:, t].astype(F32), axis=0)
+        high = total.astype(BF16)
+        tiles = [high]
+        if width > 1:
+            tiles.append((total - high.astype(F32)).astype(BF16))
+        first = kinds.index("features") - t * spaces
+        forward = jnp.logical_and(me >= first, me < first + 4)
+        for s in range(spaces):
+            for k in range(width):
+                if width < 4:
+                    chunks[s, base + k] = tiles[k]
+                    continue
+                here = parts[s * filts + k, t].astype(F32)
+                other = tiles[k].astype(F32) if k < 2 else jnp.zeros_like(here)
+                chunks[s, base + k] = jnp.where(forward, here, other).astype(BF16)
+        base += width
+
+
+def unpack_kernel(middle_scale, stem_scale, chunks, features, middle, stem):
+    spaces = chunks.shape[0]
+    widths = slot_widths(spaces)
+    found = {}
+    for u, (kind, which) in enumerate(slot_kinds(spaces)):
+        found[kind, which] = (u % spaces, sum(widths[: u // spaces]))
+    for t in range(27):
+        s, base = found["middle", t // 4]
+        start = 32 * (t % 4)
+        middle[t] = chunks[s, base][:, start : start + 32].astype(F32) * middle_scale
+    total = []
+    for half in range(2):
+        tiles = [found["stem", half], found["stem", 2 + half]]
+        total.append(sum(chunks[s, base + k].astype(F32) for s, base in tiles for k in range(2)))
+    total = jnp.concatenate(total, axis=0).T * stem_scale
+    for t in range(27):
+        stem[t] = total[4 * t : 4 * t + 4]
+    rows = []
+    for y in range(16):
+        s, base = found["features", y % 4]
+        rows.append(chunks[s, base + y // 4])
+    turned = nn(turn_matrix(16), jnp.concatenate(rows, axis=0)).astype(BF16)
+    features[...] = turned.reshape(16, 16, LANES)
 
 
 def whole(count):
@@ -194,70 +287,73 @@
     middle_cells = stem_cells // 8
     limit = pltpu.CompilerParams(vmem_limit_bytes=48 * 1024 * 1024)
 
-    mid_w = middle_weight.transpose(2, 0, 1).reshape(16, 864)
-    mid_w = jnp.pad(mid_w, ((0, 0), (0, 32)))
-    cot = cotangent.reshape(16, filts, 512).transpose(1, 0, 2)
-    packed = jnp.concatenate([jnp.broadcast_to(mid_w[None], (filts, 16, 896)), cot], axis=2)
-    gathered = lax.all_to_all(packed, "filt", 0, 0, tiled=True)
-
-    own, slab_x, slab_y, corner = pl.pallas_call(
+    own, slab_x, packed = pl.pallas_call(
         regroup_kernel,
         out_shape=[
             jax.ShapeDtypeStruct((planes, 16 * width, LANES), BF16),
             jax.ShapeDtypeStruct((planes - 1, 16 * width, LANES), BF16),
-            jax.ShapeDtypeStruct((planes, 48, LANES), BF16),
-            jax.ShapeDtypeStruct((planes - 1, 48, LANES), BF16),
-        ],
-        in_specs=whole(1),
-        out_specs=whole(4),
+            jax.ShapeDtypeStruct((filts, 11, 16, LANES), BF16),
+        ],
+        in_specs=whole(3),
+        out_specs=whole(3),
         compiler_params=limit,
         name="regroup",
-    )(volume)
-    route_x = [(s - 1, s) for s in range(1, spaces)]
-    route_y = [(f - 1, f) for f in range(1, filts)]
-    route_xy = [
-        ((s - 1) * filts + f - 1, s * filts + f) for s in range(1, spaces) for f in range(1, filts)
-    ]
-    slab_x = lax.ppermute(slab_x, "space", route_x)
-    slab_y = lax.ppermute(slab_y, "filt", route_y)
-    corner = lax.ppermute(corner, ("space", "filt"), route_xy)
+    )(volume, middle_weight.transpose(0, 2, 1), cotangent.reshape(16, 16, LANES))
+    slab_x = lax.ppermute(slab_x, "space", [(s - 1, s) for s in range(1, spaces)])
+    gathered = lax.all_to_all(packed, "filt", 0, 0, tiled=True)
+    border = pl.pallas_call(
+        border_kernel,
+        out_shape=jax.ShapeDtypeStruct((7, 48, LANES), BF16),
+        in_specs=whole(2),
+        out_specs=whole(1)[0],
+        compiler_params=limit,
+        name="border",
+    )(slab_x, own)
+    border = lax.ppermute(border, "filt", [(f - 1, f) for f in range(1, filts)])
 
     stem_w = jnp.pad(stem_weight.reshape(108, 32).T, ((0, 0), (0, 20)))
     place = jnp.asarray(place_table(), BF16)
-    per = -(-11 // spaces)
-    features, slots = pl.pallas_call(
+    widths = slot_widths(spaces)
+    slots = pl.pallas_call(
         main_kernel,
-        out_shape=[
-            jax.ShapeDtypeStruct((filts, 16, 512), BF16),
-            jax.ShapeDtypeStruct((spaces, filts, per, 16, LANES), BF16),
-        ],
-        in_specs=whole(7),
-        out_specs=whole(2),
+        out_shape=jax.ShapeDtypeStruct((spaces, filts, len(widths), 16, LANES), BF16),
+        in_specs=whole(6),
+        out_specs=whole(1)[0],
         scratch_shapes=[
             pltpu.VMEM((7, 96, 9 * LANES), BF16),
+            pltpu.VMEM((64, 896), BF16),
             pltpu.VMEM((864, 512), BF16),
             pltpu.VMEM((3, 64, 9 * LANES), F32),
             pltpu.VMEM((3, 64, 9 * LANES), BF16),
-            pltpu.VMEM((8, LANES), F32),
         ],
         compiler_params=limit,
         name="sections",
-    )(own, slab_x, slab_y, corner, stem_w, place, gathered)
-
-    features = lax.all_to_all(features, "filt", 0, 0, tiled=True)
-    features = features.transpose(1, 0, 2).reshape(16, 1, 4 * filts, LANES)
-
-    slots = slots.reshape(spaces * filts, per, 16, LANES)
+    )(own, slab_x, border, stem_w, place, gathered)
+
+    slots = slots.reshape(spaces * filts, len(widths), 16, LANES)
     parts = lax.all_to_all(slots, ("space", "filt"), 0, 0, tiled=True)
-    total = parts.astype(F32).sum(0)
-    total = lax.all_to_all(
-        jnp.broadcast_to(total[None], (spaces, per, 16, LANES)), "space", 0, 0, tiled=True
-    ).reshape(spaces * per, 16, LANES)
-    middle = total[:7].transpose(1, 0, 2).reshape(16, 896)[:, :864] / math.sqrt(middle_cells)
-    middle = middle.reshape(16, 27, 32).transpose(1, 2, 0)
-    stem = (total[7:9] + total[9:11]).reshape(32, LANES)[:, :108] / math.sqrt(stem_cells)
-    stem = stem.T.reshape(27, 4, 32)
-    return features, middle, stem
+    chunks = pl.pallas_call(
+        sum_kernel,
+        out_shape=jax.ShapeDtypeStruct((spaces, sum(widths), 16, LANES), BF16),
+        in_specs=whole(1),
+        out_specs=whole(1)[0],
+        compiler_params=limit,
+        name="sums",
+    )(parts)
+    chunks = lax.all_to_all(chunks, "space", 0, 0, tiled=True)
+    features, middle, stem = pl.pallas_call(
+        functools.partial(unpack_kernel, middle_cells**-0.5, stem_cells**-0.5),
+        out_shape=[
+            jax.ShapeDtypeStruct((16, 16, LANES), BF16),
+            jax.ShapeDtypeStruct((27, 16, 32), F32),
+            jax.ShapeDtypeStruct((27, 4, 32), F32),
+        ],
+        in_specs=whole(1),
+        out_specs=whole(3),
+        compiler_params=limit,
+        name="unpack",
+    )(chunks)
+    return features.reshape(16, 1, 16, LANES), middle.transpose(0, 2, 1), stem
 
 
 def solution(mesh):

time: 60.5 us -> 48.9 us (0.81)
  starting transfers between devices: 23.2 us -> 12.1 us
  blocking collectives: 14.9 us -> 24.4 us
  waiting for transfers between devices: 11.9 us -> 2.95 us
  local copies, waits for them, and re-layouts: 4.33 us -> 2.8 us
  Pallas kernels: 4.04 us -> 5.51 us
  other arithmetic: 0.75 us -> 0 us
    all_to_all x2 -> x0, waiting for transfers between devices: 10.4 us -> none  [the longest x1 5.66 us: body(): features = lax.all_to_all(features, 'filt', 0, 0, tiled=True)]
    all_to_all x0 -> x1, blocking collectives: none -> 8.28 us  [body(): chunks = lax.all_to_all(chunks, 'space', 0, 0, tiled=True)]
    all_to_all x2 -> x0, starting transfers between devices: 6.66 us -> none  [the longest x1 3.37 us: body(): lax.all_to_all(jnp.broadcast_to(total[None], (spaces, per, 16, LANES)), '...]
    ppermute x3 -> x2, starting transfers between devices: 10.1 us -> 6.42 us  [the longest x1 4.06 us: body(): border = lax.ppermute(border, 'filt', [(f - 1, f) for f in range(1, filts)])]
    all_to_all x1, waiting for transfers between devices: 0.01 us -> 2.94 us  [body(): gathered = lax.all_to_all(packed, 'filt', 0, 0, tiled=True)]
    reshape x7 -> x0, local copies, waits for them, and re-layouts: 2.51 us -> none  [the longest x2 0.92 us: body(): cot = cotangent.reshape(16, filts, 512).transpose(1, 0, 2)]
    unnamed x9 -> x10, local copies, waits for them, and re-layouts: 0.83 us -> 2.69 us
    ppermute x3 -> x2, waiting for transfers between devices: 1.49 us -> 0.01 us  [the longest x1 0.01 us: body(): lax.ppermute(slab_x, 'space', [(s - 1, s) for s in range(1, spaces)])]
  transfers between devices with their start and end apart: 6 -> 3, of which waited for: 3 -> 1; matrix products, arithmetic and copies ran while one was open for 1% -> 0% of each run, Pallas kernels for 1% -> 0%
where the time goes in v1:
time: 48.9 us; the launch traced here: 48.4 us
  blocking collectives  24.4 us (50%)
  starting transfers between devices  12.1 us (25%)
  Pallas kernels  5.51 us (11%)
  waiting for transfers between devices  2.95 us (6%)
  local copies, waits for them, and re-layouts  2.8 us (6%)
  between operations  0.71 us (1%)
    all_to_all x1, blocking collectives, body(): parts = lax.all_to_all(slots, ('space', 'filt'), 0, 0, tiled=True)  16.1 us
    all_to_all x1, blocking collectives, body(): chunks = lax.all_to_all(chunks, 'space', 0, 0, tiled=True)  8.28 us
    all_to_all x1, starting transfers between devices, body(): gathered = lax.all_to_all(packed, 'filt', 0, 0, tiled=True)  5.71 us
    ppermute x1, starting transfers between devices, body(): border = lax.ppermute(border, 'filt', [(f - 1, f) for f in range(1, filts)])  4.06 us
    pallas_call x1, Pallas kernels, body(): pl.pallas_call(main_kernel, out_shape=jax.ShapeDtypeStruct((spaces, filts...  3.14 us
    all_to_all x1, waiting for transfers between devices, body(): gathered = lax.all_to_all(packed, 'filt', 0, 0, tiled=True)  2.94 us
    unnamed x10, local copies, waits for them, and re-layouts  2.69 us
    ppermute x1, starting transfers between devices, body(): lax.ppermute(slab_x, 'space', [(s - 1, s) for s in range(1, spaces)])  2.36 us
  transfers between devices with their start and end apart: 3, of which 1 were waited for; matrix products, arithmetic and copies ran while one was open for 0% of the time, Pallas kernels for 0%

profile of v1, /device:TPU:0, one launch (start us, length us, event | category | flops | bytes accessed | tf_op | source)
XLA Modules:
  0.0 48.4 jit_solution(17845051602594471137)
XLA Ops:
  0.6 0.0 copy-start
  0.6 0.9 %copy-done = bf16[4,4,16,512]{3,2,1,0:T(8,128)(2,1)S(1)} copy-done((bf16[4,4,16,512]{3,2,1,0:T(8,128)(2,1)S(1)}, bf16[4,4,16,512]{3,2,1,0:T(8,128)(2,1)}, u32[]{:S(2)}) %copy-start) | copy-done | bytes 262168
  1.6 0.0 copy-start.2
  1.6 0.9 %copy-done.2 = bf16[27,32,16]{1,2,0:T(8,128)(2,1)S(1)} copy-done((bf16[27,32,16]{1,2,0:T(8,128)(2,1)S(1)}, bf16[27,32,16]{1,2,0:T(8,128)(2,1)}, u32[]{:S(2)}) %copy-start.2) | copy-done | bytes 27672
  2.5 0.0 copy-start.3
  2.5 0.8 %copy-done.3 = bf16[16,1,16,128]{3,2,1,0:T(8,128)(2,1)S(1)} copy-done((bf16[16,1,16,128]{3,2,1,0:T(8,128)(2,1)S(1)}, bf16[16,1,16,128]{3,2,1,0:T(8,128)(2,1)}, u32[]{:S(2)}) %copy-start.3) | copy-done | bytes 65560
  3.3 1.4 %regroup.1 = (bf16[4,256,128]{2,1,0:T(8,128)(2,1)S(1)}, bf16[3,256,128]{2,1,0:T(8,128)(2,1)S(1)}, bf16[4,11,16,128]{3,2,1,0:T(8,128)(2,1)}) custom-call(bf16[4,4,16,512]{3,2,1,0:T(8,128)(2,1)S(1)} %copy-done, bf16[27,16,32]{2,1,0:T(8,128)(2,1)S(1)} %bitcast.9, bf16[16,16,128]{2,1,0:T(8,128)(2,1)S(1)} %bitcast.10), custom_call_target="tpu_custom_call" | custom-call | tf_op jit(solution)/shard_map/regroup/pallas_call | solution.py:290
  4.7 2.4 %collective-permute-start = (bf16[3,256,128]{2,1,0:T(8,128)(2,1)S(1)}, bf16[3,256,128]{2,1,0:T(8,128)(2,1)S(1)}, u32[]{:S(2)}, u32[]{:S(2)}) collective-permute-start(bf16[3,256,128]{2,1,0:T(8,128)(2,1)S(1)} %get-tuple-element.10), channel_id=1, source_target_pairs={{0,4},{4,8},{8,12},{12,16},{16,20},{20,24},{24,28},{1,5},{5,9},{9,... | collective-permute-start | bytes 589832 | tf_op jit(solution)/shard_map/ppermute | solution.py:302
  7.1 5.7 %all-to-all-start = ((bf16[4,11,16,128]{3,2,1,0:T(8,128)(2,1)}), bf16[4,11,16,128]{3,2,1,0:T(8,128)(2,1)S(1)}, u32[]{:S(2)}, u32[]{:S(2)}) async-start(bf16[4,11,16,128]{3,2,1,0:T(8,128)(2,1)} %get-tuple-element.11), calls=%async_computation | async-start | bytes 360448 | tf_op jit(solution)/shard_map/all_to_all | solution.py:303
  12.8 0.0 collective-permute-done.slab_x
  12.8 0.0 copy-start.4
  12.8 0.0 copy-start.1
  12.8 4.1 %collective-permute-start.1 = (bf16[7,48,128]{2,1,0:T(8,128)(2,1)S(1)}, bf16[7,48,128]{2,1,0:T(8,128)(2,1)S(1)}, u32[]{:S(2)}, u32[]{:S(2)}) collective-permute-start(bf16[7,48,128]{2,1,0:T(8,128)(2,1)S(1)} %border.1), channel_id=1, source_target_pairs={{0,1},{1,2},{2,3},{4,5},{5,6},{6,7},{8,9},{9,10},{10,11},{12,13},{... | collective-permute-start | bytes 258056 | tf_op jit(solution)/shard_map/ppermute | solution.py:312
  16.9 0.0 copy-done.4
  16.9 0.1 copy.10
  17.0 2.9 %all-to-all-done.gathered = bf16[4,11,16,128]{3,2,1,0:T(8,128)(2,1)S(1)} async-done(((bf16[4,11,16,128]{3,2,1,0:T(8,128)(2,1)}), bf16[4,11,16,128]{3,2,1,0:T(8,128)(2,1)S(1)}, u32[]{:S(2)}, u32[]{:S(2)}) %all-to-all-start) | async-done | bytes 180256 | tf_op jit(solution)/shard_map/all_to_all | solution.py:303
  20.0 0.0 collective-permute-done.1.border
  20.0 0.0 copy-done.1
  20.0 3.1 %sections.1 = bf16[8,4,2,16,128]{4,3,2,1,0:T(8,128)(2,1)S(1)} custom-call(bf16[4,256,128]{2,1,0:T(8,128)(2,1)S(1)} %get-tuple-element.9.own, bf16[3,256,128]{2,1,0:T(8,128)(2,1)S(1)} %collective-permute-done.slab_x, bf16[7,48,128]{2,1,0:T(8,128)(2,1)S(1)} %collective-permute-done.1.border, bf16[32,128]{1,0:T(8,128)(2,1)S(1)} %pad.4.stem_w, ...), custom_call_target="tpu_custom_call" | custom-call | tf_op jit(solution)/shard_map/sections/pallas_call | solution.py:317
  23.1 16.1 %all_to_all.15.parts = bf16[32,2,16,128]{3,2,1,0:T(8,128)(2,1)S(1)} all-to-all(bf16[32,2,16,128]{3,2,1,0:T(8,128)(2,1)S(1)} %bitcast.8), channel_id=1, replica_groups=mesh['space'=8,'filt'=4] {'space','filt'}, dimensions={0} | all-to-all | bytes 524288 | tf_op jit(solution)/shard_map/all_to_all | solution.py:334
  39.2 0.1 sums.1
  39.3 8.3 %all_to_all.16.chunks = bf16[8,5,16,128]{3,2,1,0:T(8,128)(2,1)S(1)} all-to-all(bf16[8,5,16,128]{3,2,1,0:T(8,128)(2,1)S(1)} %sums.1), channel_id=1, replica_groups=mesh['space'=8,'filt'=4] {'space'}, dimensions={0} | all-to-all | bytes 327680 | tf_op jit(solution)/shard_map/all_to_all | solution.py:343
  47.6 0.9 %unpack.1 = (bf16[16,16,128]{2,1,0:T(8,128)(2,1)}, f32[27,16,32]{2,1,0:T(8,128)}, f32[27,4,32]{2,1,0:T(4,128)}) custom-call(bf16[8,5,16,128]{3,2,1,0:T(8,128)(2,1)S(1)} %all_to_all.16.chunks), custom_call_target="tpu_custom_call" | custom-call | tf_op jit(solution)/shard_map/unpack/pallas_call | solution.py:344
  (3 shorter events, 0.0 us)
Async XLA Ops:
  0.6 1.0 %copy-start = (bf16[4,4,16,512]{3,2,1,0:T(8,128)(2,1)S(1)}, bf16[4,4,16,512]{3,2,1,0:T(8,128)(2,1)}, u32[]{:S(2)}) copy-start(bf16[4,4,16,512]{3,2,1,0:T(8,128)(2,1)} %volume.1) | copy-start | bytes 786436
  1.6 0.9 %copy-start.2 = (bf16[27,32,16]{1,2,0:T(8,128)(2,1)S(1)}, bf16[27,32,16]{1,2,0:T(8,128)(2,1)}, u32[]{:S(2)}) copy-start(bf16[27,32,16]{1,2,0:T(8,128)(2,1)} %param.7) | copy-start | bytes 82948
  2.5 0.8 %copy-start.3 = (bf16[16,1,16,128]{3,2,1,0:T(8,128)(2,1)S(1)}, bf16[16,1,16,128]{3,2,1,0:T(8,128)(2,1)}, u32[]{:S(2)}) copy-start(bf16[16,1,16,128]{3,2,1,0:T(8,128)(2,1)} %param.8) | copy-start | bytes 196612
  4.7 8.1 %collective-permute-start = (bf16[3,256,128]{2,1,0:T(8,128)(2,1)S(1)}, bf16[3,256,128]{2,1,0:T(8,128)(2,1)S(1)}, u32[]{:S(2)}, u32[]{:S(2)}) collective-permute-start(bf16[3,256,128]{2,1,0:T(8,128)(2,1)S(1)} %get-tuple-element.10), channel_id=1, source_target_pairs={{0,4},{4,8},{8,12},{12,16},{16,20},{20,24},{24,28},{1,5},{5,9},{9,... | collective-permute-start | bytes 589832 | tf_op jit(solution)/shard_map/ppermute | solution.py:302
  7.1 12.9 %all-to-all-start = ((bf16[4,11,16,128]{3,2,1,0:T(8,128)(2,1)}), bf16[4,11,16,128]{3,2,1,0:T(8,128)(2,1)S(1)}, u32[]{:S(2)}, u32[]{:S(2)}) async-start(bf16[4,11,16,128]{3,2,1,0:T(8,128)(2,1)} %get-tuple-element.11), calls=%async_computation | async-start | bytes 360448 | tf_op jit(solution)/shard_map/all_to_all | solution.py:303
  12.8 4.1 %copy-start.4 = (bf16[27,4,32]{2,1,0:T(4,128)(2,1)S(1)}, bf16[27,4,32]{2,1,0:T(4,128)(2,1)}, u32[]{:S(2)}) copy-start(bf16[27,4,32]{2,1,0:T(4,128)(2,1)} %param.6) | copy-start | bytes 20740
  12.8 7.2 %copy-start.1 = (bf16[2,128,288]{2,1,0:T(8,128)(2,1)S(1)}, bf16[2,128,288]{2,1,0:T(8,128)(2,1)}, u32[]{:S(2)}) copy-start(bf16[2,128,288]{2,1,0:T(8,128)(2,1)} %constant.5.clone.place) | copy-start | bytes 442372
  12.8 7.2 %collective-permute-start.1 = (bf16[7,48,128]{2,1,0:T(8,128)(2,1)S(1)}, bf16[7,48,128]{2,1,0:T(8,128)(2,1)S(1)}, u32[]{:S(2)}, u32[]{:S(2)}) collective-permute-start(bf16[7,48,128]{2,1,0:T(8,128)(2,1)S(1)} %border.1), channel_id=1, source_target_pairs={{0,1},{1,2},{2,3},{4,5},{5,6},{6,7},{8,9},{9,10},{10,11},{12,13},{... | collective-permute-start | bytes 258056 | tf_op jit(solution)/shard_map/ppermute | solution.py:312

commit v2 on v1

--- a/solution.py
+++ b/solution.py
@@ -11,7 +11,7 @@
 F32 = jnp.float32
 BF16 = jnp.bfloat16
 LANES = 128
-STEM_ROWS = 288
+STEM_ROWS = 144
 
 
 def nn(a, b):
@@ -23,16 +23,16 @@
 
 
 def place_table():
-    table = np.zeros((2, LANES, STEM_ROWS), np.float32)
+    table = np.zeros((3, LANES, STEM_ROWS), np.float32)
     for even_odd in range(2):
         for a in range(3):
             for b in range(3):
                 for d in range(3):
                     q = 2 * even_odd + d - 1
-                    shifted, phase = (1, 3) if q < 0 else (0, q)
+                    group, phase = (2, 3) if q < 0 else (even_odd, q)
                     for c in range(4):
-                        column = 96 * a + 48 * shifted + 16 * b + 4 * phase + c
-                        table[even_odd, 4 * (9 * a + 3 * b + d) + c, column] = 1.0
+                        column = 48 * a + 16 * b + 4 * phase + c
+                        table[group, 4 * (9 * a + 3 * b + d) + c, column] = 1.0
     return table
 
 
@@ -40,31 +40,48 @@
     return lax.broadcasted_iota(jnp.int32, shape, 0), lax.broadcasted_iota(jnp.int32, shape, 1)
 
 
-def turn_matrix(count):
-    row, column = rows_lanes((count * count, count * count))
-    return ((row % count) * count + (row // count) == column).astype(F32).astype(BF16)
-
-
-def regroup_kernel(volume, weight, cotangent, own, slab_x, packed):
+def turn_matrix():
+    row, column = rows_lanes((256, 256))
+    source = lax.shift_left(row & 15, 4) + lax.shift_right_logical(row, 4)
+    return (source == column).astype(F32).astype(BF16)
+
+
+def regroup_kernel(volume_in, weight_in, cotangent_in, own, slab_x, packed, volume, weight, cotangent, sems):
+    copies = [
+        pltpu.make_async_copy(source, target, sems.at[k])
+        for k, (source, target) in enumerate(
+            [(volume_in, volume), (weight_in, weight), (cotangent_in, cotangent)]
+        )
+    ]
+    for copy in copies:
+        copy.start()
     channels, planes, width, depth = volume.shape
     z, column = rows_lanes((depth, depth))
-    select = (z == 4 * (column % LANES) + (column // LANES)).astype(F32).astype(BF16)
-    turn = turn_matrix(16)
+    source = lax.shift_left(column & (LANES - 1), 2) + lax.shift_right_logical(column, 7)
+    select = (z == source).astype(F32).astype(BF16)
+    turn = turn_matrix()
+    copies[0].wait()
     picked = nn(volume[...].reshape(channels * planes * width, depth), select).astype(BF16)
+    grouped = []
     for x in range(planes):
         parts = []
         for phase in range(4):
             for c in range(channels):
                 start = (c * planes + x) * width
                 parts.append(picked[start : start + width, phase * LANES : (phase + 1) * LANES])
-        plane = nn(turn, jnp.concatenate(parts, axis=0)).astype(BF16)
+        grouped.append(jnp.concatenate(parts, axis=0))
+    copies[1].wait()
+    copies[2].wait()
+    grouped.append(cotangent[...].reshape(256, LANES))
+    turned = nn(turn, jnp.concatenate(grouped, axis=1)).astype(BF16)
+    for x in range(planes):
+        plane = turned[:, x * LANES : (x + 1) * LANES]
         own[x] = plane
         if x > 0:
             slab_x[x - 1] = plane
 
     blank = jnp.zeros((16, 32), BF16)
     taps = [weight[t] if t < 27 else blank for t in range(28)]
-    turned = nn(turn, cotangent[...].reshape(256, LANES)).astype(BF16)
     for t in range(7):
         tile = jnp.concatenate(taps[4 * t : 4 * t + 4], axis=1)
         for f in range(packed.shape[0]):
@@ -72,7 +89,7 @@
     for f in range(packed.shape[0]):
         for j in range(4):
             row = 16 * (4 * f + j)
-            packed[f, 7 + j] = turned[row : row + 16]
+            packed[f, 7 + j] = turned[row : row + 16, planes * LANES :]
 
 
 def border_kernel(slab_x, own, border):
@@ -89,11 +106,14 @@
     return soft, jnp.where(values >= 0.0, inverse, small * inverse)
 
 
-def roll_lanes(values, amount):
-    lane = lax.broadcasted_iota(jnp.int32, values.shape, 1)
-    edge = 0 if amount == 1 else LANES - 1
-    rolled = pltpu.roll(values, amount % LANES, 1)
-    return jnp.where(lane == edge, 0.0, rolled)
+def roll_blocks(values, amount):
+    blocks = []
+    for start in range(0, values.shape[1], LANES):
+        block = values[:, start : start + LANES]
+        lane = lax.broadcasted_iota(jnp.int32, block.shape, 1)
+        edge = 0 if amount == 1 else LANES - 1
+        blocks.append(jnp.where(lane == edge, 0.0, pltpu.roll(block, amount % LANES, 1)))
+    return jnp.concatenate(blocks, axis=1)
 
 
 def slot_kinds(spaces):
@@ -118,15 +138,13 @@
 
     for x in range(7):
         plane = jnp.concatenate([border[x], slab_x[x] if x < 3 else own[x - 3]], axis=0)
-        shifted = roll_lanes(plane.astype(F32), 1).astype(BF16)
         for j in range(9):
-            lanes = pl.ds(j * LANES, LANES)
-            cols[x, 0:48, lanes] = plane[32 * j : 32 * j + 48]
-            cols[x, 48:96, lanes] = shifted[32 * j : 32 * j + 48]
-
-    weights = jnp.concatenate([nn(stem_w[...], place[0]), nn(stem_w[...], place[1])], axis=0).astype(BF16)
+            cols[x, :, pl.ds(j * LANES, LANES)] = plane[32 * j : 32 * j + 48]
+
+    weights = jnp.concatenate([nn(stem_w[...], place[g]) for g in range(3)], axis=0).astype(BF16)
     for i in range(3):
         pre = nn(weights, cols[2 * i : 2 * i + 3].reshape(STEM_ROWS, 9 * LANES))
+        pre = jnp.concatenate([pre[0:32] + roll_blocks(pre[64:96], 1), pre[32:64]], axis=0)
         soft, sig = softplus_sigmoid(pre)
         act = 0.3 * pre + 0.7 * soft
         lean = 0.3 + 0.7 * sig
@@ -138,7 +156,7 @@
         for j in range(9):
             even = act[0:32, j * LANES : (j + 1) * LANES]
             odd = act[32:64, j * LANES : (j + 1) * LANES]
-            for d, part in ((0, roll_lanes(odd, 1)), (1, even), (2, odd)):
+            for d, part in ((0, roll_blocks(odd, 1)), (1, even), (2, odd)):
                 part = part.astype(BF16)
                 for b in range(3):
                     if (j - b) % 2 == 0 and 0 <= (j - b) // 2 < 4:
@@ -176,33 +194,29 @@
         odd = jnp.concatenate([block(a, b, 2), block(a, b, 0)], axis=1)
         return jnp.concatenate([even, odd], axis=0)
 
-    both = jnp.concatenate(
-        [delta_low]
-        + [
-            jnp.concatenate(
-                [roll_lanes(delta[:, j * LANES : (j + 1) * LANES], -1) for j in range(4)], axis=1
-            ).astype(BF16)
-        ],
-        axis=0,
-    )
+    both = jnp.concatenate([delta_low, roll_blocks(delta, -1).astype(BF16)], axis=0)
     nothing = jnp.zeros((2 * blocks * 16, LANES), BF16)
     pair = jnp.concatenate(
         [jnp.concatenate([both, nothing], axis=1), jnp.concatenate([nothing, both], axis=1)], axis=0
     )
-    stem_grad = jnp.zeros((64, STEM_ROWS), F32)
+    odd_back = nn(jnp.concatenate([wide(i, 1) for i in range(3)], axis=0), both)
+    even_back = nn(
+        jnp.concatenate([jnp.concatenate([wide(i, 0), wide(i, 2)], axis=1) for i in range(3)], axis=0), pair
+    )
+    stem_grad = jnp.zeros((96, STEM_ROWS), F32)
     for i in range(3):
-        odd_back = nn(wide(i, 1), both)
-        even_back = nn(jnp.concatenate([wide(i, 0), wide(i, 2)], axis=1), pair)
         for j in range(9):
             source = even_back if j % 2 == 0 else odd_back
-            part = source[:, (j // 2) * LANES : (j // 2 + 1) * LANES]
+            part = source[64 * i : 64 * i + 64, (j // 2) * LANES : (j // 2 + 1) * LANES]
             lanes = pl.ds(j * LANES, LANES)
-            stem_back[i, :, lanes] = (part * slope[i, :, lanes]).astype(BF16)
+            part = part * slope[i, :, lanes]
+            stem_back[i, 0:64, lanes] = part.astype(BF16)
+            stem_back[i, 64:96, lanes] = roll_blocks(part[0:32], -1).astype(BF16)
         stem_grad += nt(stem_back[i], cols[2 * i : 2 * i + 3].reshape(STEM_ROWS, 9 * LANES))
     high = stem_grad.astype(BF16)
     low = (stem_grad - high.astype(F32)).astype(BF16)
     taken = sum(
-        nt(part[32 * e : 32 * e + 32], place[e]) for part in (high, low) for e in range(2)
+        nt(part[32 * g : 32 * g + 32], place[g]) for part in (high, low) for g in range(3)
     )
     high = taken.astype(BF16)
     low = (taken - high.astype(F32)).astype(BF16)
@@ -272,7 +286,7 @@
     for y in range(16):
         s, base = found["features", y % 4]
         rows.append(chunks[s, base + y // 4])
-    turned = nn(turn_matrix(16), jnp.concatenate(rows, axis=0)).astype(BF16)
+    turned = nn(turn_matrix(), jnp.concatenate(rows, axis=0)).astype(BF16)
     features[...] = turned.reshape(16, 16, LANES)
 
 
@@ -294,8 +308,14 @@
             jax.ShapeDtypeStruct((planes - 1, 16 * width, LANES), BF16),
             jax.ShapeDtypeStruct((filts, 11, 16, LANES), BF16),
         ],
-        in_specs=whole(3),
+        in_specs=[pl.BlockSpec(memory_space=pl.ANY)] * 3,
         out_specs=whole(3),
+        scratch_shapes=[
+            pltpu.VMEM(volume.shape, BF16),
+            pltpu.VMEM((27, 16, 32), BF16),
+            pltpu.VMEM((16, 16, LANES), BF16),
+            pltpu.SemaphoreType.DMA((3,)),
+        ],
         compiler_params=limit,
         name="regroup",
     )(volume, middle_weight.transpose(0, 2, 1), cotangent.reshape(16, 16, LANES))
@@ -320,11 +340,11 @@
         in_specs=whole(6),
         out_specs=whole(1)[0],
         scratch_shapes=[
-            pltpu.VMEM((7, 96, 9 * LANES), BF16),
+            pltpu.VMEM((7, 48, 9 * LANES), BF16),
             pltpu.VMEM((64, 896), BF16),
             pltpu.VMEM((864, 512), BF16),
             pltpu.VMEM((3, 64, 9 * LANES), F32),
-            pltpu.VMEM((3, 64, 9 * LANES), BF16),
+            pltpu.VMEM((3, 96, 9 * LANES), BF16),
         ],
         compiler_params=limit,
         name="sections",

time: 48.9 us -> 48.6 us (level)
    pallas_call x1, Pallas kernels: 3.14 us -> 2.51 us  [body(): pl.pallas_call(main_kernel, out_shape=jax.ShapeDtypeStruct((spaces, filts...]
where the time goes in v2:
time: 48.6 us; the launch traced here: 48.2 us
  blocking collectives  24.4 us (50%)
  starting transfers between devices  12.1 us (25%)
  Pallas kernels  5.22 us (11%)
  waiting for transfers between devices  2.95 us (6%)
  local copies, waits for them, and re-layouts  2.8 us (6%)
  between operations  0.73 us (2%)
    all_to_all x1, blocking collectives, body(): parts = lax.all_to_all(slots, ('space', 'filt'), 0, 0, tiled=True)  16.1 us
    all_to_all x1, blocking collectives, body(): chunks = lax.all_to_all(chunks, 'space', 0, 0, tiled=True)  8.28 us
    all_to_all x1, starting transfers between devices, body(): gathered = lax.all_to_all(packed, 'filt', 0, 0, tiled=True)  5.71 us
    ppermute x1, starting transfers between devices, body(): border = lax.ppermute(border, 'filt', [(f - 1, f) for f in range(1, filts)])  4.06 us
    all_to_all x1, waiting for transfers between devices, body(): gathered = lax.all_to_all(packed, 'filt', 0, 0, tiled=True)  2.94 us
    unnamed x10, local copies, waits for them, and re-layouts  2.69 us
    pallas_call x1, Pallas kernels, body(): pl.pallas_call(main_kernel, out_shape=jax.ShapeDtypeStruct((spaces, filts...  2.51 us
    ppermute x1, starting transfers between devices, body(): lax.ppermute(slab_x, 'space', [(s - 1, s) for s in range(1, spaces)])  2.37 us
  transfers between devices with their start and end apart: 3, of which 1 were waited for; matrix products, arithmetic and copies ran while one was open for 0% of the time, Pallas kernels for 0%

profile of v2, /device:TPU:0, one launch (start us, length us, event | category | flops | bytes accessed | tf_op | source)
XLA Modules:
  0.0 48.2 jit_solution(11928525599702762648)
XLA Ops:
  0.6 0.0 copy-start
  0.6 0.9 %copy-done = bf16[4,4,16,512]{3,2,1,0:T(8,128)(2,1)S(1)} copy-done((bf16[4,4,16,512]{3,2,1,0:T(8,128)(2,1)S(1)}, bf16[4,4,16,512]{3,2,1,0:T(8,128)(2,1)}, u32[]{:S(2)}) %copy-start) | copy-done | bytes 262168
  1.6 0.0 copy-start.2
  1.6 0.9 %copy-done.2 = bf16[27,32,16]{1,2,0:T(8,128)(2,1)S(1)} copy-done((bf16[27,32,16]{1,2,0:T(8,128)(2,1)S(1)}, bf16[27,32,16]{1,2,0:T(8,128)(2,1)}, u32[]{:S(2)}) %copy-start.2) | copy-done | bytes 27672
  2.5 0.0 copy-start.3
  2.5 0.8 %copy-done.3 = bf16[16,1,16,128]{3,2,1,0:T(8,128)(2,1)S(1)} copy-done((bf16[16,1,16,128]{3,2,1,0:T(8,128)(2,1)S(1)}, bf16[16,1,16,128]{3,2,1,0:T(8,128)(2,1)}, u32[]{:S(2)}) %copy-start.3) | copy-done | bytes 65560
  3.3 1.7 %regroup.1 = (bf16[4,256,128]{2,1,0:T(8,128)(2,1)S(1)}, bf16[3,256,128]{2,1,0:T(8,128)(2,1)S(1)}, bf16[4,11,16,128]{3,2,1,0:T(8,128)(2,1)}) custom-call(bf16[4,4,16,512]{3,2,1,0:T(8,128)(2,1)S(1)} %copy-done, bf16[27,16,32]{2,1,0:T(8,128)(2,1)S(1)} %bitcast.9, bf16[16,16,128]{2,1,0:T(8,128)(2,1)S(1)} %bitcast.10), custom_call_target="tpu_custom_call" | custom-call | tf_op jit(solution)/shard_map/regroup/pallas_call | solution.py:304
  5.1 2.4 %collective-permute-start = (bf16[3,256,128]{2,1,0:T(8,128)(2,1)S(1)}, bf16[3,256,128]{2,1,0:T(8,128)(2,1)S(1)}, u32[]{:S(2)}, u32[]{:S(2)}) collective-permute-start(bf16[3,256,128]{2,1,0:T(8,128)(2,1)S(1)} %get-tuple-element.10), channel_id=1, source_target_pairs={{0,4},{4,8},{8,12},{12,16},{16,20},{20,24},{24,28},{1,5},{5,9},{9,... | collective-permute-start | bytes 589832 | tf_op jit(solution)/shard_map/ppermute | solution.py:322
  7.5 5.7 %all-to-all-start = ((bf16[4,11,16,128]{3,2,1,0:T(8,128)(2,1)}), bf16[4,11,16,128]{3,2,1,0:T(8,128)(2,1)S(1)}, u32[]{:S(2)}, u32[]{:S(2)}) async-start(bf16[4,11,16,128]{3,2,1,0:T(8,128)(2,1)} %get-tuple-element.11), calls=%async_computation | async-start | bytes 360448 | tf_op jit(solution)/shard_map/all_to_all | solution.py:323
  13.2 0.0 collective-permute-done.slab_x
  13.2 0.0 copy-start.4
  13.2 0.0 copy-start.1
  13.2 4.1 %collective-permute-start.1 = (bf16[7,48,128]{2,1,0:T(8,128)(2,1)S(1)}, bf16[7,48,128]{2,1,0:T(8,128)(2,1)S(1)}, u32[]{:S(2)}, u32[]{:S(2)}) collective-permute-start(bf16[7,48,128]{2,1,0:T(8,128)(2,1)S(1)} %border.1), channel_id=1, source_target_pairs={{0,1},{1,2},{2,3},{4,5},{5,6},{6,7},{8,9},{9,10},{10,11},{12,13},{... | collective-permute-start | bytes 258056 | tf_op jit(solution)/shard_map/ppermute | solution.py:332
  17.3 0.0 copy-done.4
  17.3 0.1 copy.10
  17.4 2.9 %all-to-all-done.gathered = bf16[4,11,16,128]{3,2,1,0:T(8,128)(2,1)S(1)} async-done(((bf16[4,11,16,128]{3,2,1,0:T(8,128)(2,1)}), bf16[4,11,16,128]{3,2,1,0:T(8,128)(2,1)S(1)}, u32[]{:S(2)}, u32[]{:S(2)}) %all-to-all-start) | async-done | bytes 180256 | tf_op jit(solution)/shard_map/all_to_all | solution.py:323
  20.3 0.0 collective-permute-done.1.border
  20.3 0.0 copy-done.1
  20.3 2.5 %sections.1 = bf16[8,4,2,16,128]{4,3,2,1,0:T(8,128)(2,1)S(1)} custom-call(bf16[4,256,128]{2,1,0:T(8,128)(2,1)S(1)} %get-tuple-element.9.own, bf16[3,256,128]{2,1,0:T(8,128)(2,1)S(1)} %collective-permute-done.slab_x, bf16[7,48,128]{2,1,0:T(8,128)(2,1)S(1)} %collective-permute-done.1.border, bf16[32,128]{1,0:T(8,128)(2,1)S(1)} %pad.4.stem_w, ...), custom_call_target="tpu_custom_call" | custom-call | tf_op jit(solution)/shard_map/sections/pallas_call | solution.py:337
  22.9 16.1 %all_to_all.15.parts = bf16[32,2,16,128]{3,2,1,0:T(8,128)(2,1)S(1)} all-to-all(bf16[32,2,16,128]{3,2,1,0:T(8,128)(2,1)S(1)} %bitcast.8), channel_id=1, replica_groups=mesh['space'=8,'filt'=4] {'space','filt'}, dimensions={0} | all-to-all | bytes 524288 | tf_op jit(solution)/shard_map/all_to_all | solution.py:354
  39.0 0.1 sums.1
  39.0 8.3 %all_to_all.16.chunks = bf16[8,5,16,128]{3,2,1,0:T(8,128)(2,1)S(1)} all-to-all(bf16[8,5,16,128]{3,2,1,0:T(8,128)(2,1)S(1)} %sums.1), channel_id=1, replica_groups=mesh['space'=8,'filt'=4] {'space'}, dimensions={0} | all-to-all | bytes 327680 | tf_op jit(solution)/shard_map/all_to_all | solution.py:363
  47.3 0.9 %unpack.1 = (bf16[16,16,128]{2,1,0:T(8,128)(2,1)}, f32[27,16,32]{2,1,0:T(8,128)}, f32[27,4,32]{2,1,0:T(4,128)}) custom-call(bf16[8,5,16,128]{3,2,1,0:T(8,128)(2,1)S(1)} %all_to_all.16.chunks), custom_call_target="tpu_custom_call" | custom-call | tf_op jit(solution)/shard_map/unpack/pallas_call | solution.py:364
  (3 shorter events, 0.0 us)
Async XLA Ops:
  0.6 1.0 %copy-start = (bf16[4,4,16,512]{3,2,1,0:T(8,128)(2,1)S(1)}, bf16[4,4,16,512]{3,2,1,0:T(8,128)(2,1)}, u32[]{:S(2)}) copy-start(bf16[4,4,16,512]{3,2,1,0:T(8,128)(2,1)} %volume_in.1) | copy-start | bytes 786436
  1.6 0.9 %copy-start.2 = (bf16[27,32,16]{1,2,0:T(8,128)(2,1)S(1)}, bf16[27,32,16]{1,2,0:T(8,128)(2,1)}, u32[]{:S(2)}) copy-start(bf16[27,32,16]{1,2,0:T(8,128)(2,1)} %param.7) | copy-start | bytes 82948
  2.5 0.8 %copy-start.3 = (bf16[16,1,16,128]{3,2,1,0:T(8,128)(2,1)S(1)}, bf16[16,1,16,128]{3,2,1,0:T(8,128)(2,1)}, u32[]{:S(2)}) copy-start(bf16[16,1,16,128]{3,2,1,0:T(8,128)(2,1)} %param.8) | copy-start | bytes 196612
  5.1 8.1 %collective-permute-start = (bf16[3,256,128]{2,1,0:T(8,128)(2,1)S(1)}, bf16[3,256,128]{2,1,0:T(8,128)(2,1)S(1)}, u32[]{:S(2)}, u32[]{:S(2)}) collective-permute-start(bf16[3,256,128]{2,1,0:T(8,128)(2,1)S(1)} %get-tuple-element.10), channel_id=1, source_target_pairs={{0,4},{4,8},{8,12},{12,16},{16,20},{20,24},{24,28},{1,5},{5,9},{9,... | collective-permute-start | bytes 589832 | tf_op jit(solution)/shard_map/ppermute | solution.py:322
  7.5 12.9 %all-to-all-start = ((bf16[4,11,16,128]{3,2,1,0:T(8,128)(2,1)}), bf16[4,11,16,128]{3,2,1,0:T(8,128)(2,1)S(1)}, u32[]{:S(2)}, u32[]{:S(2)}) async-start(bf16[4,11,16,128]{3,2,1,0:T(8,128)(2,1)} %get-tuple-element.11), calls=%async_computation | async-start | bytes 360448 | tf_op jit(solution)/shard_map/all_to_all | solution.py:323
  13.2 4.1 %copy-start.4 = (bf16[27,4,32]{2,1,0:T(4,128)(2,1)S(1)}, bf16[27,4,32]{2,1,0:T(4,128)(2,1)}, u32[]{:S(2)}) copy-start(bf16[27,4,32]{2,1,0:T(4,128)(2,1)} %param.6) | copy-start | bytes 20740
  13.2 7.2 %copy-start.1 = (bf16[3,128,144]{2,1,0:T(8,128)(2,1)S(1)}, bf16[3,128,144]{2,1,0:T(8,128)(2,1)}, u32[]{:S(2)}) copy-start(bf16[3,128,144]{2,1,0:T(8,128)(2,1)} %constant.5.clone.place) | copy-start | bytes 331780
  13.2 7.2 %collective-permute-start.1 = (bf16[7,48,128]{2,1,0:T(8,128)(2,1)S(1)}, bf16[7,48,128]{2,1,0:T(8,128)(2,1)S(1)}, u32[]{:S(2)}, u32[]{:S(2)}) collective-permute-start(bf16[7,48,128]{2,1,0:T(8,128)(2,1)S(1)} %border.1), channel_id=1, source_target_pairs={{0,1},{1,2},{2,3},{4,5},{5,6},{6,7},{8,9},{9,10},{10,11},{12,13},{... | collective-permute-start | bytes 258056 | tf_op jit(solution)/shard_map/ppermute | solution.py:332

commit v3 on v2

--- a/solution.py
+++ b/solution.py
@@ -116,22 +116,7 @@
     return jnp.concatenate(blocks, axis=1)
 
 
-def slot_kinds(spaces):
-    kinds = [("middle", u) for u in range(7)] + [("none", 0)]
-    kinds += [("stem", u) for u in range(4)] + [("features", u) for u in range(4)]
-    return kinds + [("none", 0)] * (-len(kinds) % spaces)
-
-
-def slot_widths(spaces):
-    kinds = [kind for kind, _ in slot_kinds(spaces)]
-    widths = []
-    for t in range(len(kinds) // spaces):
-        mine = kinds[t * spaces : (t + 1) * spaces]
-        widths.append(4 if "features" in mine else 2 if "stem" in mine else 1)
-    return widths
-
-
-def main_kernel(own, slab_x, border, stem_w, place, gathered, slots, cols, mid_w, mid_cols, slope, stem_back):
+def main_kernel(own, slab_x, border, stem_w, place, gathered, parts, cols, mid_w, mid_cols, slope, stem_back):
     blocks = gathered.shape[0]
     keep_x = jnp.where(lax.axis_index("space") > 0, 1.0, 0.0).astype(F32)
     keep_y = jnp.where(lax.axis_index("filt") > 0, 1.0, 0.0).astype(F32)
@@ -215,79 +200,38 @@
         stem_grad += nt(stem_back[i], cols[2 * i : 2 * i + 3].reshape(STEM_ROWS, 9 * LANES))
     high = stem_grad.astype(BF16)
     low = (stem_grad - high.astype(F32)).astype(BF16)
-    taken = sum(
+    stem = sum(
         nt(part[32 * g : 32 * g + 32], place[g]) for part in (high, low) for g in range(3)
-    )
-    high = taken.astype(BF16)
-    low = (taken - high.astype(F32)).astype(BF16)
-
-    mid_low = mid_grad.astype(BF16)
-    mid_low = jnp.concatenate([mid_low, jnp.zeros((blocks * 16, 32), BF16)], axis=1)
-    blank = jnp.zeros((16, LANES), BF16)
-    spaces = slots.shape[0]
+    ).astype(BF16)
+
+    middle = mid_grad.astype(BF16)
+    middle = jnp.concatenate([middle, jnp.zeros((blocks * 16, 32), BF16)], axis=1)
     for f in range(blocks):
         rows = slice(16 * f, 16 * f + 16)
-        for u, (kind, which) in enumerate(slot_kinds(spaces)):
-            lanes = slice(which * LANES, (which + 1) * LANES)
-            if kind == "middle":
-                value = mid_low[rows, lanes]
-            elif kind == "stem":
-                value = (high, low)[which // 2][16 * (which % 2) : 16 * (which % 2) + 16]
-            elif kind == "features":
-                value = features[rows, lanes]
-            else:
-                value = blank
-            slots[u % spaces, f, u // spaces] = value
-
-
-def sum_kernel(parts, chunks):
-    spaces = chunks.shape[0]
-    filts = parts.shape[0] // spaces
-    me = lax.axis_index("space")
-    kinds = [kind for kind, _ in slot_kinds(spaces)]
-    base = 0
-    for t, width in enumerate(slot_widths(spaces)):
-        total = jnp.sum(parts[:, t].astype(F32), axis=0)
-        high = total.astype(BF16)
-        tiles = [high]
-        if width > 1:
-            tiles.append((total - high.astype(F32)).astype(BF16))
-        first = kinds.index("features") - t * spaces
-        forward = jnp.logical_and(me >= first, me < first + 4)
-        for s in range(spaces):
-            for k in range(width):
-                if width < 4:
-                    chunks[s, base + k] = tiles[k]
-                    continue
-                here = parts[s * filts + k, t].astype(F32)
-                other = tiles[k].astype(F32) if k < 2 else jnp.zeros_like(here)
-                chunks[s, base + k] = jnp.where(forward, here, other).astype(BF16)
-        base += width
-
-
-def unpack_kernel(middle_scale, stem_scale, chunks, features, middle, stem):
-    spaces = chunks.shape[0]
-    widths = slot_widths(spaces)
-    found = {}
-    for u, (kind, which) in enumerate(slot_kinds(spaces)):
-        found[kind, which] = (u % spaces, sum(widths[: u // spaces]))
+        for t in range(7):
+            parts[f, t] = middle[rows, t * LANES : (t + 1) * LANES]
+        for half in range(2):
+            parts[f, 7 + half] = stem[16 * half : 16 * half + 16]
+        for j in range(4):
+            parts[f, 9 + j] = features[rows, j * LANES : (j + 1) * LANES]
+
+
+def sum_kernel(parts, sums, features):
+    total = jnp.sum(parts[:, 0:9].astype(F32), axis=0).astype(BF16)
+    for s in range(sums.shape[0]):
+        sums[s] = total
+    rows = [parts[f, 9 + j] for f in range(parts.shape[0]) for j in range(4)]
+    features[...] = nn(turn_matrix(), jnp.concatenate(rows, axis=0)).astype(BF16).reshape(16, 16, LANES)
+
+
+def unpack_kernel(middle_scale, stem_scale, sums, middle, stem):
+    total = jnp.sum(sums[...].astype(F32), axis=0)
     for t in range(27):
-        s, base = found["middle", t // 4]
         start = 32 * (t % 4)
-        middle[t] = chunks[s, base][:, start : start + 32].astype(F32) * middle_scale
-    total = []
-    for half in range(2):
-        tiles = [found["stem", half], found["stem", 2 + half]]
-        total.append(sum(chunks[s, base + k].astype(F32) for s, base in tiles for k in range(2)))
-    total = jnp.concatenate(total, axis=0).T * stem_scale
+        middle[t] = total[t // 4, :, start : start + 32] * middle_scale
+    turned = jnp.concatenate([total[7], total[8]], axis=0).T * stem_scale
     for t in range(27):
-        stem[t] = total[4 * t : 4 * t + 4]
-    rows = []
-    for y in range(16):
-        s, base = found["features", y % 4]
-        rows.append(chunks[s, base + y // 4])
-    turned = nn(turn_matrix(), jnp.concatenate(rows, axis=0)).astype(BF16)
-    features[...] = turned.reshape(16, 16, LANES)
+        stem[t] = turned[4 * t : 4 * t + 4]
 
 
 def whole(count):
@@ -301,6 +245,7 @@
     middle_cells = stem_cells // 8
     limit = pltpu.CompilerParams(vmem_limit_bytes=48 * 1024 * 1024)
 
+    raw = (volume, middle_weight.transpose(0, 2, 1), cotangent.reshape(16, 16, LANES))
     own, slab_x, packed = pl.pallas_call(
         regroup_kernel,
         out_shape=[
@@ -308,7 +253,7 @@
             jax.ShapeDtypeStruct((planes - 1, 16 * width, LANES), BF16),
             jax.ShapeDtypeStruct((filts, 11, 16, LANES), BF16),
         ],
-        in_specs=[pl.BlockSpec(memory_space=pl.ANY)] * 3,
+        in_specs=[pl.BlockSpec(memory_space=pltpu.HBM)] * 3,
         out_specs=whole(3),
         scratch_shapes=[
             pltpu.VMEM(volume.shape, BF16),
@@ -318,7 +263,7 @@
         ],
         compiler_params=limit,
         name="regroup",
-    )(volume, middle_weight.transpose(0, 2, 1), cotangent.reshape(16, 16, LANES))
+    )(*[pltpu.with_memory_space_constraint(x, pltpu.HBM) for x in raw])
     slab_x = lax.ppermute(slab_x, "space", [(s - 1, s) for s in range(1, spaces)])
     gathered = lax.all_to_all(packed, "filt", 0, 0, tiled=True)
     border = pl.pallas_call(
@@ -333,10 +278,9 @@
 
     stem_w = jnp.pad(stem_weight.reshape(108, 32).T, ((0, 0), (0, 20)))
     place = jnp.asarray(place_table(), BF16)
-    widths = slot_widths(spaces)
-    slots = pl.pallas_call(
+    parts = pl.pallas_call(
         main_kernel,
-        out_shape=jax.ShapeDtypeStruct((spaces, filts, len(widths), 16, LANES), BF16),
+        out_shape=jax.ShapeDtypeStruct((filts, 13, 16, LANES), BF16),
         in_specs=whole(6),
         out_specs=whole(1)[0],
         scratch_shapes=[
@@ -350,29 +294,30 @@
         name="sections",
     )(own, slab_x, border, stem_w, place, gathered)
 
-    slots = slots.reshape(spaces * filts, len(widths), 16, LANES)
-    parts = lax.all_to_all(slots, ("space", "filt"), 0, 0, tiled=True)
-    chunks = pl.pallas_call(
+    parts = lax.all_to_all(parts, "filt", 0, 0, tiled=True)
+    sums, features = pl.pallas_call(
         sum_kernel,
-        out_shape=jax.ShapeDtypeStruct((spaces, sum(widths), 16, LANES), BF16),
+        out_shape=[
+            jax.ShapeDtypeStruct((spaces, 9, 16, LANES), BF16),
+            jax.ShapeDtypeStruct((16, 16, LANES), BF16),
+        ],
         in_specs=whole(1),
-        out_specs=whole(1)[0],
+        out_specs=whole(2),
         compiler_params=limit,
         name="sums",
     )(parts)
-    chunks = lax.all_to_all(chunks, "space", 0, 0, tiled=True)
-    features, middle, stem = pl.pallas_call(
+    sums = lax.all_to_all(sums, "space", 0, 0, tiled=True)
+    middle, stem = pl.pallas_call(
         functools.partial(unpack_kernel, middle_cells**-0.5, stem_cells**-0.5),
         out_shape=[
-            jax.ShapeDtypeStruct((16, 16, LANES), BF16),
             jax.ShapeDtypeStruct((27, 16, 32), F32),
             jax.ShapeDtypeStruct((27, 4, 32), F32),
         ],
         in_specs=whole(1),
-        out_specs=whole(3),
+        out_specs=whole(2),
         compiler_params=limit,
         name="unpack",
-    )(chunks)
+    )(sums)
     return features.reshape(16, 1, 16, LANES), middle.transpose(0, 2, 1), stem
 
 

time: 48.6 us -> 46.5 us (0.957)
  local copies, waits for them, and re-layouts: 2.8 us -> 0.12 us
  Pallas kernels: 5.22 us -> 6.42 us
  blocking collectives: 24.4 us -> 23.8 us
    unnamed x10 -> x4, local copies, waits for them, and re-layouts: 2.69 us -> 0.01 us
    pallas_call x2, Pallas kernels: 2.58 us -> 3.31 us  [the longest x1 2.48 us: body(): pl.pallas_call(main_kernel, out_shape=jax.ShapeDtypeStruct((filts, 13, 16...]
    all_to_all x2, blocking collectives: 24.4 us -> 23.8 us  [the longest x1 13.8 us: body(): parts = lax.all_to_all(parts, 'filt', 0, 0, tiled=True)]
    pallas_call x1, Pallas kernels: 1.75 us -> 2.28 us  [body(): pl.pallas_call(regroup_kernel, out_shape=[jax.ShapeDtypeStruct((planes, 1...]
where the time goes in v3:
time: 46.5 us; the launch traced here: 46.1 us
  blocking collectives  23.8 us (51%)
  starting transfers between devices  12.1 us (26%)
  Pallas kernels  6.42 us (14%)
  waiting for transfers between devices  2.95 us (6%)
  between operations  0.69 us (1%)
    all_to_all x1, blocking collectives, body(): parts = lax.all_to_all(parts, 'filt', 0, 0, tiled=True)  13.8 us
    all_to_all x1, blocking collectives, body(): sums = lax.all_to_all(sums, 'space', 0, 0, tiled=True)  10 us
    all_to_all x1, starting transfers between devices, body(): gathered = lax.all_to_all(packed, 'filt', 0, 0, tiled=True)  5.71 us
    ppermute x1, starting transfers between devices, body(): border = lax.ppermute(border, 'filt', [(f - 1, f) for f in range(1, filts)])  4.06 us
    all_to_all x1, waiting for transfers between devices, body(): gathered = lax.all_to_all(packed, 'filt', 0, 0, tiled=True)  2.95 us
    pallas_call x1, Pallas kernels, body(): pl.pallas_call(main_kernel, out_shape=jax.ShapeDtypeStruct((filts, 13, 16...  2.48 us
    ppermute x1, starting transfers between devices, body(): lax.ppermute(slab_x, 'space', [(s - 1, s) for s in range(1, spaces)])  2.37 us
    pallas_call x1, Pallas kernels, body(): pl.pallas_call(regroup_kernel, out_shape=[jax.ShapeDtypeStruct((planes, 1...  2.28 us
  transfers between devices with their start and end apart: 3, of which 1 were waited for; matrix products, arithmetic and copies ran while one was open for 0% of the time, Pallas kernels for 0%

profile of v3, /device:TPU:0, one launch (start us, length us, event | category | flops | bytes accessed | tf_op | source)
XLA Modules:
  0.0 46.1 jit_solution(7129534830418596609)
XLA Ops:
  0.6 2.3 %regroup.1 = (bf16[4,256,128]{2,1,0:T(8,128)(2,1)S(1)}, bf16[3,256,128]{2,1,0:T(8,128)(2,1)S(1)}, bf16[4,11,16,128]{3,2,1,0:T(8,128)(2,1)}) custom-call(bf16[4,4,16,512]{3,2,1,0:T(8,128)(2,1)} %volume_in.1, bf16[27,16,32]{2,1,0:T(8,128)(2,1)} %bitcast.7, bf16[16,16,128]{2,1,0:T(8,128)(2,1)} %bitcast.8), custom_call_target="tpu_custom_call" | custom-call | tf_op jit(solution)/shard_map/regroup/pallas_call | solution.py:249
  2.9 2.4 %collective-permute-start = (bf16[3,256,128]{2,1,0:T(8,128)(2,1)S(1)}, bf16[3,256,128]{2,1,0:T(8,128)(2,1)S(1)}, u32[]{:S(2)}, u32[]{:S(2)}) collective-permute-start(bf16[3,256,128]{2,1,0:T(8,128)(2,1)S(1)} %get-tuple-element.11), channel_id=1, source_target_pairs={{0,4},{4,8},{8,12},{12,16},{16,20},{20,24},{24,28},{1,5},{5,9},{9,... | collective-permute-start | bytes 589832 | tf_op jit(solution)/shard_map/ppermute | solution.py:267
  5.3 5.7 %all-to-all-start = ((bf16[4,11,16,128]{3,2,1,0:T(8,128)(2,1)}), bf16[4,11,16,128]{3,2,1,0:T(8,128)(2,1)S(1)}, u32[]{:S(2)}, u32[]{:S(2)}) async-start(bf16[4,11,16,128]{3,2,1,0:T(8,128)(2,1)} %get-tuple-element.12), calls=%async_computation | async-start | bytes 360448 | tf_op jit(solution)/shard_map/all_to_all | solution.py:268
  11.0 0.0 collective-permute-done.slab_x
  11.0 0.0 copy-start.1
  11.0 0.0 copy-start
  11.0 4.1 %collective-permute-start.1 = (bf16[7,48,128]{2,1,0:T(8,128)(2,1)S(1)}, bf16[7,48,128]{2,1,0:T(8,128)(2,1)S(1)}, u32[]{:S(2)}, u32[]{:S(2)}) collective-permute-start(bf16[7,48,128]{2,1,0:T(8,128)(2,1)S(1)} %border.1), channel_id=1, source_target_pairs={{0,1},{1,2},{2,3},{4,5},{5,6},{6,7},{8,9},{9,10},{10,11},{12,13},{... | collective-permute-start | bytes 258056 | tf_op jit(solution)/shard_map/ppermute | solution.py:277
  15.1 0.0 copy-done.1
  15.1 0.1 copy.10
  15.2 2.9 %all-to-all-done.gathered = bf16[4,11,16,128]{3,2,1,0:T(8,128)(2,1)S(1)} async-done(((bf16[4,11,16,128]{3,2,1,0:T(8,128)(2,1)}), bf16[4,11,16,128]{3,2,1,0:T(8,128)(2,1)S(1)}, u32[]{:S(2)}, u32[]{:S(2)}) %all-to-all-start) | async-done | bytes 180256 | tf_op jit(solution)/shard_map/all_to_all | solution.py:268
  18.2 0.0 collective-permute-done.1.border
  18.2 0.0 copy-done
  18.2 2.5 %sections.1 = bf16[4,13,16,128]{3,2,1,0:T(8,128)(2,1)S(1)} custom-call(bf16[4,256,128]{2,1,0:T(8,128)(2,1)S(1)} %get-tuple-element.10.own, bf16[3,256,128]{2,1,0:T(8,128)(2,1)S(1)} %collective-permute-done.slab_x, bf16[7,48,128]{2,1,0:T(8,128)(2,1)S(1)} %collective-permute-done.1.border, bf16[32,128]{1,0:T(8,128)(2,1)S(1)} %pad.4.stem_w, ...), custom_call_target="tpu_custom_call" | custom-call | tf_op jit(solution)/shard_map/sections/pallas_call | solution.py:281
  20.7 13.8 %all_to_all.15.parts = bf16[4,13,16,128]{3,2,1,0:T(8,128)(2,1)S(1)} all-to-all(bf16[4,13,16,128]{3,2,1,0:T(8,128)(2,1)S(1)} %sections.1), channel_id=1, replica_groups=mesh['space'=8,'filt'=4] {'filt'}, dimensions={0} | all-to-all | bytes 425984 | tf_op jit(solution)/shard_map/all_to_all | solution.py:297
  34.5 0.8 %sums.1 = (bf16[8,9,16,128]{3,2,1,0:T(8,128)(2,1)S(1)}, bf16[16,16,128]{2,1,0:T(8,128)(2,1)}) custom-call(bf16[4,13,16,128]{3,2,1,0:T(8,128)(2,1)S(1)} %all_to_all.15.parts), custom_call_target="tpu_custom_call" | custom-call | tf_op jit(solution)/shard_map/sums/pallas_call | solution.py:298
  35.3 10.0 %all_to_all.16.sums = bf16[8,9,16,128]{3,2,1,0:T(8,128)(2,1)S(1)} all-to-all(bf16[8,9,16,128]{3,2,1,0:T(8,128)(2,1)S(1)} %get-tuple-element.14), channel_id=1, replica_groups=mesh['space'=8,'filt'=4] {'space'}, dimensions={0} | all-to-all | bytes 589824 | tf_op jit(solution)/shard_map/all_to_all | solution.py:309
  45.3 0.8 %unpack.1 = (f32[27,16,32]{2,1,0:T(8,128)}, f32[27,4,32]{2,1,0:T(4,128)}) custom-call(bf16[8,9,16,128]{3,2,1,0:T(8,128)(2,1)S(1)} %all_to_all.16.sums), custom_call_target="tpu_custom_call" | custom-call | tf_op jit(solution)/shard_map/unpack/pallas_call | solution.py:310
  (3 shorter events, 0.0 us)
Async XLA Ops:
  2.9 8.1 %collective-permute-start = (bf16[3,256,128]{2,1,0:T(8,128)(2,1)S(1)}, bf16[3,256,128]{2,1,0:T(8,128)(2,1)S(1)}, u32[]{:S(2)}, u32[]{:S(2)}) collective-permute-start(bf16[3,256,128]{2,1,0:T(8,128)(2,1)S(1)} %get-tuple-element.11), channel_id=1, source_target_pairs={{0,4},{4,8},{8,12},{12,16},{16,20},{20,24},{24,28},{1,5},{5,9},{9,... | collective-permute-start | bytes 589832 | tf_op jit(solution)/shard_map/ppermute | solution.py:267
  5.3 12.9 %all-to-all-start = ((bf16[4,11,16,128]{3,2,1,0:T(8,128)(2,1)}), bf16[4,11,16,128]{3,2,1,0:T(8,128)(2,1)S(1)}, u32[]{:S(2)}, u32[]{:S(2)}) async-start(bf16[4,11,16,128]{3,2,1,0:T(8,128)(2,1)} %get-tuple-element.12), calls=%async_computation | async-start | bytes 360448 | tf_op jit(solution)/shard_map/all_to_all | solution.py:268
  11.0 4.1 %copy-start.1 = (bf16[27,4,32]{2,1,0:T(4,128)(2,1)S(1)}, bf16[27,4,32]{2,1,0:T(4,128)(2,1)}, u32[]{:S(2)}) copy-start(bf16[27,4,32]{2,1,0:T(4,128)(2,1)} %param.6) | copy-start | bytes 20740
  11.0 7.2 %copy-start = (bf16[3,128,144]{2,1,0:T(8,128)(2,1)S(1)}, bf16[3,128,144]{2,1,0:T(8,128)(2,1)}, u32[]{:S(2)}) copy-start(bf16[3,128,144]{2,1,0:T(8,128)(2,1)} %constant.5.clone.place) | copy-start | bytes 331780
  11.0 7.2 %collective-permute-start.1 = (bf16[7,48,128]{2,1,0:T(8,128)(2,1)S(1)}, bf16[7,48,128]{2,1,0:T(8,128)(2,1)S(1)}, u32[]{:S(2)}, u32[]{:S(2)}) collective-permute-start(bf16[7,48,128]{2,1,0:T(8,128)(2,1)S(1)} %border.1), channel_id=1, source_target_pairs={{0,1},{1,2},{2,3},{4,5},{5,6},{6,7},{8,9},{9,10},{10,11},{12,13},{... | collective-permute-start | bytes 258056 | tf_op jit(solution)/shard_map/ppermute | solution.py:277

commit v4 on v3

--- a/solution.py
+++ b/solution.py
@@ -116,37 +116,59 @@
     return jnp.concatenate(blocks, axis=1)
 
 
-def main_kernel(own, slab_x, border, stem_w, place, gathered, parts, cols, mid_w, mid_cols, slope, stem_back):
+def fill_columns(cols, planes, count):
+    for x, plane in enumerate(planes):
+        for j in range(count):
+            cols[x, :, pl.ds(j * LANES, LANES)] = plane[32 * j : 32 * j + 48]
+
+
+def stem_forward(weights, cols, i, keep):
+    pre = nn(weights, cols[2 * i : 2 * i + 3].reshape(STEM_ROWS, cols.shape[2]))
+    pre = jnp.concatenate([pre[0:32] + roll_blocks(pre[64:96], 1), pre[32:64]], axis=0)
+    soft, sig = softplus_sigmoid(pre)
+    act = (0.3 * pre + 0.7 * soft) * keep
+    taps = jnp.concatenate([roll_blocks(act[32:64], 1), act], axis=0).astype(BF16)
+    return (0.3 + 0.7 * sig) * keep, taps
+
+
+def keep_space():
+    return jnp.where(lax.axis_index("space") > 0, 1.0, 0.0).astype(F32)
+
+
+def inner_kernel(own, slab_x, stem_w, place, weights, cols, slope, taps):
+    weights[...] = jnp.concatenate([nn(stem_w[...], place[g]) for g in range(3)], axis=0).astype(BF16)
+    planes = [slab_x[x, 16:256] if x < 3 else own[x - 3, 16:256] for x in range(7)]
+    fill_columns(cols, planes, 7)
+    for i in range(3):
+        slope[i], taps[i] = stem_forward(weights[...], cols, i, keep_space() if i == 0 else 1.0)
+
+
+def main_kernel(
+    own, slab_x, border, place, gathered, weights, cols, slope, taps, parts, low_cols, mid_w, mid_cols, stem_back, low_back,
+):
     blocks = gathered.shape[0]
-    keep_x = jnp.where(lax.axis_index("space") > 0, 1.0, 0.0).astype(F32)
     keep_y = jnp.where(lax.axis_index("filt") > 0, 1.0, 0.0).astype(F32)
-
-    for x in range(7):
-        plane = jnp.concatenate([border[x], slab_x[x] if x < 3 else own[x - 3]], axis=0)
+    planes = [
+        jnp.concatenate([border[x], slab_x[x, 0:32] if x < 3 else own[x - 3, 0:32]], axis=0)
+        for x in range(7)
+    ]
+    fill_columns(low_cols, planes, 2)
+    low_slope = []
+    for i in range(3):
+        keep = jnp.where(lax.broadcasted_iota(jnp.int32, (64, 2 * LANES), 1) < LANES, keep_y, 1.0)
+        if i == 0:
+            keep = keep * keep_space()
+        one_slope, low_taps = stem_forward(weights[...], low_cols, i, keep)
+        low_slope.append(one_slope)
         for j in range(9):
-            cols[x, :, pl.ds(j * LANES, LANES)] = plane[32 * j : 32 * j + 48]
-
-    weights = jnp.concatenate([nn(stem_w[...], place[g]) for g in range(3)], axis=0).astype(BF16)
-    for i in range(3):
-        pre = nn(weights, cols[2 * i : 2 * i + 3].reshape(STEM_ROWS, 9 * LANES))
-        pre = jnp.concatenate([pre[0:32] + roll_blocks(pre[64:96], 1), pre[32:64]], axis=0)
-        soft, sig = softplus_sigmoid(pre)
-        act = 0.3 * pre + 0.7 * soft
-        lean = 0.3 + 0.7 * sig
-        keep = jnp.where(lax.broadcasted_iota(jnp.int32, pre.shape, 1) < LANES, keep_y, 1.0)
-        if i == 0:
-            keep = keep * keep_x
-        slope[i] = lean * keep
-        act = act * keep
-        for j in range(9):
-            even = act[0:32, j * LANES : (j + 1) * LANES]
-            odd = act[32:64, j * LANES : (j + 1) * LANES]
-            for d, part in ((0, roll_blocks(odd, 1)), (1, even), (2, odd)):
-                part = part.astype(BF16)
-                for b in range(3):
-                    if (j - b) % 2 == 0 and 0 <= (j - b) // 2 < 4:
-                        row = 32 * (9 * i + 3 * b + d)
-                        mid_cols[row : row + 32, pl.ds((j - b) // 2 * LANES, LANES)] = part
+            if j < 2:
+                part = low_taps[:, j * LANES : (j + 1) * LANES]
+            else:
+                part = taps[i, :, pl.ds((j - 2) * LANES, LANES)]
+            for b in range(3):
+                if (j - b) % 2 == 0 and 0 <= (j - b) // 2 < 4:
+                    row = 96 * (3 * i + b)
+                    mid_cols[row : row + 96, pl.ds((j - b) // 2 * LANES, LANES)] = part
 
     for f in range(blocks):
         for t in range(7):
@@ -193,11 +215,16 @@
         for j in range(9):
             source = even_back if j % 2 == 0 else odd_back
             part = source[64 * i : 64 * i + 64, (j // 2) * LANES : (j // 2 + 1) * LANES]
-            lanes = pl.ds(j * LANES, LANES)
-            part = part * slope[i, :, lanes]
-            stem_back[i, 0:64, lanes] = part.astype(BF16)
-            stem_back[i, 64:96, lanes] = roll_blocks(part[0:32], -1).astype(BF16)
-        stem_grad += nt(stem_back[i], cols[2 * i : 2 * i + 3].reshape(STEM_ROWS, 9 * LANES))
+            if j < 2:
+                target, lanes = low_back, pl.ds(j * LANES, LANES)
+                part = part * low_slope[i][:, j * LANES : (j + 1) * LANES]
+            else:
+                target, lanes = stem_back, pl.ds((j - 2) * LANES, LANES)
+                part = part * slope[i, :, lanes]
+            target[i, 0:64, lanes] = part.astype(BF16)
+            target[i, 64:96, lanes] = roll_blocks(part[0:32], -1).astype(BF16)
+        stem_grad += nt(stem_back[i], cols[2 * i : 2 * i + 3].reshape(STEM_ROWS, 7 * LANES))
+        stem_grad += nt(low_back[i], low_cols[2 * i : 2 * i + 3].reshape(STEM_ROWS, 2 * LANES))
     high = stem_grad.astype(BF16)
     low = (stem_grad - high.astype(F32)).astype(BF16)
     stem = sum(
@@ -216,10 +243,13 @@
             parts[f, 9 + j] = features[rows, j * LANES : (j + 1) * LANES]
 
 
-def sum_kernel(parts, sums, features):
+def sum_kernel(parts, sums):
     total = jnp.sum(parts[:, 0:9].astype(F32), axis=0).astype(BF16)
     for s in range(sums.shape[0]):
         sums[s] = total
+
+
+def features_kernel(parts, features):
     rows = [parts[f, 9 + j] for f in range(parts.shape[0]) for j in range(4)]
     features[...] = nn(turn_matrix(), jnp.concatenate(rows, axis=0)).astype(BF16).reshape(16, 16, LANES)
 
@@ -278,33 +308,53 @@
 
     stem_w = jnp.pad(stem_weight.reshape(108, 32).T, ((0, 0), (0, 20)))
     place = jnp.asarray(place_table(), BF16)
+    weights, cols, slope, taps = pl.pallas_call(
+        inner_kernel,
+        out_shape=[
+            jax.ShapeDtypeStruct((96, STEM_ROWS), BF16),
+            jax.ShapeDtypeStruct((7, 48, 7 * LANES), BF16),
+            jax.ShapeDtypeStruct((3, 64, 7 * LANES), F32),
+            jax.ShapeDtypeStruct((3, 96, 7 * LANES), BF16),
+        ],
+        in_specs=whole(4),
+        out_specs=whole(4),
+        compiler_params=limit,
+        cost_estimate=pl.CostEstimate(flops=200_000_000, bytes_accessed=4_000_000, transcendentals=500_000),
+        name="stem_inner",
+    )(own, slab_x, stem_w, place)
     parts = pl.pallas_call(
         main_kernel,
         out_shape=jax.ShapeDtypeStruct((filts, 13, 16, LANES), BF16),
-        in_specs=whole(6),
+        in_specs=whole(9),
         out_specs=whole(1)[0],
         scratch_shapes=[
-            pltpu.VMEM((7, 48, 9 * LANES), BF16),
+            pltpu.VMEM((7, 48, 2 * LANES), BF16),
             pltpu.VMEM((64, 896), BF16),
             pltpu.VMEM((864, 512), BF16),
-            pltpu.VMEM((3, 64, 9 * LANES), F32),
-            pltpu.VMEM((3, 96, 9 * LANES), BF16),
+            pltpu.VMEM((3, 96, 7 * LANES), BF16),
+            pltpu.VMEM((3, 96, 2 * LANES), BF16),
         ],
         compiler_params=limit,
         name="sections",
-    )(own, slab_x, border, stem_w, place, gathered)
+    )(own, slab_x, border, place, gathered, weights, cols, slope, taps)
 
     parts = lax.all_to_all(parts, "filt", 0, 0, tiled=True)
-    sums, features = pl.pallas_call(
+    sums = pl.pallas_call(
         sum_kernel,
-        out_shape=[
-            jax.ShapeDtypeStruct((spaces, 9, 16, LANES), BF16),
-            jax.ShapeDtypeStruct((16, 16, LANES), BF16),
-        ],
+        out_shape=jax.ShapeDtypeStruct((spaces, 9, 16, LANES), BF16),
         in_specs=whole(1),
-        out_specs=whole(2),
+        out_specs=whole(1)[0],
         compiler_params=limit,
         name="sums",
+    )(parts)
+    features = pl.pallas_call(
+        features_kernel,
+        out_shape=jax.ShapeDtypeStruct((16, 16, LANES), BF16),
+        in_specs=whole(1),
+        out_specs=whole(1)[0],
+        compiler_params=limit,
+        cost_estimate=pl.CostEstimate(flops=20_000_000, bytes_accessed=2_000_000, transcendentals=0),
+        name="features",
     )(parts)
     sums = lax.all_to_all(sums, "space", 0, 0, tiled=True)
     middle, stem = pl.pallas_call(

time: 46.5 us -> 46.7 us (level)
  blocking collectives: 23.8 us -> 13.7 us
  waiting for transfers between devices: 2.95 us -> 8.53 us
  starting transfers between devices: 12.1 us -> 15.6 us
  Pallas kernels: 6.42 us -> 7.65 us
    all_to_all x1 -> x0, blocking collectives: 10 us -> none  [body(): sums = lax.all_to_all(sums, 'space', 0, 0, tiled=True)]
    all_to_all x0 -> x1, waiting for transfers between devices: none -> 6.41 us  [body(): sums = lax.all_to_all(sums, 'space', 0, 0, tiled=True)]
    all_to_all x0 -> x1, starting transfers between devices: none -> 3.42 us  [body(): sums = lax.all_to_all(sums, 'space', 0, 0, tiled=True)]
    pallas_call x1 -> x3, Pallas kernels: 0.83 us -> 2.36 us  [the longest x1 0.82 us: body(): pl.pallas_call(inner_kernel, out_shape=[jax.ShapeDtypeStruct((96, STEM_RO...]
    all_to_all x1, waiting for transfers between devices: 2.95 us -> 2.11 us  [body(): gathered = lax.all_to_all(packed, 'filt', 0, 0, tiled=True)]
  transfers between devices with their start and end apart: 3 -> 4, of which waited for: 1 -> 2; matrix products, arithmetic and copies ran while one was open for 0% -> 0% of each run, Pallas kernels for 0% -> 4%
where the time goes in v4:
time: 46.7 us; the launch traced here: 46.3 us
  starting transfers between devices  15.6 us (33%)
  blocking collectives  13.7 us (29%)
  waiting for transfers between devices  8.53 us (18%)
  Pallas kernels  7.65 us (16%)
  between operations  0.72 us (2%)
    all_to_all x1, blocking collectives, body(): parts = lax.all_to_all(parts, 'filt', 0, 0, tiled=True)  13.7 us
    all_to_all x1, waiting for transfers between devices, body(): sums = lax.all_to_all(sums, 'space', 0, 0, tiled=True)  6.41 us
    all_to_all x1, starting transfers between devices, body(): gathered = lax.all_to_all(packed, 'filt', 0, 0, tiled=True)  5.71 us
    ppermute x1, starting transfers between devices, body(): border = lax.ppermute(border, 'filt', [(f - 1, f) for f in range(1, filts)])  4.06 us
    all_to_all x1, starting transfers between devices, body(): sums = lax.all_to_all(sums, 'space', 0, 0, tiled=True)  3.42 us
    ppermute x1, starting transfers between devices, body(): lax.ppermute(slab_x, 'space', [(s - 1, s) for s in range(1, spaces)])  2.37 us
    pallas_call x1, Pallas kernels, body(): pl.pallas_call(regroup_kernel, out_shape=[jax.ShapeDtypeStruct((planes, 1...  2.28 us
    pallas_call x1, Pallas kernels, body(): pl.pallas_call(main_kernel, out_shape=jax.ShapeDtypeStruct((filts, 13, 16...  2.19 us
  transfers between devices with their start and end apart: 4, of which 2 were waited for; matrix products, arithmetic and copies ran while one was open for 0% of the time, Pallas kernels for 4%

profile of v4, /device:TPU:0, one launch (start us, length us, event | category | flops | bytes accessed | tf_op | source)
XLA Modules:
  0.0 46.3 jit_solution(17140049933612337351)
XLA Ops:
  0.6 2.3 %regroup.1 = (bf16[4,256,128]{2,1,0:T(8,128)(2,1)S(1)}, bf16[3,256,128]{2,1,0:T(8,128)(2,1)S(1)}, bf16[4,11,16,128]{3,2,1,0:T(8,128)(2,1)}) custom-call(bf16[4,4,16,512]{3,2,1,0:T(8,128)(2,1)} %volume_in.1, bf16[27,16,32]{2,1,0:T(8,128)(2,1)} %bitcast.7, bf16[16,16,128]{2,1,0:T(8,128)(2,1)} %bitcast.9), custom_call_target="tpu_custom_call" | custom-call | tf_op jit(solution)/shard_map/regroup/pallas_call | solution.py:279
  2.9 2.4 %collective-permute-start = (bf16[3,256,128]{2,1,0:T(8,128)(2,1)S(1)}, bf16[3,256,128]{2,1,0:T(8,128)(2,1)S(1)}, u32[]{:S(2)}, u32[]{:S(2)}) collective-permute-start(bf16[3,256,128]{2,1,0:T(8,128)(2,1)S(1)} %get-tuple-element.13), channel_id=1, source_target_pairs={{0,4},{4,8},{8,12},{12,16},{16,20},{20,24},{24,28},{1,5},{5,9},{9,... | collective-permute-start | bytes 589832 | tf_op jit(solution)/shard_map/ppermute | solution.py:297
  5.3 5.7 %all-to-all-start = ((bf16[4,11,16,128]{3,2,1,0:T(8,128)(2,1)}), bf16[4,11,16,128]{3,2,1,0:T(8,128)(2,1)S(1)}, u32[]{:S(2)}, u32[]{:S(2)}) async-start(bf16[4,11,16,128]{3,2,1,0:T(8,128)(2,1)} %get-tuple-element.14), calls=%async_computation | async-start | bytes 360448 | tf_op jit(solution)/shard_map/all_to_all | solution.py:298
  11.0 0.0 collective-permute-done.slab_x
  11.0 0.0 copy-start.1
  11.0 0.0 copy-start
  11.0 4.1 %collective-permute-start.1 = (bf16[7,48,128]{2,1,0:T(8,128)(2,1)S(1)}, bf16[7,48,128]{2,1,0:T(8,128)(2,1)S(1)}, u32[]{:S(2)}, u32[]{:S(2)}) collective-permute-start(bf16[7,48,128]{2,1,0:T(8,128)(2,1)S(1)} %border.1), channel_id=1, source_target_pairs={{0,1},{1,2},{2,3},{4,5},{5,6},{6,7},{8,9},{9,10},{10,11},{12,13},{... | collective-permute-start | bytes 258056 | tf_op jit(solution)/shard_map/ppermute | solution.py:307
  15.1 0.0 copy-done.1
  15.1 0.1 copy.10
  15.2 0.0 copy-done
  15.2 0.8 %stem_inner.1 = (bf16[96,144]{1,0:T(8,128)(2,1)S(1)}, bf16[7,48,896]{2,1,0:T(8,128)(2,1)S(1)}, f32[3,64,896]{2,1,0:T(8,128)S(1)}, bf16[3,96,896]{2,1,0:T(8,128)(2,1)S(1)}) custom-call(bf16[4,256,128]{2,1,0:T(8,128)(2,1)S(1)} %get-tuple-element.12.own, bf16[3,256,128]{2,1,0:T(8,128)(2,1)S(1)} %collective-permute-done.slab_x, bf16[32,128]{1,0:T(8,128)(2,1)S(1)} %pad.4.stem_w, ...), custom_call_target="tpu_custom_call" | custom-call | flops 200000000 | bytes 4000000 | tf_op jit(solution)/shard_map/stem_inner/pallas_call | solution.py:311
  16.1 2.1 %all-to-all-done.gathered = bf16[4,11,16,128]{3,2,1,0:T(8,128)(2,1)S(1)} async-done(((bf16[4,11,16,128]{3,2,1,0:T(8,128)(2,1)}), bf16[4,11,16,128]{3,2,1,0:T(8,128)(2,1)S(1)}, u32[]{:S(2)}, u32[]{:S(2)}) %all-to-all-start) | async-done | bytes 180256 | tf_op jit(solution)/shard_map/all_to_all | solution.py:298
  18.2 0.0 collective-permute-done.1.border
  18.2 2.2 %sections.1 = bf16[4,13,16,128]{3,2,1,0:T(8,128)(2,1)S(1)} custom-call(bf16[4,256,128]{2,1,0:T(8,128)(2,1)S(1)} %get-tuple-element.12.own, bf16[3,256,128]{2,1,0:T(8,128)(2,1)S(1)} %collective-permute-done.slab_x, bf16[7,48,128]{2,1,0:T(8,128)(2,1)S(1)} %collective-permute-done.1.border, bf16[3,128,144]{2,1,0:T(8,128)(2,1)S(1)} %copy-done, ...), custom_call_target="tpu_custom_call" | custom-call | tf_op jit(solution)/shard_map/sections/pallas_call | solution.py:325
  20.4 13.7 %all_to_all.15.parts = bf16[4,13,16,128]{3,2,1,0:T(8,128)(2,1)S(1)} all-to-all(bf16[4,13,16,128]{3,2,1,0:T(8,128)(2,1)S(1)} %sections.1), channel_id=1, replica_groups=mesh['space'=8,'filt'=4] {'filt'}, dimensions={0} | all-to-all | bytes 425984 | tf_op jit(solution)/shard_map/all_to_all | solution.py:341
  34.1 0.7 %sums.1 = bf16[8,9,16,128]{3,2,1,0:T(8,128)(2,1)} custom-call(bf16[4,13,16,128]{3,2,1,0:T(8,128)(2,1)S(1)} %all_to_all.15.parts), custom_call_target="tpu_custom_call" | custom-call | tf_op jit(solution)/shard_map/sums/pallas_call | solution.py:342
  34.9 3.4 %all-to-all-start.2 = ((bf16[8,9,16,128]{3,2,1,0:T(8,128)(2,1)}), bf16[8,9,16,128]{3,2,1,0:T(8,128)(2,1)S(1)}, u32[]{:S(2)}, u32[]{:S(2)}) async-start(bf16[8,9,16,128]{3,2,1,0:T(8,128)(2,1)} %sums.1), calls=%async_computation.2 | async-start | bytes 589824 | tf_op jit(solution)/shard_map/all_to_all | solution.py:359
  38.3 0.8 %features.1 = bf16[16,16,128]{2,1,0:T(8,128)(2,1)} custom-call(bf16[4,13,16,128]{3,2,1,0:T(8,128)(2,1)S(1)} %all_to_all.15.parts), custom_call_target="tpu_custom_call" | custom-call | flops 20000000 | bytes 2000000 | tf_op jit(solution)/shard_map/features/pallas_call | solution.py:350
  39.1 6.4 %all-to-all-done.2.sums = bf16[8,9,16,128]{3,2,1,0:T(8,128)(2,1)S(1)} async-done(((bf16[8,9,16,128]{3,2,1,0:T(8,128)(2,1)}), bf16[8,9,16,128]{3,2,1,0:T(8,128)(2,1)S(1)}, u32[]{:S(2)}, u32[]{:S(2)}) %all-to-all-start.2) | async-done | bytes 294944 | tf_op jit(solution)/shard_map/all_to_all | solution.py:359
  45.5 0.8 %unpack.1 = (f32[27,16,32]{2,1,0:T(8,128)}, f32[27,4,32]{2,1,0:T(4,128)}) custom-call(bf16[8,9,16,128]{3,2,1,0:T(8,128)(2,1)S(1)} %all-to-all-done.2.sums), custom_call_target="tpu_custom_call" | custom-call | tf_op jit(solution)/shard_map/unpack/pallas_call | solution.py:360
  (3 shorter events, 0.0 us)
Async XLA Ops:
  2.9 8.1 %collective-permute-start = (bf16[3,256,128]{2,1,0:T(8,128)(2,1)S(1)}, bf16[3,256,128]{2,1,0:T(8,128)(2,1)S(1)}, u32[]{:S(2)}, u32[]{:S(2)}) collective-permute-start(bf16[3,256,128]{2,1,0:T(8,128)(2,1)S(1)} %get-tuple-element.13), channel_id=1, source_target_pairs={{0,4},{4,8},{8,12},{12,16},{16,20},{20,24},{24,28},{1,5},{5,9},{9,... | collective-permute-start | bytes 589832 | tf_op jit(solution)/shard_map/ppermute | solution.py:297
  5.3 12.9 %all-to-all-start = ((bf16[4,11,16,128]{3,2,1,0:T(8,128)(2,1)}), bf16[4,11,16,128]{3,2,1,0:T(8,128)(2,1)S(1)}, u32[]{:S(2)}, u32[]{:S(2)}) async-start(bf16[4,11,16,128]{3,2,1,0:T(8,128)(2,1)} %get-tuple-element.14), calls=%async_computation | async-start | bytes 360448 | tf_op jit(solution)/shard_map/all_to_all | solution.py:298
  11.0 4.1 %copy-start.1 = (bf16[27,4,32]{2,1,0:T(4,128)(2,1)S(1)}, bf16[27,4,32]{2,1,0:T(4,128)(2,1)}, u32[]{:S(2)}) copy-start(bf16[27,4,32]{2,1,0:T(4,128)(2,1)} %param.6) | copy-start | bytes 20740
  11.0 4.2 %copy-start = (bf16[3,128,144]{2,1,0:T(8,128)(2,1)S(1)}, bf16[3,128,144]{2,1,0:T(8,128)(2,1)}, u32[]{:S(2)}) copy-start(bf16[3,128,144]{2,1,0:T(8,128)(2,1)} %constant.5.clone.place) | copy-start | bytes 331780
  11.0 7.2 %collective-permute-start.1 = (bf16[7,48,128]{2,1,0:T(8,128)(2,1)S(1)}, bf16[7,48,128]{2,1,0:T(8,128)(2,1)S(1)}, u32[]{:S(2)}, u32[]{:S(2)}) collective-permute-start(bf16[7,48,128]{2,1,0:T(8,128)(2,1)S(1)} %border.1), channel_id=1, source_target_pairs={{0,1},{1,2},{2,3},{4,5},{5,6},{6,7},{8,9},{9,10},{10,11},{12,13},{... | collective-permute-start | bytes 258056 | tf_op jit(solution)/shard_map/ppermute | solution.py:307
  34.9 10.6 %all-to-all-start.2 = ((bf16[8,9,16,128]{3,2,1,0:T(8,128)(2,1)}), bf16[8,9,16,128]{3,2,1,0:T(8,128)(2,1)S(1)}, u32[]{:S(2)}, u32[]{:S(2)}) async-start(bf16[8,9,16,128]{3,2,1,0:T(8,128)(2,1)} %sums.1), calls=%async_computation.2 | async-start | bytes 589824 | tf_op jit(solution)/shard_map/all_to_all | solution.py:359

commit v5 on v4

--- a/solution.py
+++ b/solution.py
@@ -46,21 +46,37 @@
     return (source == column).astype(F32).astype(BF16)
 
 
-def regroup_kernel(volume_in, weight_in, cotangent_in, own, slab_x, packed, volume, weight, cotangent, sems):
+def regroup_kernel(volume_in, weight_in, cotangent_in, own, slab_x, packed_out, volume, weight, cotangent, packed, sems):
     copies = [
         pltpu.make_async_copy(source, target, sems.at[k])
         for k, (source, target) in enumerate(
-            [(volume_in, volume), (weight_in, weight), (cotangent_in, cotangent)]
+            [(weight_in, weight), (cotangent_in, cotangent), (volume_in, volume), (packed, packed_out)]
         )
     ]
-    for copy in copies:
+    for copy in copies[:3]:
         copy.start()
     channels, planes, width, depth = volume.shape
     z, column = rows_lanes((depth, depth))
     source = lax.shift_left(column & (LANES - 1), 2) + lax.shift_right_logical(column, 7)
     select = (z == source).astype(F32).astype(BF16)
     turn = turn_matrix()
+
+    blank = jnp.zeros((16, 32), BF16)
     copies[0].wait()
+    taps = [weight[t] if t < 27 else blank for t in range(28)]
+    for t in range(7):
+        tile = jnp.concatenate(taps[4 * t : 4 * t + 4], axis=1)
+        for f in range(packed.shape[0]):
+            packed[f, t] = tile
+    copies[1].wait()
+    turned = nn(turn, cotangent[...].reshape(256, LANES)).astype(BF16)
+    for f in range(packed.shape[0]):
+        for j in range(4):
+            row = 16 * (4 * f + j)
+            packed[f, 7 + j] = turned[row : row + 16]
+    copies[3].start()
+
+    copies[2].wait()
     picked = nn(volume[...].reshape(channels * planes * width, depth), select).astype(BF16)
     grouped = []
     for x in range(planes):
@@ -70,26 +86,13 @@
                 start = (c * planes + x) * width
                 parts.append(picked[start : start + width, phase * LANES : (phase + 1) * LANES])
         grouped.append(jnp.concatenate(parts, axis=0))
-    copies[1].wait()
-    copies[2].wait()
-    grouped.append(cotangent[...].reshape(256, LANES))
     turned = nn(turn, jnp.concatenate(grouped, axis=1)).astype(BF16)
     for x in range(planes):
         plane = turned[:, x * LANES : (x + 1) * LANES]
         own[x] = plane
         if x > 0:
             slab_x[x - 1] = plane
-
-    blank = jnp.zeros((16, 32), BF16)
-    taps = [weight[t] if t < 27 else blank for t in range(28)]
-    for t in range(7):
-        tile = jnp.concatenate(taps[4 * t : 4 * t + 4], axis=1)
-        for f in range(packed.shape[0]):
-            packed[f, t] = tile
-    for f in range(packed.shape[0]):
-        for j in range(4):
-            row = 16 * (4 * f + j)
-            packed[f, 7 + j] = turned[row : row + 16, planes * LANES :]
+    copies[3].wait()
 
 
 def border_kernel(slab_x, own, border):
@@ -249,12 +252,9 @@
         sums[s] = total
 
 
-def features_kernel(parts, features):
+def unpack_kernel(middle_scale, stem_scale, sums, parts, features, middle, stem):
     rows = [parts[f, 9 + j] for f in range(parts.shape[0]) for j in range(4)]
     features[...] = nn(turn_matrix(), jnp.concatenate(rows, axis=0)).astype(BF16).reshape(16, 16, LANES)
-
-
-def unpack_kernel(middle_scale, stem_scale, sums, middle, stem):
     total = jnp.sum(sums[...].astype(F32), axis=0)
     for t in range(27):
         start = 32 * (t % 4)
@@ -284,12 +284,13 @@
             jax.ShapeDtypeStruct((filts, 11, 16, LANES), BF16),
         ],
         in_specs=[pl.BlockSpec(memory_space=pltpu.HBM)] * 3,
-        out_specs=whole(3),
+        out_specs=whole(2) + [pl.BlockSpec(memory_space=pl.ANY)],
         scratch_shapes=[
             pltpu.VMEM(volume.shape, BF16),
             pltpu.VMEM((27, 16, 32), BF16),
             pltpu.VMEM((16, 16, LANES), BF16),
-            pltpu.SemaphoreType.DMA((3,)),
+            pltpu.VMEM((filts, 11, 16, LANES), BF16),
+            pltpu.SemaphoreType.DMA((4,)),
         ],
         compiler_params=limit,
         name="regroup",
@@ -347,27 +348,19 @@
         compiler_params=limit,
         name="sums",
     )(parts)
-    features = pl.pallas_call(
-        features_kernel,
-        out_shape=jax.ShapeDtypeStruct((16, 16, LANES), BF16),
-        in_specs=whole(1),
-        out_specs=whole(1)[0],
-        compiler_params=limit,
-        cost_estimate=pl.CostEstimate(flops=20_000_000, bytes_accessed=2_000_000, transcendentals=0),
-        name="features",
-    )(parts)
     sums = lax.all_to_all(sums, "space", 0, 0, tiled=True)
-    middle, stem = pl.pallas_call(
+    features, middle, stem = pl.pallas_call(
         functools.partial(unpack_kernel, middle_cells**-0.5, stem_cells**-0.5),
         out_shape=[
+            jax.ShapeDtypeStruct((16, 16, LANES), BF16),
             jax.ShapeDtypeStruct((27, 16, 32), F32),
             jax.ShapeDtypeStruct((27, 4, 32), F32),
         ],
-        in_specs=whole(1),
-        out_specs=whole(2),
+        in_specs=whole(2),
+        out_specs=whole(3),
         compiler_params=limit,
         name="unpack",
-    )(sums)
+    )(sums, parts)
     return features.reshape(16, 1, 16, LANES), middle.transpose(0, 2, 1), stem
 
 

time: 46.7 us -> 45 us (0.964)
  blocking collectives: 13.7 us -> 23.8 us
  waiting for transfers between devices: 8.53 us -> 2.12 us
  starting transfers between devices: 15.6 us -> 12.1 us
  Pallas kernels: 7.65 us -> 5.81 us
    all_to_all x0 -> x1, blocking collectives: none -> 10 us  [body(): sums = lax.all_to_all(sums, 'space', 0, 0, tiled=True)]
    all_to_all x1 -> x0, waiting for transfers between devices: 6.41 us -> none  [body(): sums = lax.all_to_all(sums, 'space', 0, 0, tiled=True)]
    all_to_all x1 -> x0, starting transfers between devices: 3.42 us -> none  [body(): sums = lax.all_to_all(sums, 'space', 0, 0, tiled=True)]
    pallas_call x1 -> x0, Pallas kernels: 0.81 us -> none  [body(): pl.pallas_call(features_kernel, out_shape=jax.ShapeDtypeStruct((16, 16, L...]
    pallas_call x1, Pallas kernels: 0.74 us -> 0.03 us  [body(): pl.pallas_call(sum_kernel, out_shape=jax.ShapeDtypeStruct((spaces, 9, 16,...]
  transfers between devices with their start and end apart: 4 -> 3, of which waited for: 2 -> 1; matrix products, arithmetic and copies ran while one was open for 0% -> 0% of each run, Pallas kernels for 4% -> 2%
where the time goes in v5:
time: 45 us; the launch traced here: 44.7 us
  blocking collectives  23.8 us (53%)
  starting transfers between devices  12.1 us (27%)
  Pallas kernels  5.81 us (13%)
  waiting for transfers between devices  2.12 us (5%)
  between operations  0.71 us (2%)
    all_to_all x1, blocking collectives, body(): parts = lax.all_to_all(parts, 'filt', 0, 0, tiled=True)  13.7 us
    all_to_all x1, blocking collectives, body(): sums = lax.all_to_all(sums, 'space', 0, 0, tiled=True)  10 us
    all_to_all x1, starting transfers between devices, body(): gathered = lax.all_to_all(packed, 'filt', 0, 0, tiled=True)  5.71 us
    ppermute x1, starting transfers between devices, body(): border = lax.ppermute(border, 'filt', [(f - 1, f) for f in range(1, filts)])  4.06 us
    ppermute x1, starting transfers between devices, body(): lax.ppermute(slab_x, 'space', [(s - 1, s) for s in range(1, spaces)])  2.37 us
    pallas_call x1, Pallas kernels, body(): pl.pallas_call(main_kernel, out_shape=jax.ShapeDtypeStruct((filts, 13, 16...  2.19 us
    all_to_all x1, waiting for transfers between devices, body(): gathered = lax.all_to_all(packed, 'filt', 0, 0, tiled=True)  2.12 us
    pallas_call x1, Pallas kernels, body(): pl.pallas_call(regroup_kernel, out_shape=[jax.ShapeDtypeStruct((planes, 1...  1.88 us
  transfers between devices with their start and end apart: 3, of which 1 were waited for; matrix products, arithmetic and copies ran while one was open for 0% of the time, Pallas kernels for 2%

profile of v5, /device:TPU:0, one launch (start us, length us, event | category | flops | bytes accessed | tf_op | source)
XLA Modules:
  0.0 44.7 jit_solution(1659071056118598269)
XLA Ops:
  0.6 1.9 %regroup.1 = (bf16[4,256,128]{2,1,0:T(8,128)(2,1)S(1)}, bf16[3,256,128]{2,1,0:T(8,128)(2,1)S(1)}, bf16[4,11,16,128]{3,2,1,0:T(8,128)(2,1)}) custom-call(bf16[4,4,16,512]{3,2,1,0:T(8,128)(2,1)} %volume_in.1, bf16[27,16,32]{2,1,0:T(8,128)(2,1)} %bitcast.7, bf16[16,16,128]{2,1,0:T(8,128)(2,1)} %bitcast.8), custom_call_target="tpu_custom_call" | custom-call | tf_op jit(solution)/shard_map/regroup/pallas_call | solution.py:279
  2.5 2.4 %collective-permute-start = (bf16[3,256,128]{2,1,0:T(8,128)(2,1)S(1)}, bf16[3,256,128]{2,1,0:T(8,128)(2,1)S(1)}, u32[]{:S(2)}, u32[]{:S(2)}) collective-permute-start(bf16[3,256,128]{2,1,0:T(8,128)(2,1)S(1)} %get-tuple-element.14), channel_id=1, source_target_pairs={{0,4},{4,8},{8,12},{12,16},{16,20},{20,24},{24,28},{1,5},{5,9},{9,... | collective-permute-start | bytes 589832 | tf_op jit(solution)/shard_map/ppermute | solution.py:298
  4.9 5.7 %all-to-all-start = ((bf16[4,11,16,128]{3,2,1,0:T(8,128)(2,1)}), bf16[4,11,16,128]{3,2,1,0:T(8,128)(2,1)S(1)}, u32[]{:S(2)}, u32[]{:S(2)}) async-start(bf16[4,11,16,128]{3,2,1,0:T(8,128)(2,1)} %get-tuple-element.15), calls=%async_computation | async-start | bytes 360448 | tf_op jit(solution)/shard_map/all_to_all | solution.py:299
  10.6 0.0 collective-permute-done.slab_x
  10.6 0.0 copy-start.1
  10.6 0.0 copy-start
  10.6 4.1 %collective-permute-start.1 = (bf16[7,48,128]{2,1,0:T(8,128)(2,1)S(1)}, bf16[7,48,128]{2,1,0:T(8,128)(2,1)S(1)}, u32[]{:S(2)}, u32[]{:S(2)}) collective-permute-start(bf16[7,48,128]{2,1,0:T(8,128)(2,1)S(1)} %border.1), channel_id=1, source_target_pairs={{0,1},{1,2},{2,3},{4,5},{5,6},{6,7},{8,9},{9,10},{10,11},{12,13},{... | collective-permute-start | bytes 258056 | tf_op jit(solution)/shard_map/ppermute | solution.py:308
  14.7 0.0 copy-done.1
  14.7 0.1 copy.10
  14.8 0.0 copy-done
  14.8 0.8 %stem_inner.1 = (bf16[96,144]{1,0:T(8,128)(2,1)S(1)}, bf16[7,48,896]{2,1,0:T(8,128)(2,1)S(1)}, f32[3,64,896]{2,1,0:T(8,128)S(1)}, bf16[3,96,896]{2,1,0:T(8,128)(2,1)S(1)}) custom-call(bf16[4,256,128]{2,1,0:T(8,128)(2,1)S(1)} %get-tuple-element.13.own, bf16[3,256,128]{2,1,0:T(8,128)(2,1)S(1)} %collective-permute-done.slab_x, bf16[32,128]{1,0:T(8,128)(2,1)S(1)} %pad.4.stem_w, ...), custom_call_target="tpu_custom_call" | custom-call | flops 200000000 | bytes 4000000 | tf_op jit(solution)/shard_map/stem_inner/pallas_call | solution.py:312
  15.7 2.1 %all-to-all-done.gathered = bf16[4,11,16,128]{3,2,1,0:T(8,128)(2,1)S(1)} async-done(((bf16[4,11,16,128]{3,2,1,0:T(8,128)(2,1)}), bf16[4,11,16,128]{3,2,1,0:T(8,128)(2,1)S(1)}, u32[]{:S(2)}, u32[]{:S(2)}) %all-to-all-start) | async-done | bytes 180256 | tf_op jit(solution)/shard_map/all_to_all | solution.py:299
  17.8 0.0 collective-permute-done.1.border
  17.8 2.2 %sections.1 = bf16[4,13,16,128]{3,2,1,0:T(8,128)(2,1)S(1)} custom-call(bf16[4,256,128]{2,1,0:T(8,128)(2,1)S(1)} %get-tuple-element.13.own, bf16[3,256,128]{2,1,0:T(8,128)(2,1)S(1)} %collective-permute-done.slab_x, bf16[7,48,128]{2,1,0:T(8,128)(2,1)S(1)} %collective-permute-done.1.border, bf16[3,128,144]{2,1,0:T(8,128)(2,1)S(1)} %copy-done, ...), custom_call_target="tpu_custom_call" | custom-call | tf_op jit(solution)/shard_map/sections/pallas_call | solution.py:326
  20.0 13.7 %all_to_all.15.parts = bf16[4,13,16,128]{3,2,1,0:T(8,128)(2,1)S(1)} all-to-all(bf16[4,13,16,128]{3,2,1,0:T(8,128)(2,1)S(1)} %sections.1), channel_id=1, replica_groups=mesh['space'=8,'filt'=4] {'filt'}, dimensions={0} | all-to-all | bytes 425984 | tf_op jit(solution)/shard_map/all_to_all | solution.py:342
  33.8 10.0 %all_to_all.16.sums = bf16[8,9,16,128]{3,2,1,0:T(8,128)(2,1)S(1)} all-to-all(bf16[8,9,16,128]{3,2,1,0:T(8,128)(2,1)S(1)} %sums.1), channel_id=1, replica_groups=mesh['space'=8,'filt'=4] {'space'}, dimensions={0} | all-to-all | bytes 589824 | tf_op jit(solution)/shard_map/all_to_all | solution.py:351
  43.8 0.9 %unpack.1 = (bf16[16,16,128]{2,1,0:T(8,128)(2,1)}, f32[27,16,32]{2,1,0:T(8,128)}, f32[27,4,32]{2,1,0:T(4,128)}) custom-call(bf16[8,9,16,128]{3,2,1,0:T(8,128)(2,1)S(1)} %all_to_all.16.sums, bf16[4,13,16,128]{3,2,1,0:T(8,128)(2,1)S(1)} %all_to_all.15.parts), custom_call_target="tpu_custom_call" | custom-call | tf_op jit(solution)/shard_map/unpack/pallas_call | solution.py:352
  (4 shorter events, 0.1 us)
Async XLA Ops:
  2.5 8.1 %collective-permute-start = (bf16[3,256,128]{2,1,0:T(8,128)(2,1)S(1)}, bf16[3,256,128]{2,1,0:T(8,128)(2,1)S(1)}, u32[]{:S(2)}, u32[]{:S(2)}) collective-permute-start(bf16[3,256,128]{2,1,0:T(8,128)(2,1)S(1)} %get-tuple-element.14), channel_id=1, source_target_pairs={{0,4},{4,8},{8,12},{12,16},{16,20},{20,24},{24,28},{1,5},{5,9},{9,... | collective-permute-start | bytes 589832 | tf_op jit(solution)/shard_map/ppermute | solution.py:298
  4.9 12.9 %all-to-all-start = ((bf16[4,11,16,128]{3,2,1,0:T(8,128)(2,1)}), bf16[4,11,16,128]{3,2,1,0:T(8,128)(2,1)S(1)}, u32[]{:S(2)}, u32[]{:S(2)}) async-start(bf16[4,11,16,128]{3,2,1,0:T(8,128)(2,1)} %get-tuple-element.15), calls=%async_computation | async-start | bytes 360448 | tf_op jit(solution)/shard_map/all_to_all | solution.py:299
  10.6 4.1 %copy-start.1 = (bf16[27,4,32]{2,1,0:T(4,128)(2,1)S(1)}, bf16[27,4,32]{2,1,0:T(4,128)(2,1)}, u32[]{:S(2)}) copy-start(bf16[27,4,32]{2,1,0:T(4,128)(2,1)} %param.6) | copy-start | bytes 20740
  10.6 4.2 %copy-start = (bf16[3,128,144]{2,1,0:T(8,128)(2,1)S(1)}, bf16[3,128,144]{2,1,0:T(8,128)(2,1)}, u32[]{:S(2)}) copy-start(bf16[3,128,144]{2,1,0:T(8,128)(2,1)} %constant.5.clone.place) | copy-start | bytes 331780
  10.6 7.2 %collective-permute-start.1 = (bf16[7,48,128]{2,1,0:T(8,128)(2,1)S(1)}, bf16[7,48,128]{2,1,0:T(8,128)(2,1)S(1)}, u32[]{:S(2)}, u32[]{:S(2)}) collective-permute-start(bf16[7,48,128]{2,1,0:T(8,128)(2,1)S(1)} %border.1), channel_id=1, source_target_pairs={{0,1},{1,2},{2,3},{4,5},{5,6},{6,7},{8,9},{9,10},{10,11},{12,13},{... | collective-permute-start | bytes 258056 | tf_op jit(solution)/shard_map/ppermute | solution.py:308

commit v6 on v5

--- a/solution.py
+++ b/solution.py
@@ -47,15 +47,12 @@
 
 
 def regroup_kernel(volume_in, weight_in, cotangent_in, own, slab_x, packed_out, volume, weight, cotangent, packed, sems):
-    copies = [
-        pltpu.make_async_copy(source, target, sems.at[k])
-        for k, (source, target) in enumerate(
-            [(weight_in, weight), (cotangent_in, cotangent), (volume_in, volume), (packed, packed_out)]
-        )
-    ]
-    for copy in copies[:3]:
+    channels, planes, width, depth = volume.shape
+    pairs = [(weight_in, weight), (cotangent_in, cotangent), (packed, packed_out)]
+    pairs += [(volume_in.at[c], volume.at[c]) for c in range(channels)]
+    copies = [pltpu.make_async_copy(*pair, sems.at[k]) for k, pair in enumerate(pairs)]
+    for copy in copies[:2] + copies[3:]:
         copy.start()
-    channels, planes, width, depth = volume.shape
     z, column = rows_lanes((depth, depth))
     source = lax.shift_left(column & (LANES - 1), 2) + lax.shift_right_logical(column, 7)
     select = (z == source).astype(F32).astype(BF16)
@@ -74,9 +71,10 @@
         for j in range(4):
             row = 16 * (4 * f + j)
             packed[f, 7 + j] = turned[row : row + 16]
-    copies[3].start()
-
-    copies[2].wait()
+    copies[2].start()
+
+    for copy in copies[3:]:
+        copy.wait()
     picked = nn(volume[...].reshape(channels * planes * width, depth), select).astype(BF16)
     grouped = []
     for x in range(planes):
@@ -92,7 +90,7 @@
         own[x] = plane
         if x > 0:
             slab_x[x - 1] = plane
-    copies[3].wait()
+    copies[2].wait()
 
 
 def border_kernel(slab_x, own, border):
@@ -146,8 +144,81 @@
         slope[i], taps[i] = stem_forward(weights[...], cols, i, keep_space() if i == 0 else 1.0)
 
 
-def main_kernel(
-    own, slab_x, border, place, gathered, weights, cols, slope, taps, parts, low_cols, mid_w, mid_cols, stem_back, low_back,
+def fill_taps(mid_cols, part, i, j, first, count):
+    for b in range(3):
+        if (j - b) % 2 == 0 and first <= (j - b) // 2 < first + count:
+            row = 96 * (3 * i + b)
+            mid_cols[row : row + 96, pl.ds(((j - b) // 2 - first) * LANES, LANES)] = part
+
+
+def middle_cells_step(mid_w, mid_cols, cotangent):
+    pre = nn(mid_w[:, 0:864], mid_cols[...])
+    soft, sig = softplus_sigmoid(pre)
+    delta = cotangent.astype(F32) * (0.3 + 0.7 * sig)
+    delta_low = delta.astype(BF16)
+    mid_grad = nt(delta_low, mid_cols[...])
+    both = jnp.concatenate([delta_low, roll_blocks(delta, -1).astype(BF16)], axis=0)
+    return (0.3 * pre + 0.7 * soft).astype(BF16), mid_grad, both
+
+
+def put_back(target, i, start, part):
+    lanes = pl.ds(start, LANES)
+    target[i, 0:64, lanes] = part.astype(BF16)
+    target[i, 64:96, lanes] = roll_blocks(part[0:32], -1).astype(BF16)
+
+
+def upper_kernel(
+    gathered, cols, slope, taps, features, mid_grad, stem_grad, mid_w, odd_w, even_w, mid_cols, stem_back,
+):
+    blocks = gathered.shape[0]
+    for f in range(blocks):
+        for t in range(7):
+            mid_w[16 * f : 16 * f + 16, t * LANES : (t + 1) * LANES] = gathered[f, t]
+    for i in range(3):
+        for j in range(2, 9):
+            fill_taps(mid_cols, taps[i, :, pl.ds((j - 2) * LANES, LANES)], i, j, 1, 3)
+    cotangent = jnp.concatenate(
+        [jnp.concatenate([gathered[f, 7 + j] for j in range(1, 4)], axis=1) for f in range(blocks)], axis=0
+    )
+    features[...], mid_grad[...], both = middle_cells_step(mid_w, mid_cols, cotangent)
+
+    turned = jnp.concatenate(
+        [mid_w[:, t * LANES : (t + 1) * LANES].astype(F32).T for t in range(7)], axis=0
+    ).astype(BF16)
+    zero = jnp.zeros((32, blocks * 16), BF16)
+
+    def block(a, b, d):
+        row = 32 * (9 * a + 3 * b + d)
+        return turned[row : row + 32]
+
+    def wide(a, b):
+        even = jnp.concatenate([block(a, b, 1), zero], axis=1)
+        odd = jnp.concatenate([block(a, b, 2), block(a, b, 0)], axis=1)
+        return jnp.concatenate([even, odd], axis=0)
+
+    odd_w[...] = jnp.concatenate([wide(i, 1) for i in range(3)], axis=0)
+    even_w[...] = jnp.concatenate(
+        [jnp.concatenate([wide(i, 0), wide(i, 2)], axis=1) for i in range(3)], axis=0
+    )
+    nothing = jnp.zeros((2 * blocks * 16, LANES), BF16)
+    pair = jnp.concatenate(
+        [jnp.concatenate([both, nothing], axis=1), jnp.concatenate([nothing, both], axis=1)], axis=0
+    )
+    odd_back = nn(odd_w[...], both)
+    even_back = nn(even_w[...], pair)
+    total = jnp.zeros((96, STEM_ROWS), F32)
+    for i in range(3):
+        for j in range(7):
+            source = even_back if j % 2 == 0 else odd_back
+            part = source[64 * i : 64 * i + 64, (j // 2) * LANES : (j // 2 + 1) * LANES]
+            put_back(stem_back, i, j * LANES, part * slope[i, :, pl.ds(j * LANES, LANES)])
+        total += nt(stem_back[i], cols[2 * i : 2 * i + 3].reshape(STEM_ROWS, 7 * LANES))
+    stem_grad[...] = total
+
+
+def lower_kernel(
+    own, slab_x, border, place, gathered, weights, cols, slope, taps, upper_features, upper_mid, upper_stem,
+    mid_w, odd_w, even_w, parts, low_cols, mid_cols, low_back,
 ):
     blocks = gathered.shape[0]
     keep_y = jnp.where(lax.axis_index("filt") > 0, 1.0, 0.0).astype(F32)
@@ -163,78 +234,32 @@
             keep = keep * keep_space()
         one_slope, low_taps = stem_forward(weights[...], low_cols, i, keep)
         low_slope.append(one_slope)
-        for j in range(9):
-            if j < 2:
-                part = low_taps[:, j * LANES : (j + 1) * LANES]
-            else:
-                part = taps[i, :, pl.ds((j - 2) * LANES, LANES)]
-            for b in range(3):
-                if (j - b) % 2 == 0 and 0 <= (j - b) // 2 < 4:
-                    row = 96 * (3 * i + b)
-                    mid_cols[row : row + 96, pl.ds((j - b) // 2 * LANES, LANES)] = part
-
-    for f in range(blocks):
-        for t in range(7):
-            mid_w[16 * f : 16 * f + 16, t * LANES : (t + 1) * LANES] = gathered[f, t]
-    cotangent = jnp.concatenate(
-        [
-            jnp.concatenate([gathered[f, 7 + j] for j in range(4)], axis=1)
-            for f in range(blocks)
-        ],
-        axis=0,
-    )
-    pre = nn(mid_w[:, 0:864], mid_cols[...])
-    soft, sig = softplus_sigmoid(pre)
-    features = (0.3 * pre + 0.7 * soft).astype(BF16)
-    delta = cotangent.astype(F32) * (0.3 + 0.7 * sig)
-    delta_low = delta.astype(BF16)
-    mid_grad = nt(delta_low, mid_cols[...])
-
-    turned = jnp.concatenate(
-        [mid_w[:, t * LANES : (t + 1) * LANES].astype(F32).T for t in range(7)], axis=0
-    ).astype(BF16)
-    zero = jnp.zeros((32, blocks * 16), BF16)
-
-    def block(a, b, d):
-        row = 32 * (9 * a + 3 * b + d)
-        return turned[row : row + 32]
-
-    def wide(a, b):
-        even = jnp.concatenate([block(a, b, 1), zero], axis=1)
-        odd = jnp.concatenate([block(a, b, 2), block(a, b, 0)], axis=1)
-        return jnp.concatenate([even, odd], axis=0)
-
-    both = jnp.concatenate([delta_low, roll_blocks(delta, -1).astype(BF16)], axis=0)
-    nothing = jnp.zeros((2 * blocks * 16, LANES), BF16)
-    pair = jnp.concatenate(
-        [jnp.concatenate([both, nothing], axis=1), jnp.concatenate([nothing, both], axis=1)], axis=0
-    )
-    odd_back = nn(jnp.concatenate([wide(i, 1) for i in range(3)], axis=0), both)
-    even_back = nn(
-        jnp.concatenate([jnp.concatenate([wide(i, 0), wide(i, 2)], axis=1) for i in range(3)], axis=0), pair
-    )
-    stem_grad = jnp.zeros((96, STEM_ROWS), F32)
+        for j in range(2):
+            fill_taps(mid_cols, low_taps[:, j * LANES : (j + 1) * LANES], i, j, 0, 1)
+        fill_taps(mid_cols, taps[i, :, 0:LANES], i, 2, 0, 1)
+    cotangent = jnp.concatenate([gathered[f, 7] for f in range(blocks)], axis=0)
+    features, mid_grad, both = middle_cells_step(mid_w, mid_cols, cotangent)
+
+    back = [nn(even_w[:, 0:LANES], both), nn(odd_w[...], both), nn(even_w[:, LANES:], both)]
+    stem_grad = upper_stem[...]
     for i in range(3):
-        for j in range(9):
-            source = even_back if j % 2 == 0 else odd_back
-            part = source[64 * i : 64 * i + 64, (j // 2) * LANES : (j // 2 + 1) * LANES]
-            if j < 2:
-                target, lanes = low_back, pl.ds(j * LANES, LANES)
-                part = part * low_slope[i][:, j * LANES : (j + 1) * LANES]
-            else:
-                target, lanes = stem_back, pl.ds((j - 2) * LANES, LANES)
-                part = part * slope[i, :, lanes]
-            target[i, 0:64, lanes] = part.astype(BF16)
-            target[i, 64:96, lanes] = roll_blocks(part[0:32], -1).astype(BF16)
-        stem_grad += nt(stem_back[i], cols[2 * i : 2 * i + 3].reshape(STEM_ROWS, 7 * LANES))
-        stem_grad += nt(low_back[i], low_cols[2 * i : 2 * i + 3].reshape(STEM_ROWS, 2 * LANES))
+        for j in range(2):
+            part = back[j][64 * i : 64 * i + 64] * low_slope[i][:, j * LANES : (j + 1) * LANES]
+            put_back(low_back, i, j * LANES, part)
+        put_back(low_back, i, 2 * LANES, back[2][64 * i : 64 * i + 64] * slope[i, :, 0:LANES])
+        low = low_cols[2 * i : 2 * i + 3].reshape(STEM_ROWS, 2 * LANES)
+        near = cols[2 * i : 2 * i + 3, :, 0:LANES].reshape(STEM_ROWS, LANES)
+        stem_grad += nt(low_back[i], jnp.concatenate([low, near], axis=1))
     high = stem_grad.astype(BF16)
-    low = (stem_grad - high.astype(F32)).astype(BF16)
-    stem = sum(
-        nt(part[32 * g : 32 * g + 32], place[g]) for part in (high, low) for g in range(3)
-    ).astype(BF16)
-
-    middle = mid_grad.astype(BF16)
+    both = jnp.concatenate([high, (stem_grad - high.astype(F32)).astype(BF16)], axis=0)
+    stem = 0.0
+    for g in range(3):
+        rows = jnp.concatenate([both[32 * g : 32 * g + 32], both[96 + 32 * g : 128 + 32 * g]], axis=0)
+        taken = nt(rows, place[g])
+        stem += taken[0:32] + taken[32:64]
+    stem = stem.astype(BF16)
+
+    middle = (mid_grad + upper_mid[...]).astype(BF16)
     middle = jnp.concatenate([middle, jnp.zeros((blocks * 16, 32), BF16)], axis=1)
     for f in range(blocks):
         rows = slice(16 * f, 16 * f + 16)
@@ -242,8 +267,9 @@
             parts[f, t] = middle[rows, t * LANES : (t + 1) * LANES]
         for half in range(2):
             parts[f, 7 + half] = stem[16 * half : 16 * half + 16]
-        for j in range(4):
-            parts[f, 9 + j] = features[rows, j * LANES : (j + 1) * LANES]
+        parts[f, 9] = features[rows]
+        for j in range(3):
+            parts[f, 10 + j] = upper_features[rows, j * LANES : (j + 1) * LANES]
 
 
 def sum_kernel(parts, sums):
@@ -252,16 +278,29 @@
         sums[s] = total
 
 
-def unpack_kernel(middle_scale, stem_scale, sums, parts, features, middle, stem):
-    rows = [parts[f, 9 + j] for f in range(parts.shape[0]) for j in range(4)]
-    features[...] = nn(turn_matrix(), jnp.concatenate(rows, axis=0)).astype(BF16).reshape(16, 16, LANES)
+def unpack_kernel(
+    middle_scale, stem_scale, sums, parts, features_out, middle_out, stem_out, features, middle, stem, sems,
+):
+    copies = [
+        pltpu.make_async_copy(source, target, sems.at[k])
+        for k, (source, target) in enumerate(
+            [(middle, middle_out), (stem, stem_out), (features, features_out)]
+        )
+    ]
     total = jnp.sum(sums[...].astype(F32), axis=0)
     for t in range(27):
         start = 32 * (t % 4)
         middle[t] = total[t // 4, :, start : start + 32] * middle_scale
+    copies[0].start()
+    rows = [parts[f, 9 + j] for f in range(parts.shape[0]) for j in range(4)]
+    features[...] = nn(turn_matrix(), jnp.concatenate(rows, axis=0)).astype(BF16).reshape(16, 16, LANES)
+    copies[2].start()
     turned = jnp.concatenate([total[7], total[8]], axis=0).T * stem_scale
     for t in range(27):
         stem[t] = turned[4 * t : 4 * t + 4]
+    copies[1].start()
+    for copy in copies:
+        copy.wait()
 
 
 def whole(count):
@@ -290,7 +329,7 @@
             pltpu.VMEM((27, 16, 32), BF16),
             pltpu.VMEM((16, 16, LANES), BF16),
             pltpu.VMEM((filts, 11, 16, LANES), BF16),
-            pltpu.SemaphoreType.DMA((4,)),
+            pltpu.SemaphoreType.DMA((3 + channels,)),
         ],
         compiler_params=limit,
         name="regroup",
@@ -323,21 +362,39 @@
         cost_estimate=pl.CostEstimate(flops=200_000_000, bytes_accessed=4_000_000, transcendentals=500_000),
         name="stem_inner",
     )(own, slab_x, stem_w, place)
+    upper = pl.pallas_call(
+        upper_kernel,
+        out_shape=[
+            jax.ShapeDtypeStruct((64, 3 * LANES), BF16),
+            jax.ShapeDtypeStruct((64, 864), F32),
+            jax.ShapeDtypeStruct((96, STEM_ROWS), F32),
+            jax.ShapeDtypeStruct((64, 896), BF16),
+            jax.ShapeDtypeStruct((192, LANES), BF16),
+            jax.ShapeDtypeStruct((192, 2 * LANES), BF16),
+        ],
+        in_specs=whole(4),
+        out_specs=whole(6),
+        scratch_shapes=[
+            pltpu.VMEM((864, 3 * LANES), BF16),
+            pltpu.VMEM((3, 96, 7 * LANES), BF16),
+        ],
+        compiler_params=limit,
+        cost_estimate=pl.CostEstimate(flops=300_000_000, bytes_accessed=4_000_000, transcendentals=100_000),
+        name="upper_cells",
+    )(gathered, cols, slope, taps)
     parts = pl.pallas_call(
-        main_kernel,
+        lower_kernel,
         out_shape=jax.ShapeDtypeStruct((filts, 13, 16, LANES), BF16),
-        in_specs=whole(9),
+        in_specs=whole(15),
         out_specs=whole(1)[0],
         scratch_shapes=[
             pltpu.VMEM((7, 48, 2 * LANES), BF16),
-            pltpu.VMEM((64, 896), BF16),
-            pltpu.VMEM((864, 512), BF16),
-            pltpu.VMEM((3, 96, 7 * LANES), BF16),
-            pltpu.VMEM((3, 96, 2 * LANES), BF16),
-        ],
-        compiler_params=limit,
-        name="sections",
-    )(own, slab_x, border, place, gathered, weights, cols, slope, taps)
+            pltpu.VMEM((864, LANES), BF16),
+            pltpu.VMEM((3, 96, 3 * LANES), BF16),
+        ],
+        compiler_params=limit,
+        name="lower_cells",
+    )(own, slab_x, border, place, gathered, weights, cols, slope, taps, *upper)
 
     parts = lax.all_to_all(parts, "filt", 0, 0, tiled=True)
     sums = pl.pallas_call(
@@ -357,7 +414,13 @@
             jax.ShapeDtypeStruct((27, 4, 32), F32),
         ],
         in_specs=whole(2),
-        out_specs=whole(3),
+        out_specs=[pl.BlockSpec(memory_space=pl.ANY)] * 3,
+        scratch_shapes=[
+            pltpu.VMEM((16, 16, LANES), BF16),
+            pltpu.VMEM((27, 16, 32), F32),
+            pltpu.VMEM((27, 4, 32), F32),
+            pltpu.SemaphoreType.DMA((3,)),
+        ],
         compiler_params=limit,
         name="unpack",
     )(sums, parts)

time: 45 us -> 47.6 us (1.058)
  blocking collectives: 23.8 us -> 27.2 us
  waiting for transfers between devices: 2.12 us -> 1.05 us
  Pallas kernels: 5.81 us -> 6.53 us
    all_to_all x1, blocking collectives: 10 us -> 15.4 us  [body(): sums = lax.all_to_all(sums, 'space', 0, 0, tiled=True)]
    all_to_all x1, waiting for transfers between devices: 2.12 us -> 0.01 us  [body(): gathered = lax.all_to_all(packed, 'filt', 0, 0, tiled=True)]
    all_to_all x1, blocking collectives: 13.7 us -> 11.8 us  [body(): parts = lax.all_to_all(parts, 'filt', 0, 0, tiled=True)]
    ppermute x1, waiting for transfers between devices: 0.01 us -> 1.04 us  [body(): lax.ppermute(slab_x, 'space', [(s - 1, s) for s in range(1, spaces)])]
    ppermute x1, starting transfers between devices: 2.37 us -> 1.46 us  [body(): lax.ppermute(slab_x, 'space', [(s - 1, s) for s in range(1, spaces)])]
    pallas_call x1 -> x2, Pallas kernels: 2.19 us -> 2.85 us  [the longest x1 1.44 us: body(): pl.pallas_call(upper_kernel, out_shape=[jax.ShapeDtypeStruct((64, 3 * LAN...]
    all_to_all x1, starting transfers between devices: 5.71 us -> 6.33 us  [body(): gathered = lax.all_to_all(packed, 'filt', 0, 0, tiled=True)]
  transfers between devices with their start and end apart: 3 -> 3, of which waited for: 1 -> 1; matrix products, arithmetic and copies ran while one was open for 0% -> 0% of each run, Pallas kernels for 2% -> 5%
where the time goes in v6:
time: 47.6 us; the launch traced here: 47.3 us
  blocking collectives  27.2 us (57%)
  starting transfers between devices  11.7 us (25%)
  Pallas kernels  6.53 us (14%)
  waiting for transfers between devices  1.05 us (2%)
  between operations  0.73 us (2%)
    all_to_all x1, blocking collectives, body(): sums = lax.all_to_all(sums, 'space', 0, 0, tiled=True)  15.4 us
    all_to_all x1, blocking collectives, body(): parts = lax.all_to_all(parts, 'filt', 0, 0, tiled=True)  11.8 us
    all_to_all x1, starting transfers between devices, body(): gathered = lax.all_to_all(packed, 'filt', 0, 0, tiled=True)  6.33 us
    ppermute x1, starting transfers between devices, body(): border = lax.ppermute(border, 'filt', [(f - 1, f) for f in range(1, filts)])  3.89 us
    pallas_call x1, Pallas kernels, body(): pl.pallas_call(regroup_kernel, out_shape=[jax.ShapeDtypeStruct((planes, 1...  1.9 us
    ppermute x1, starting transfers between devices, body(): lax.ppermute(slab_x, 'space', [(s - 1, s) for s in range(1, spaces)])  1.46 us
    pallas_call x1, Pallas kernels, body(): pl.pallas_call(upper_kernel, out_shape=[jax.ShapeDtypeStruct((64, 3 * LAN...  1.44 us
    pallas_call x1, Pallas kernels, body(): pl.pallas_call(lower_kernel, out_shape=jax.ShapeDtypeStruct((filts, 13, 1...  1.4 us
  transfers between devices with their start and end apart: 3, of which 1 were waited for; matrix products, arithmetic and copies ran while one was open for 0% of the time, Pallas kernels for 5%

profile of v6, /device:TPU:0, one launch (start us, length us, event | category | flops | bytes accessed | tf_op | source)
XLA Modules:
  0.0 47.3 jit_solution(6391414684495273431)
XLA Ops:
  0.6 1.9 %regroup.1 = (bf16[4,256,128]{2,1,0:T(8,128)(2,1)S(1)}, bf16[3,256,128]{2,1,0:T(8,128)(2,1)S(1)}, bf16[4,11,16,128]{3,2,1,0:T(8,128)(2,1)}) custom-call(bf16[4,4,16,512]{3,2,1,0:T(8,128)(2,1)} %volume_in.1, bf16[27,16,32]{2,1,0:T(8,128)(2,1)} %bitcast.7, bf16[16,16,128]{2,1,0:T(8,128)(2,1)} %bitcast.8), custom_call_target="tpu_custom_call" | custom-call | tf_op jit(solution)/shard_map/regroup/pallas_call | solution.py:318
  2.5 6.3 %all-to-all-start = ((bf16[4,11,16,128]{3,2,1,0:T(8,128)(2,1)}), bf16[4,11,16,128]{3,2,1,0:T(8,128)(2,1)S(1)}, u32[]{:S(2)}, u32[]{:S(2)}) async-start(bf16[4,11,16,128]{3,2,1,0:T(8,128)(2,1)} %get-tuple-element.21), calls=%async_computation | async-start | bytes 360448 | tf_op jit(solution)/shard_map/all_to_all | solution.py:338
  8.9 1.5 %collective-permute-start = (bf16[3,256,128]{2,1,0:T(8,128)(2,1)S(1)}, bf16[3,256,128]{2,1,0:T(8,128)(2,1)S(1)}, u32[]{:S(2)}, u32[]{:S(2)}) collective-permute-start(bf16[3,256,128]{2,1,0:T(8,128)(2,1)S(1)} %get-tuple-element.20), channel_id=1, source_target_pairs={{0,4},{4,8},{8,12},{12,16},{16,20},{20,24},{24,28},{1,5},{5,9},{9,... | collective-permute-start | bytes 589832 | tf_op jit(solution)/shard_map/ppermute | solution.py:337
  10.3 1.0 %collective-permute-done.slab_x = bf16[3,256,128]{2,1,0:T(8,128)(2,1)S(1)} collective-permute-done((bf16[3,256,128]{2,1,0:T(8,128)(2,1)S(1)}, bf16[3,256,128]{2,1,0:T(8,128)(2,1)S(1)}, u32[]{:S(2)}, u32[]{:S(2)}) %collective-permute-start) | collective-permute-done | bytes 196640 | tf_op jit(solution)/shard_map/ppermute | solution.py:337
  11.4 0.0 copy-start.1
  11.4 0.0 copy-start
  11.4 3.9 %collective-permute-start.1 = (bf16[7,48,128]{2,1,0:T(8,128)(2,1)S(1)}, bf16[7,48,128]{2,1,0:T(8,128)(2,1)S(1)}, u32[]{:S(2)}, u32[]{:S(2)}) collective-permute-start(bf16[7,48,128]{2,1,0:T(8,128)(2,1)S(1)} %border.1), channel_id=1, source_target_pairs={{0,1},{1,2},{2,3},{4,5},{5,6},{6,7},{8,9},{9,10},{10,11},{12,13},{... | collective-permute-start | bytes 258056 | tf_op jit(solution)/shard_map/ppermute | solution.py:347
  15.3 0.0 copy-done.1
  15.3 0.1 copy.10
  15.4 0.0 copy-done
  15.4 0.8 %stem_inner.1 = (bf16[96,144]{1,0:T(8,128)(2,1)S(1)}, bf16[7,48,896]{2,1,0:T(8,128)(2,1)S(1)}, f32[3,64,896]{2,1,0:T(8,128)S(1)}, bf16[3,96,896]{2,1,0:T(8,128)(2,1)S(1)}) custom-call(bf16[4,256,128]{2,1,0:T(8,128)(2,1)S(1)} %get-tuple-element.19.own, bf16[3,256,128]{2,1,0:T(8,128)(2,1)S(1)} %collective-permute-done.slab_x, bf16[32,128]{1,0:T(8,128)(2,1)S(1)} %pad.4.stem_w, ...), custom_call_target="tpu_custom_call" | custom-call | flops 200000000 | bytes 4000000 | tf_op jit(solution)/shard_map/stem_inner/pallas_call | solution.py:351
  16.3 0.0 all-to-all-done.gathered
  16.3 1.4 %upper_cells.1 = (bf16[64,384]{1,0:T(8,128)(2,1)S(1)}, f32[64,864]{1,0:T(8,128)S(1)}, f32[96,144]{1,0:T(8,128)S(1)}, bf16[64,896]{1,0:T(8,128)(2,1)S(1)}, bf16[1...) custom-call(bf16[4,11,16,128]{3,2,1,0:T(8,128)(2,1)S(1)} %all-to-all-done.gathered, ...), custom_call_target="tpu_custom_call" | custom-call | flops 300000000 | bytes 4000000 | tf_op jit(solution)/shard_map/upper_cells/pallas_call | solution.py:365
  17.7 0.0 collective-permute-done.1.border
  17.7 1.4 %lower_cells.1 = bf16[4,13,16,128]{3,2,1,0:T(8,128)(2,1)S(1)} custom-call(bf16[4,256,128]{2,1,0:T(8,128)(2,1)S(1)} %get-tuple-element.19.own, bf16[3,256,128]{2,1,0:T(8,128)(2,1)S(1)} %collective-permute-done.slab_x, bf16[7,48,128]{2,1,0:T(8,128)(2,1)S(1)} %collective-permute-done.1.border, bf16[3,128,144]{2,1,0:T(8,128)(2,1)S(1)} %copy-done, ...), custom_call_target="tpu_custom_call" | custom-call | tf_op jit(solution)/shard_map/lower_cells/pallas_call | solution.py:385
  19.1 11.8 %all_to_all.15.parts = bf16[4,13,16,128]{3,2,1,0:T(8,128)(2,1)S(1)} all-to-all(bf16[4,13,16,128]{3,2,1,0:T(8,128)(2,1)S(1)} %lower_cells.1), channel_id=1, replica_groups=mesh['space'=8,'filt'=4] {'filt'}, dimensions={0} | all-to-all | bytes 425984 | tf_op jit(solution)/shard_map/all_to_all | solution.py:399
  31.0 15.4 %all_to_all.16.sums = bf16[8,9,16,128]{3,2,1,0:T(8,128)(2,1)S(1)} all-to-all(bf16[8,9,16,128]{3,2,1,0:T(8,128)(2,1)S(1)} %sums.1), channel_id=1, replica_groups=mesh['space'=8,'filt'=4] {'space'}, dimensions={0} | all-to-all | bytes 589824 | tf_op jit(solution)/shard_map/all_to_all | solution.py:408
  46.4 0.9 %unpack.1 = (bf16[16,16,128]{2,1,0:T(8,128)(2,1)}, f32[27,16,32]{2,1,0:T(8,128)}, f32[27,4,32]{2,1,0:T(4,128)}) custom-call(bf16[8,9,16,128]{3,2,1,0:T(8,128)(2,1)S(1)} %all_to_all.16.sums, bf16[4,13,16,128]{3,2,1,0:T(8,128)(2,1)S(1)} %all_to_all.15.parts), custom_call_target="tpu_custom_call" | custom-call | tf_op jit(solution)/shard_map/unpack/pallas_call | solution.py:409
  (4 shorter events, 0.1 us)
Async XLA Ops:
  2.5 13.7 %all-to-all-start = ((bf16[4,11,16,128]{3,2,1,0:T(8,128)(2,1)}), bf16[4,11,16,128]{3,2,1,0:T(8,128)(2,1)S(1)}, u32[]{:S(2)}, u32[]{:S(2)}) async-start(bf16[4,11,16,128]{3,2,1,0:T(8,128)(2,1)} %get-tuple-element.21), calls=%async_computation | async-start | bytes 360448 | tf_op jit(solution)/shard_map/all_to_all | solution.py:338
  8.9 2.5 %collective-permute-start = (bf16[3,256,128]{2,1,0:T(8,128)(2,1)S(1)}, bf16[3,256,128]{2,1,0:T(8,128)(2,1)S(1)}, u32[]{:S(2)}, u32[]{:S(2)}) collective-permute-start(bf16[3,256,128]{2,1,0:T(8,128)(2,1)S(1)} %get-tuple-element.20), channel_id=1, source_target_pairs={{0,4},{4,8},{8,12},{12,16},{16,20},{20,24},{24,28},{1,5},{5,9},{9,... | collective-permute-start | bytes 589832 | tf_op jit(solution)/shard_map/ppermute | solution.py:337
  11.4 3.9 %copy-start.1 = (bf16[27,4,32]{2,1,0:T(4,128)(2,1)S(1)}, bf16[27,4,32]{2,1,0:T(4,128)(2,1)}, u32[]{:S(2)}) copy-start(bf16[27,4,32]{2,1,0:T(4,128)(2,1)} %param.6) | copy-start | bytes 20740
  11.4 4.1 %copy-start = (bf16[3,128,144]{2,1,0:T(8,128)(2,1)S(1)}, bf16[3,128,144]{2,1,0:T(8,128)(2,1)}, u32[]{:S(2)}) copy-start(bf16[3,128,144]{2,1,0:T(8,128)(2,1)} %constant.5.clone.place) | copy-start | bytes 331780
  11.4 6.3 %collective-permute-start.1 = (bf16[7,48,128]{2,1,0:T(8,128)(2,1)S(1)}, bf16[7,48,128]{2,1,0:T(8,128)(2,1)S(1)}, u32[]{:S(2)}, u32[]{:S(2)}) collective-permute-start(bf16[7,48,128]{2,1,0:T(8,128)(2,1)S(1)} %border.1), channel_id=1, source_target_pairs={{0,1},{1,2},{2,3},{4,5},{5,6},{6,7},{8,9},{9,10},{10,11},{12,13},{... | collective-permute-start | bytes 258056 | tf_op jit(solution)/shard_map/ppermute | solution.py:347

commit v7 on v6

--- a/solution.py
+++ b/solution.py
@@ -379,7 +379,6 @@
             pltpu.VMEM((3, 96, 7 * LANES), BF16),
         ],
         compiler_params=limit,
-        cost_estimate=pl.CostEstimate(flops=300_000_000, bytes_accessed=4_000_000, transcendentals=100_000),
         name="upper_cells",
     )(gathered, cols, slope, taps)
     parts = pl.pallas_call(
@@ -393,6 +392,7 @@
             pltpu.VMEM((3, 96, 3 * LANES), BF16),
         ],
         compiler_params=limit,
+        cost_estimate=pl.CostEstimate(flops=600_000_000, bytes_accessed=8_000_000, transcendentals=500_000),
         name="lower_cells",
     )(own, slab_x, border, place, gathered, weights, cols, slope, taps, *upper)
 

time: 47.6 us -> 44.3 us (0.931)
  blocking collectives: 27.2 us -> 22.3 us
  waiting for transfers between devices: 1.05 us -> 2.11 us
    all_to_all x1, blocking collectives: 15.4 us -> 10 us  [body(): sums = lax.all_to_all(sums, 'space', 0, 0, tiled=True)]
    all_to_all x1, waiting for transfers between devices: 0.01 us -> 2.11 us  [body(): gathered = lax.all_to_all(packed, 'filt', 0, 0, tiled=True)]
    ppermute x1, waiting for transfers between devices: 1.04 us -> 0.01 us  [body(): lax.ppermute(slab_x, 'space', [(s - 1, s) for s in range(1, spaces)])]
    ppermute x1, starting transfers between devices: 1.46 us -> 2.37 us  [body(): lax.ppermute(slab_x, 'space', [(s - 1, s) for s in range(1, spaces)])]
    all_to_all x1, starting transfers between devices: 6.33 us -> 5.71 us  [body(): gathered = lax.all_to_all(packed, 'filt', 0, 0, tiled=True)]
    all_to_all x1, blocking collectives: 11.8 us -> 12.3 us  [body(): parts = lax.all_to_all(parts, 'filt', 0, 0, tiled=True)]
where the time goes in v7:
time: 44.3 us; the launch traced here: 43.9 us
  blocking collectives  22.3 us (50%)
  starting transfers between devices  12.1 us (27%)
  Pallas kernels  6.52 us (15%)
  waiting for transfers between devices  2.11 us (5%)
  between operations  0.73 us (2%)
    all_to_all x1, blocking collectives, body(): parts = lax.all_to_all(parts, 'filt', 0, 0, tiled=True)  12.3 us
    all_to_all x1, blocking collectives, body(): sums = lax.all_to_all(sums, 'space', 0, 0, tiled=True)  10 us
    all_to_all x1, starting transfers between devices, body(): gathered = lax.all_to_all(packed, 'filt', 0, 0, tiled=True)  5.71 us
    ppermute x1, starting transfers between devices, body(): border = lax.ppermute(border, 'filt', [(f - 1, f) for f in range(1, filts)])  4.06 us
    ppermute x1, starting transfers between devices, body(): lax.ppermute(slab_x, 'space', [(s - 1, s) for s in range(1, spaces)])  2.37 us
    all_to_all x1, waiting for transfers between devices, body(): gathered = lax.all_to_all(packed, 'filt', 0, 0, tiled=True)  2.11 us
    pallas_call x1, Pallas kernels, body(): pl.pallas_call(regroup_kernel, out_shape=[jax.ShapeDtypeStruct((planes, 1...  1.9 us
    pallas_call x1, Pallas kernels, body(): pl.pallas_call(upper_kernel, out_shape=[jax.ShapeDtypeStruct((64, 3 * LAN...  1.44 us
  transfers between devices with their start and end apart: 3, of which 1 were waited for; matrix products, arithmetic and copies ran while one was open for 0% of the time, Pallas kernels for 5%

profile of v7, /device:TPU:0, one launch (start us, length us, event | category | flops | bytes accessed | tf_op | source)
XLA Modules:
  0.0 43.9 jit_solution(14053652923721467762)
XLA Ops:
  0.6 1.9 %regroup.1 = (bf16[4,256,128]{2,1,0:T(8,128)(2,1)S(1)}, bf16[3,256,128]{2,1,0:T(8,128)(2,1)S(1)}, bf16[4,11,16,128]{3,2,1,0:T(8,128)(2,1)}) custom-call(bf16[4,4,16,512]{3,2,1,0:T(8,128)(2,1)} %volume_in.1, bf16[27,16,32]{2,1,0:T(8,128)(2,1)} %bitcast.7, bf16[16,16,128]{2,1,0:T(8,128)(2,1)} %bitcast.8), custom_call_target="tpu_custom_call" | custom-call | tf_op jit(solution)/shard_map/regroup/pallas_call | solution.py:318
  2.5 2.4 %collective-permute-start = (bf16[3,256,128]{2,1,0:T(8,128)(2,1)S(1)}, bf16[3,256,128]{2,1,0:T(8,128)(2,1)S(1)}, u32[]{:S(2)}, u32[]{:S(2)}) collective-permute-start(bf16[3,256,128]{2,1,0:T(8,128)(2,1)S(1)} %get-tuple-element.20), channel_id=1, source_target_pairs={{0,4},{4,8},{8,12},{12,16},{16,20},{20,24},{24,28},{1,5},{5,9},{9,... | collective-permute-start | bytes 589832 | tf_op jit(solution)/shard_map/ppermute | solution.py:337
  4.9 5.7 %all-to-all-start = ((bf16[4,11,16,128]{3,2,1,0:T(8,128)(2,1)}), bf16[4,11,16,128]{3,2,1,0:T(8,128)(2,1)S(1)}, u32[]{:S(2)}, u32[]{:S(2)}) async-start(bf16[4,11,16,128]{3,2,1,0:T(8,128)(2,1)} %get-tuple-element.21), calls=%async_computation | async-start | bytes 360448 | tf_op jit(solution)/shard_map/all_to_all | solution.py:338
  10.6 0.0 collective-permute-done.slab_x
  10.6 0.0 copy-start.1
  10.6 0.0 copy-start
  10.7 4.1 %collective-permute-start.1 = (bf16[7,48,128]{2,1,0:T(8,128)(2,1)S(1)}, bf16[7,48,128]{2,1,0:T(8,128)(2,1)S(1)}, u32[]{:S(2)}, u32[]{:S(2)}) collective-permute-start(bf16[7,48,128]{2,1,0:T(8,128)(2,1)S(1)} %border.1), channel_id=1, source_target_pairs={{0,1},{1,2},{2,3},{4,5},{5,6},{6,7},{8,9},{9,10},{10,11},{12,13},{... | collective-permute-start | bytes 258056 | tf_op jit(solution)/shard_map/ppermute | solution.py:347
  14.7 0.0 copy-done.1
  14.8 0.1 copy.10
  14.9 0.0 copy-done
  14.9 0.8 %stem_inner.1 = (bf16[96,144]{1,0:T(8,128)(2,1)S(1)}, bf16[7,48,896]{2,1,0:T(8,128)(2,1)S(1)}, f32[3,64,896]{2,1,0:T(8,128)S(1)}, bf16[3,96,896]{2,1,0:T(8,128)(2,1)S(1)}) custom-call(bf16[4,256,128]{2,1,0:T(8,128)(2,1)S(1)} %get-tuple-element.19.own, bf16[3,256,128]{2,1,0:T(8,128)(2,1)S(1)} %collective-permute-done.slab_x, bf16[32,128]{1,0:T(8,128)(2,1)S(1)} %pad.4.stem_w, ...), custom_call_target="tpu_custom_call" | custom-call | flops 200000000 | bytes 4000000 | tf_op jit(solution)/shard_map/stem_inner/pallas_call | solution.py:351
  15.7 2.1 %all-to-all-done.gathered = bf16[4,11,16,128]{3,2,1,0:T(8,128)(2,1)S(1)} async-done(((bf16[4,11,16,128]{3,2,1,0:T(8,128)(2,1)}), bf16[4,11,16,128]{3,2,1,0:T(8,128)(2,1)S(1)}, u32[]{:S(2)}, u32[]{:S(2)}) %all-to-all-start) | async-done | bytes 180256 | tf_op jit(solution)/shard_map/all_to_all | solution.py:338
  17.8 1.4 %upper_cells.1 = (bf16[64,384]{1,0:T(8,128)(2,1)S(1)}, f32[64,864]{1,0:T(8,128)S(1)}, f32[96,144]{1,0:T(8,128)S(1)}, bf16[64,896]{1,0:T(8,128)(2,1)S(1)}, bf16[1...) custom-call(bf16[4,11,16,128]{3,2,1,0:T(8,128)(2,1)S(1)} %all-to-all-done.gathered, ...), custom_call_target="tpu_custom_call" | custom-call | tf_op jit(solution)/shard_map/upper_cells/pallas_call | solution.py:365
  19.3 0.0 collective-permute-done.1.border
  19.3 1.4 %lower_cells.1 = bf16[4,13,16,128]{3,2,1,0:T(8,128)(2,1)S(1)} custom-call(bf16[4,256,128]{2,1,0:T(8,128)(2,1)S(1)} %get-tuple-element.19.own, bf16[3,256,128]{2,1,0:T(8,128)(2,1)S(1)} %collective-permute-done.slab_x, bf16[7,48,128]{2,1,0:T(8,128)(2,1)S(1)} %collective-permute-done.1.border, bf16[3,128,144]{2,1,0:T(8,128)(2,1)S(1)} %copy-done, ...), custom_call_target="tpu_custom_call" | custom-call | flops 600000000 | bytes 8000000 | tf_op jit(solution)/shard_map/lower_cells/pallas_call | solution.py:384
  20.7 12.3 %all_to_all.15.parts = bf16[4,13,16,128]{3,2,1,0:T(8,128)(2,1)S(1)} all-to-all(bf16[4,13,16,128]{3,2,1,0:T(8,128)(2,1)S(1)} %lower_cells.1), channel_id=1, replica_groups=mesh['space'=8,'filt'=4] {'filt'}, dimensions={0} | all-to-all | bytes 425984 | tf_op jit(solution)/shard_map/all_to_all | solution.py:399
  33.0 10.0 %all_to_all.16.sums = bf16[8,9,16,128]{3,2,1,0:T(8,128)(2,1)S(1)} all-to-all(bf16[8,9,16,128]{3,2,1,0:T(8,128)(2,1)S(1)} %sums.1), channel_id=1, replica_groups=mesh['space'=8,'filt'=4] {'space'}, dimensions={0} | all-to-all | bytes 589824 | tf_op jit(solution)/shard_map/all_to_all | solution.py:408
  43.0 0.9 %unpack.1 = (bf16[16,16,128]{2,1,0:T(8,128)(2,1)}, f32[27,16,32]{2,1,0:T(8,128)}, f32[27,4,32]{2,1,0:T(4,128)}) custom-call(bf16[8,9,16,128]{3,2,1,0:T(8,128)(2,1)S(1)} %all_to_all.16.sums, bf16[4,13,16,128]{3,2,1,0:T(8,128)(2,1)S(1)} %all_to_all.15.parts), custom_call_target="tpu_custom_call" | custom-call | tf_op jit(solution)/shard_map/unpack/pallas_call | solution.py:409
  (4 shorter events, 0.1 us)
Async XLA Ops:
  2.5 8.1 %collective-permute-start = (bf16[3,256,128]{2,1,0:T(8,128)(2,1)S(1)}, bf16[3,256,128]{2,1,0:T(8,128)(2,1)S(1)}, u32[]{:S(2)}, u32[]{:S(2)}) collective-permute-start(bf16[3,256,128]{2,1,0:T(8,128)(2,1)S(1)} %get-tuple-element.20), channel_id=1, source_target_pairs={{0,4},{4,8},{8,12},{12,16},{16,20},{20,24},{24,28},{1,5},{5,9},{9,... | collective-permute-start | bytes 589832 | tf_op jit(solution)/shard_map/ppermute | solution.py:337
  4.9 12.9 %all-to-all-start = ((bf16[4,11,16,128]{3,2,1,0:T(8,128)(2,1)}), bf16[4,11,16,128]{3,2,1,0:T(8,128)(2,1)S(1)}, u32[]{:S(2)}, u32[]{:S(2)}) async-start(bf16[4,11,16,128]{3,2,1,0:T(8,128)(2,1)} %get-tuple-element.21), calls=%async_computation | async-start | bytes 360448 | tf_op jit(solution)/shard_map/all_to_all | solution.py:338
  10.6 4.1 %copy-start.1 = (bf16[27,4,32]{2,1,0:T(4,128)(2,1)S(1)}, bf16[27,4,32]{2,1,0:T(4,128)(2,1)}, u32[]{:S(2)}) copy-start(bf16[27,4,32]{2,1,0:T(4,128)(2,1)} %param.6) | copy-start | bytes 20740
  10.6 4.2 %copy-start = (bf16[3,128,144]{2,1,0:T(8,128)(2,1)S(1)}, bf16[3,128,144]{2,1,0:T(8,128)(2,1)}, u32[]{:S(2)}) copy-start(bf16[3,128,144]{2,1,0:T(8,128)(2,1)} %constant.5.clone.place) | copy-start | bytes 331780
  10.7 8.6 %collective-permute-start.1 = (bf16[7,48,128]{2,1,0:T(8,128)(2,1)S(1)}, bf16[7,48,128]{2,1,0:T(8,128)(2,1)S(1)}, u32[]{:S(2)}, u32[]{:S(2)}) collective-permute-start(bf16[7,48,128]{2,1,0:T(8,128)(2,1)S(1)} %border.1), channel_id=1, source_target_pairs={{0,1},{1,2},{2,3},{4,5},{5,6},{6,7},{8,9},{9,10},{10,11},{12,13},{... | collective-permute-start | bytes 258056 | tf_op jit(solution)/shard_map/ppermute | solution.py:347

commit v8 on v7

--- a/solution.py
+++ b/solution.py
@@ -273,9 +273,7 @@
 
 
 def sum_kernel(parts, sums):
-    total = jnp.sum(parts[:, 0:9].astype(F32), axis=0).astype(BF16)
-    for s in range(sums.shape[0]):
-        sums[s] = total
+    sums[...] = jnp.sum(parts[:, 0:9].astype(F32), axis=0).astype(BF16)
 
 
 def unpack_kernel(
@@ -399,13 +397,13 @@
     parts = lax.all_to_all(parts, "filt", 0, 0, tiled=True)
     sums = pl.pallas_call(
         sum_kernel,
-        out_shape=jax.ShapeDtypeStruct((spaces, 9, 16, LANES), BF16),
+        out_shape=jax.ShapeDtypeStruct((9, 16, LANES), BF16),
         in_specs=whole(1),
         out_specs=whole(1)[0],
         compiler_params=limit,
         name="sums",
     )(parts)
-    sums = lax.all_to_all(sums, "space", 0, 0, tiled=True)
+    sums = lax.all_gather(sums, "space")
     features, middle, stem = pl.pallas_call(
         functools.partial(unpack_kernel, middle_cells**-0.5, stem_cells**-0.5),
         out_shape=[

time: 44.3 us -> 43.8 us (0.989)
    all_to_all x1 -> x0, blocking collectives: 10 us -> none  [body(): sums = lax.all_to_all(sums, 'space', 0, 0, tiled=True)]
    all_gather x0 -> x1, blocking collectives: none -> 9.61 us  [body(): sums = lax.all_gather(sums, 'space')]
where the time goes in v8:
time: 43.8 us; the launch traced here: 43.5 us
  blocking collectives  21.9 us (50%)
  starting transfers between devices  12.1 us (28%)
  Pallas kernels  6.52 us (15%)
  waiting for transfers between devices  2.11 us (5%)
  between operations  0.73 us (2%)
    all_to_all x1, blocking collectives, body(): parts = lax.all_to_all(parts, 'filt', 0, 0, tiled=True)  12.3 us
    all_gather x1, blocking collectives, body(): sums = lax.all_gather(sums, 'space')  9.61 us
    all_to_all x1, starting transfers between devices, body(): gathered = lax.all_to_all(packed, 'filt', 0, 0, tiled=True)  5.71 us
    ppermute x1, starting transfers between devices, body(): border = lax.ppermute(border, 'filt', [(f - 1, f) for f in range(1, filts)])  4.06 us
    ppermute x1, starting transfers between devices, body(): lax.ppermute(slab_x, 'space', [(s - 1, s) for s in range(1, spaces)])  2.37 us
    all_to_all x1, waiting for transfers between devices, body(): gathered = lax.all_to_all(packed, 'filt', 0, 0, tiled=True)  2.11 us
    pallas_call x1, Pallas kernels, body(): pl.pallas_call(regroup_kernel, out_shape=[jax.ShapeDtypeStruct((planes, 1...  1.9 us
    pallas_call x1, Pallas kernels, body(): pl.pallas_call(upper_kernel, out_shape=[jax.ShapeDtypeStruct((64, 3 * LAN...  1.44 us
  transfers between devices with their start and end apart: 3, of which 1 were waited for; matrix products, arithmetic and copies ran while one was open for 0% of the time, Pallas kernels for 5%

profile of v8, /device:TPU:0, one launch (start us, length us, event | category | flops | bytes accessed | tf_op | source)
XLA Modules:
  0.0 43.5 jit_solution(5819689195923256603)
XLA Ops:
  0.6 1.9 %regroup.1 = (bf16[4,256,128]{2,1,0:T(8,128)(2,1)S(1)}, bf16[3,256,128]{2,1,0:T(8,128)(2,1)S(1)}, bf16[4,11,16,128]{3,2,1,0:T(8,128)(2,1)}) custom-call(bf16[4,4,16,512]{3,2,1,0:T(8,128)(2,1)} %volume_in.1, bf16[27,16,32]{2,1,0:T(8,128)(2,1)} %bitcast.9, bf16[16,16,128]{2,1,0:T(8,128)(2,1)} %bitcast.10), custom_call_target="tpu_custom_call" | custom-call | tf_op jit(solution)/shard_map/regroup/pallas_call | solution.py:316
  2.5 2.4 %collective-permute-start = (bf16[3,256,128]{2,1,0:T(8,128)(2,1)S(1)}, bf16[3,256,128]{2,1,0:T(8,128)(2,1)S(1)}, u32[]{:S(2)}, u32[]{:S(2)}) collective-permute-start(bf16[3,256,128]{2,1,0:T(8,128)(2,1)S(1)} %get-tuple-element.20), channel_id=1, source_target_pairs={{0,4},{4,8},{8,12},{12,16},{16,20},{20,24},{24,28},{1,5},{5,9},{9,... | collective-permute-start | bytes 589832 | tf_op jit(solution)/shard_map/ppermute | solution.py:335
  4.9 5.7 %all-to-all-start = ((bf16[4,11,16,128]{3,2,1,0:T(8,128)(2,1)}), bf16[4,11,16,128]{3,2,1,0:T(8,128)(2,1)S(1)}, u32[]{:S(2)}, u32[]{:S(2)}) async-start(bf16[4,11,16,128]{3,2,1,0:T(8,128)(2,1)} %get-tuple-element.21), calls=%async_computation | async-start | bytes 360448 | tf_op jit(solution)/shard_map/all_to_all | solution.py:336
  10.6 0.0 collective-permute-done.slab_x
  10.6 0.0 copy-start.1
  10.6 0.0 copy-start
  10.7 4.1 %collective-permute-start.1 = (bf16[7,48,128]{2,1,0:T(8,128)(2,1)S(1)}, bf16[7,48,128]{2,1,0:T(8,128)(2,1)S(1)}, u32[]{:S(2)}, u32[]{:S(2)}) collective-permute-start(bf16[7,48,128]{2,1,0:T(8,128)(2,1)S(1)} %border.1), channel_id=1, source_target_pairs={{0,1},{1,2},{2,3},{4,5},{5,6},{6,7},{8,9},{9,10},{10,11},{12,13},{... | collective-permute-start | bytes 258056 | tf_op jit(solution)/shard_map/ppermute | solution.py:345
  14.7 0.0 copy-done.1
  14.8 0.1 copy.12
  14.9 0.0 copy-done
  14.9 0.8 %stem_inner.1 = (bf16[96,144]{1,0:T(8,128)(2,1)S(1)}, bf16[7,48,896]{2,1,0:T(8,128)(2,1)S(1)}, f32[3,64,896]{2,1,0:T(8,128)S(1)}, bf16[3,96,896]{2,1,0:T(8,128)(2,1)S(1)}) custom-call(bf16[4,256,128]{2,1,0:T(8,128)(2,1)S(1)} %get-tuple-element.19.own, bf16[3,256,128]{2,1,0:T(8,128)(2,1)S(1)} %collective-permute-done.slab_x, bf16[32,128]{1,0:T(8,128)(2,1)S(1)} %pad.4.stem_w, ...), custom_call_target="tpu_custom_call" | custom-call | flops 200000000 | bytes 4000000 | tf_op jit(solution)/shard_map/stem_inner/pallas_call | solution.py:349
  15.7 2.1 %all-to-all-done.gathered = bf16[4,11,16,128]{3,2,1,0:T(8,128)(2,1)S(1)} async-done(((bf16[4,11,16,128]{3,2,1,0:T(8,128)(2,1)}), bf16[4,11,16,128]{3,2,1,0:T(8,128)(2,1)S(1)}, u32[]{:S(2)}, u32[]{:S(2)}) %all-to-all-start) | async-done | bytes 180256 | tf_op jit(solution)/shard_map/all_to_all | solution.py:336
  17.8 1.4 %upper_cells.1 = (bf16[64,384]{1,0:T(8,128)(2,1)S(1)}, f32[64,864]{1,0:T(8,128)S(1)}, f32[96,144]{1,0:T(8,128)S(1)}, bf16[64,896]{1,0:T(8,128)(2,1)S(1)}, bf16[1...) custom-call(bf16[4,11,16,128]{3,2,1,0:T(8,128)(2,1)S(1)} %all-to-all-done.gathered, ...), custom_call_target="tpu_custom_call" | custom-call | tf_op jit(solution)/shard_map/upper_cells/pallas_call | solution.py:363
  19.3 0.0 collective-permute-done.1.border
  19.3 1.4 %lower_cells.1 = bf16[4,13,16,128]{3,2,1,0:T(8,128)(2,1)S(1)} custom-call(bf16[4,256,128]{2,1,0:T(8,128)(2,1)S(1)} %get-tuple-element.19.own, bf16[3,256,128]{2,1,0:T(8,128)(2,1)S(1)} %collective-permute-done.slab_x, bf16[7,48,128]{2,1,0:T(8,128)(2,1)S(1)} %collective-permute-done.1.border, bf16[3,128,144]{2,1,0:T(8,128)(2,1)S(1)} %copy-done, ...), custom_call_target="tpu_custom_call" | custom-call | flops 600000000 | bytes 8000000 | tf_op jit(solution)/shard_map/lower_cells/pallas_call | solution.py:382
  20.7 12.3 %all_to_all.10.parts = bf16[4,13,16,128]{3,2,1,0:T(8,128)(2,1)S(1)} all-to-all(bf16[4,13,16,128]{3,2,1,0:T(8,128)(2,1)S(1)} %lower_cells.1), channel_id=1, replica_groups=mesh['space'=8,'filt'=4] {'filt'}, dimensions={0} | all-to-all | bytes 425984 | tf_op jit(solution)/shard_map/all_to_all | solution.py:397
  33.0 9.6 %all-gather = bf16[72,16,128]{2,1,0:T(8,128)(2,1)S(1)} all-gather(bf16[9,16,128]{2,1,0:T(8,128)(2,1)S(1)} %sums.1), channel_id=2, replica_groups=mesh['space'=8,'filt'=4] {'space'}, dimensions={0}, use_global_device_ids=true | all-gather | bytes 331776 | tf_op jit(solution)/shard_map/all_gather | solution.py:406
  42.6 0.9 %unpack.1 = (bf16[16,16,128]{2,1,0:T(8,128)(2,1)}, f32[27,16,32]{2,1,0:T(8,128)}, f32[27,4,32]{2,1,0:T(4,128)}) custom-call(bf16[8,9,16,128]{3,2,1,0:T(8,128)(2,1)S(1)} %bitcast.8, bf16[4,13,16,128]{3,2,1,0:T(8,128)(2,1)S(1)} %all_to_all.10.parts), custom_call_target="tpu_custom_call" | custom-call | tf_op jit(solution)/shard_map/unpack/pallas_call | solution.py:407
  (4 shorter events, 0.1 us)
Async XLA Ops:
  2.5 8.1 %collective-permute-start = (bf16[3,256,128]{2,1,0:T(8,128)(2,1)S(1)}, bf16[3,256,128]{2,1,0:T(8,128)(2,1)S(1)}, u32[]{:S(2)}, u32[]{:S(2)}) collective-permute-start(bf16[3,256,128]{2,1,0:T(8,128)(2,1)S(1)} %get-tuple-element.20), channel_id=1, source_target_pairs={{0,4},{4,8},{8,12},{12,16},{16,20},{20,24},{24,28},{1,5},{5,9},{9,... | collective-permute-start | bytes 589832 | tf_op jit(solution)/shard_map/ppermute | solution.py:335
  4.9 12.9 %all-to-all-start = ((bf16[4,11,16,128]{3,2,1,0:T(8,128)(2,1)}), bf16[4,11,16,128]{3,2,1,0:T(8,128)(2,1)S(1)}, u32[]{:S(2)}, u32[]{:S(2)}) async-start(bf16[4,11,16,128]{3,2,1,0:T(8,128)(2,1)} %get-tuple-element.21), calls=%async_computation | async-start | bytes 360448 | tf_op jit(solution)/shard_map/all_to_all | solution.py:336
  10.6 4.1 %copy-start.1 = (bf16[27,4,32]{2,1,0:T(4,128)(2,1)S(1)}, bf16[27,4,32]{2,1,0:T(4,128)(2,1)}, u32[]{:S(2)}) copy-start(bf16[27,4,32]{2,1,0:T(4,128)(2,1)} %param.6) | copy-start | bytes 20740
  10.6 4.2 %copy-start = (bf16[3,128,144]{2,1,0:T(8,128)(2,1)S(1)}, bf16[3,128,144]{2,1,0:T(8,128)(2,1)}, u32[]{:S(2)}) copy-start(bf16[3,128,144]{2,1,0:T(8,128)(2,1)} %constant.5.clone.place) | copy-start | bytes 331780
  10.7 8.6 %collective-permute-start.1 = (bf16[7,48,128]{2,1,0:T(8,128)(2,1)S(1)}, bf16[7,48,128]{2,1,0:T(8,128)(2,1)S(1)}, u32[]{:S(2)}, u32[]{:S(2)}) collective-permute-start(bf16[7,48,128]{2,1,0:T(8,128)(2,1)S(1)} %border.1), channel_id=1, source_target_pairs={{0,1},{1,2},{2,3},{4,5},{5,6},{6,7},{8,9},{9,10},{10,11},{12,13},{... | collective-permute-start | bytes 258056 | tf_op jit(solution)/shard_map/ppermute | solution.py:345

commit v9 on v8

--- a/solution.py
+++ b/solution.py
@@ -67,10 +67,10 @@
             packed[f, t] = tile
     copies[1].wait()
     turned = nn(turn, cotangent[...].reshape(256, LANES)).astype(BF16)
-    for f in range(packed.shape[0]):
+    for k, f in enumerate(exchange_order(packed.shape[0])):
         for j in range(4):
             row = 16 * (4 * f + j)
-            packed[f, 7 + j] = turned[row : row + 16]
+            packed[k, 7 + j] = turned[row : row + 16]
     copies[2].start()
 
     for copy in copies[3:]:
@@ -171,14 +171,16 @@
     gathered, cols, slope, taps, features, mid_grad, stem_grad, mid_w, odd_w, even_w, mid_cols, stem_back,
 ):
     blocks = gathered.shape[0]
-    for f in range(blocks):
+    order = exchange_order(blocks)
+    for k, f in enumerate(order):
         for t in range(7):
-            mid_w[16 * f : 16 * f + 16, t * LANES : (t + 1) * LANES] = gathered[f, t]
+            mid_w[16 * f : 16 * f + 16, t * LANES : (t + 1) * LANES] = gathered[k, t]
     for i in range(3):
         for j in range(2, 9):
             fill_taps(mid_cols, taps[i, :, pl.ds((j - 2) * LANES, LANES)], i, j, 1, 3)
     cotangent = jnp.concatenate(
-        [jnp.concatenate([gathered[f, 7 + j] for j in range(1, 4)], axis=1) for f in range(blocks)], axis=0
+        [jnp.concatenate([gathered[order.index(f), 7 + j] for j in range(1, 4)], axis=1) for f in range(blocks)],
+        axis=0,
     )
     features[...], mid_grad[...], both = middle_cells_step(mid_w, mid_cols, cotangent)
 
@@ -237,7 +239,8 @@
         for j in range(2):
             fill_taps(mid_cols, low_taps[:, j * LANES : (j + 1) * LANES], i, j, 0, 1)
         fill_taps(mid_cols, taps[i, :, 0:LANES], i, 2, 0, 1)
-    cotangent = jnp.concatenate([gathered[f, 7] for f in range(blocks)], axis=0)
+    order = exchange_order(blocks)
+    cotangent = jnp.concatenate([gathered[order.index(f), 7] for f in range(blocks)], axis=0)
     features, mid_grad, both = middle_cells_step(mid_w, mid_cols, cotangent)
 
     back = [nn(even_w[:, 0:LANES], both), nn(odd_w[...], both), nn(even_w[:, LANES:], both)]
@@ -261,15 +264,15 @@
 
     middle = (mid_grad + upper_mid[...]).astype(BF16)
     middle = jnp.concatenate([middle, jnp.zeros((blocks * 16, 32), BF16)], axis=1)
-    for f in range(blocks):
+    for k, f in enumerate(order):
         rows = slice(16 * f, 16 * f + 16)
         for t in range(7):
-            parts[f, t] = middle[rows, t * LANES : (t + 1) * LANES]
+            parts[k, t] = middle[rows, t * LANES : (t + 1) * LANES]
         for half in range(2):
-            parts[f, 7 + half] = stem[16 * half : 16 * half + 16]
-        parts[f, 9] = features[rows]
+            parts[k, 7 + half] = stem[16 * half : 16 * half + 16]
+        parts[k, 9] = features[rows]
         for j in range(3):
-            parts[f, 10 + j] = upper_features[rows, j * LANES : (j + 1) * LANES]
+            parts[k, 10 + j] = upper_features[rows, j * LANES : (j + 1) * LANES]
 
 
 def sum_kernel(parts, sums):
@@ -290,7 +293,8 @@
         start = 32 * (t % 4)
         middle[t] = total[t // 4, :, start : start + 32] * middle_scale
     copies[0].start()
-    rows = [parts[f, 9 + j] for f in range(parts.shape[0]) for j in range(4)]
+    order = exchange_order(parts.shape[0])
+    rows = [parts[order.index(f), 9 + j] for f in range(parts.shape[0]) for j in range(4)]
     features[...] = nn(turn_matrix(), jnp.concatenate(rows, axis=0)).astype(BF16).reshape(16, 16, LANES)
     copies[2].start()
     turned = jnp.concatenate([total[7], total[8]], axis=0).T * stem_scale
@@ -301,6 +305,15 @@
         copy.wait()
 
 
+def exchange_order(filts):
+    return sorted(range(filts), key=lambda f: (abs(f - filts // 2), f))
+
+
+def exchange(chunks):
+    groups = [exchange_order(lax.axis_size("filt"))]
+    return lax.all_to_all(chunks, "filt", 0, 0, axis_index_groups=groups, tiled=True)
+
+
 def whole(count):
     return [pl.BlockSpec(memory_space=pltpu.VMEM)] * count
 
@@ -333,7 +346,7 @@
         name="regroup",
     )(*[pltpu.with_memory_space_constraint(x, pltpu.HBM) for x in raw])
     slab_x = lax.ppermute(slab_x, "space", [(s - 1, s) for s in range(1, spaces)])
-    gathered = lax.all_to_all(packed, "filt", 0, 0, tiled=True)
+    gathered = exchange(packed)
     border = pl.pallas_call(
         border_kernel,
         out_shape=jax.ShapeDtypeStruct((7, 48, LANES), BF16),
@@ -394,7 +407,7 @@
         name="lower_cells",
     )(own, slab_x, border, place, gathered, weights, cols, slope, taps, *upper)
 
-    parts = lax.all_to_all(parts, "filt", 0, 0, tiled=True)
+    parts = exchange(parts)
     sums = pl.pallas_call(
         sum_kernel,
         out_shape=jax.ShapeDtypeStruct((9, 16, LANES), BF16),

time: 43.8 us -> 41.4 us (0.945)
  waiting for transfers between devices: 2.11 us -> 0.58 us
  blocking collectives: 21.9 us -> 21.4 us
    all_to_all x1, waiting for transfers between devices: 2.11 us -> 0.26 us  [exchange(): lax.all_to_all(chunks, 'filt', 0, 0, axis_index_groups=groups, tiled=True)]
    ppermute x1, starting transfers between devices: 4.06 us -> 2.6 us  [body(): border = lax.ppermute(border, 'filt', [(f - 1, f) for f in range(1, filts)])]
    all_to_all x1, blocking collectives: 12.3 us -> 11 us  [exchange(): lax.all_to_all(chunks, 'filt', 0, 0, axis_index_groups=groups, tiled=True)]
    all_to_all x1, starting transfers between devices: 5.71 us -> 6.76 us  [exchange(): lax.all_to_all(chunks, 'filt', 0, 0, axis_index_groups=groups, tiled=True)]
    all_gather x1, blocking collectives: 9.61 us -> 10.5 us  [body(): sums = lax.all_gather(sums, 'space')]
  transfers between devices with their start and end apart: 3 -> 3, of which waited for: 1 -> 2; matrix products, arithmetic and copies ran while one was open for 0% -> 0% of each run, Pallas kernels for 5% -> 5%
where the time goes in v9:
time: 41.4 us; the launch traced here: 41.1 us
  blocking collectives  21.4 us (52%)
  starting transfers between devices  11.7 us (28%)
  Pallas kernels  6.49 us (16%)
  between operations  0.72 us (2%)
  waiting for transfers between devices  0.58 us (1%)
    all_to_all x1, blocking collectives, exchange(): lax.all_to_all(chunks, 'filt', 0, 0, axis_index_groups=groups, tiled=True)  11 us
    all_gather x1, blocking collectives, body(): sums = lax.all_gather(sums, 'space')  10.5 us
    all_to_all x1, starting transfers between devices, exchange(): lax.all_to_all(chunks, 'filt', 0, 0, axis_index_groups=groups, tiled=True)  6.76 us
    ppermute x1, starting transfers between devices, body(): border = lax.ppermute(border, 'filt', [(f - 1, f) for f in range(1, filts)])  2.6 us
    ppermute x1, starting transfers between devices, body(): lax.ppermute(slab_x, 'space', [(s - 1, s) for s in range(1, spaces)])  2.37 us
    pallas_call x1, Pallas kernels, body(): pl.pallas_call(regroup_kernel, out_shape=[jax.ShapeDtypeStruct((planes, 1...  1.9 us
    pallas_call x1, Pallas kernels, body(): pl.pallas_call(upper_kernel, out_shape=[jax.ShapeDtypeStruct((64, 3 * LAN...  1.43 us
    pallas_call x1, Pallas kernels, body(): pl.pallas_call(lower_kernel, out_shape=jax.ShapeDtypeStruct((filts, 13, 1...  1.4 us
  transfers between devices with their start and end apart: 3, of which 2 were waited for; matrix products, arithmetic and copies ran while one was open for 0% of the time, Pallas kernels for 5%

profile of v9, /device:TPU:0, one launch (start us, length us, event | category | flops | bytes accessed | tf_op | source)
XLA Modules:
  0.0 41.1 jit_solution(10312539380745155971)
XLA Ops:
  0.6 1.9 %regroup.1 = (bf16[4,256,128]{2,1,0:T(8,128)(2,1)S(1)}, bf16[3,256,128]{2,1,0:T(8,128)(2,1)S(1)}, bf16[4,11,16,128]{3,2,1,0:T(8,128)(2,1)}) custom-call(bf16[4,4,16,512]{3,2,1,0:T(8,128)(2,1)} %volume_in.1, bf16[27,16,32]{2,1,0:T(8,128)(2,1)} %bitcast.9, bf16[16,16,128]{2,1,0:T(8,128)(2,1)} %bitcast.10), custom_call_target="tpu_custom_call" | custom-call | tf_op jit(solution)/shard_map/regroup/pallas_call | solution.py:329
  2.5 2.4 %collective-permute-start = (bf16[3,256,128]{2,1,0:T(8,128)(2,1)S(1)}, bf16[3,256,128]{2,1,0:T(8,128)(2,1)S(1)}, u32[]{:S(2)}, u32[]{:S(2)}) collective-permute-start(bf16[3,256,128]{2,1,0:T(8,128)(2,1)S(1)} %get-tuple-element.20), channel_id=1, source_target_pairs={{0,4},{4,8},{8,12},{12,16},{16,20},{20,24},{24,28},{1,5},{5,9},{9,... | collective-permute-start | bytes 589832 | tf_op jit(solution)/shard_map/ppermute | solution.py:348
  4.9 6.8 %all-to-all-start = ((bf16[4,11,16,128]{3,2,1,0:T(8,128)(2,1)}), bf16[4,11,16,128]{3,2,1,0:T(8,128)(2,1)S(1)}, u32[]{:S(2)}, u32[]{:S(2)}) async-start(bf16[4,11,16,128]{3,2,1,0:T(8,128)(2,1)} %get-tuple-element.21), calls=%async_computation | async-start | bytes 360448 | tf_op jit(solution)/shard_map/all_to_all | solution.py:314
  11.7 0.0 collective-permute-done.slab_x
  11.7 0.0 copy-start.1
  11.7 0.0 copy-start
  11.7 2.6 %collective-permute-start.1 = (bf16[7,48,128]{2,1,0:T(8,128)(2,1)S(1)}, bf16[7,48,128]{2,1,0:T(8,128)(2,1)S(1)}, u32[]{:S(2)}, u32[]{:S(2)}) collective-permute-start(bf16[7,48,128]{2,1,0:T(8,128)(2,1)S(1)} %border.1), channel_id=1, source_target_pairs={{0,1},{1,2},{2,3},{4,5},{5,6},{6,7},{8,9},{9,10},{10,11},{12,13},{... | collective-permute-start | bytes 258056 | tf_op jit(solution)/shard_map/ppermute | solution.py:358
  14.3 0.0 copy-done.1
  14.3 0.1 copy.12
  14.4 0.0 copy-done
  14.5 0.8 %stem_inner.1 = (bf16[96,144]{1,0:T(8,128)(2,1)S(1)}, bf16[7,48,896]{2,1,0:T(8,128)(2,1)S(1)}, f32[3,64,896]{2,1,0:T(8,128)S(1)}, bf16[3,96,896]{2,1,0:T(8,128)(2,1)S(1)}) custom-call(bf16[4,256,128]{2,1,0:T(8,128)(2,1)S(1)} %get-tuple-element.19.own, bf16[3,256,128]{2,1,0:T(8,128)(2,1)S(1)} %collective-permute-done.slab_x, bf16[32,128]{1,0:T(8,128)(2,1)S(1)} %pad.4.stem_w, ...), custom_call_target="tpu_custom_call" | custom-call | flops 200000000 | bytes 4000000 | tf_op jit(solution)/shard_map/stem_inner/pallas_call | solution.py:362
  15.3 0.3 all-to-all-done.gathered
  15.5 1.4 %upper_cells.1 = (bf16[64,384]{1,0:T(8,128)(2,1)S(1)}, f32[64,864]{1,0:T(8,128)S(1)}, f32[96,144]{1,0:T(8,128)S(1)}, bf16[64,896]{1,0:T(8,128)(2,1)S(1)}, bf16[1...) custom-call(bf16[4,11,16,128]{3,2,1,0:T(8,128)(2,1)S(1)} %all-to-all-done.gathered, ...), custom_call_target="tpu_custom_call" | custom-call | tf_op jit(solution)/shard_map/upper_cells/pallas_call | solution.py:376
  17.0 0.3 collective-permute-done.1.border
  17.3 1.4 %lower_cells.1 = bf16[4,13,16,128]{3,2,1,0:T(8,128)(2,1)S(1)} custom-call(bf16[4,256,128]{2,1,0:T(8,128)(2,1)S(1)} %get-tuple-element.19.own, bf16[3,256,128]{2,1,0:T(8,128)(2,1)S(1)} %collective-permute-done.slab_x, bf16[7,48,128]{2,1,0:T(8,128)(2,1)S(1)} %collective-permute-done.1.border, bf16[3,128,144]{2,1,0:T(8,128)(2,1)S(1)} %copy-done, ...), custom_call_target="tpu_custom_call" | custom-call | flops 600000000 | bytes 8000000 | tf_op jit(solution)/shard_map/lower_cells/pallas_call | solution.py:395
  18.7 11.0 %all_to_all.10.parts = bf16[4,13,16,128]{3,2,1,0:T(8,128)(2,1)S(1)} all-to-all(bf16[4,13,16,128]{3,2,1,0:T(8,128)(2,1)S(1)} %lower_cells.1), channel_id=1, replica_groups={{2,1,3,0},{6,5,7,4},{10,9,11,8},{14,13,15,12},{18,17,19,16},{22,21,23,2..., dimensions={0} | all-to-all | bytes 425984 | tf_op jit(solution)/shard_map/all_to_all | solution.py:314
  29.7 10.5 %all-gather = bf16[72,16,128]{2,1,0:T(8,128)(2,1)S(1)} all-gather(bf16[9,16,128]{2,1,0:T(8,128)(2,1)S(1)} %sums.1), channel_id=2, replica_groups=mesh['space'=8,'filt'=4] {'space'}, dimensions={0}, use_global_device_ids=true | all-gather | bytes 331776 | tf_op jit(solution)/shard_map/all_gather | solution.py:419
  40.2 0.9 %unpack.1 = (bf16[16,16,128]{2,1,0:T(8,128)(2,1)}, f32[27,16,32]{2,1,0:T(8,128)}, f32[27,4,32]{2,1,0:T(4,128)}) custom-call(bf16[8,9,16,128]{3,2,1,0:T(8,128)(2,1)S(1)} %bitcast.8, bf16[4,13,16,128]{3,2,1,0:T(8,128)(2,1)S(1)} %all_to_all.10.parts), custom_call_target="tpu_custom_call" | custom-call | tf_op jit(solution)/shard_map/unpack/pallas_call | solution.py:420
  (4 shorter events, 0.1 us)
Async XLA Ops:
  2.5 9.1 %collective-permute-start = (bf16[3,256,128]{2,1,0:T(8,128)(2,1)S(1)}, bf16[3,256,128]{2,1,0:T(8,128)(2,1)S(1)}, u32[]{:S(2)}, u32[]{:S(2)}) collective-permute-start(bf16[3,256,128]{2,1,0:T(8,128)(2,1)S(1)} %get-tuple-element.20), channel_id=1, source_target_pairs={{0,4},{4,8},{8,12},{12,16},{16,20},{20,24},{24,28},{1,5},{5,9},{9,... | collective-permute-start | bytes 589832 | tf_op jit(solution)/shard_map/ppermute | solution.py:348
  4.9 10.6 %all-to-all-start = ((bf16[4,11,16,128]{3,2,1,0:T(8,128)(2,1)}), bf16[4,11,16,128]{3,2,1,0:T(8,128)(2,1)S(1)}, u32[]{:S(2)}, u32[]{:S(2)}) async-start(bf16[4,11,16,128]{3,2,1,0:T(8,128)(2,1)} %get-tuple-element.21), calls=%async_computation | async-start | bytes 360448 | tf_op jit(solution)/shard_map/all_to_all | solution.py:314
  11.7 2.6 %copy-start.1 = (bf16[27,4,32]{2,1,0:T(4,128)(2,1)S(1)}, bf16[27,4,32]{2,1,0:T(4,128)(2,1)}, u32[]{:S(2)}) copy-start(bf16[27,4,32]{2,1,0:T(4,128)(2,1)} %param.6) | copy-start | bytes 20740
  11.7 2.8 %copy-start = (bf16[3,128,144]{2,1,0:T(8,128)(2,1)S(1)}, bf16[3,128,144]{2,1,0:T(8,128)(2,1)}, u32[]{:S(2)}) copy-start(bf16[3,128,144]{2,1,0:T(8,128)(2,1)} %constant.5.clone.place) | copy-start | bytes 331780
  11.7 5.6 %collective-permute-start.1 = (bf16[7,48,128]{2,1,0:T(8,128)(2,1)S(1)}, bf16[7,48,128]{2,1,0:T(8,128)(2,1)S(1)}, u32[]{:S(2)}, u32[]{:S(2)}) collective-permute-start(bf16[7,48,128]{2,1,0:T(8,128)(2,1)S(1)} %border.1), channel_id=1, source_target_pairs={{0,1},{1,2},{2,3},{4,5},{5,6},{6,7},{8,9},{9,10},{10,11},{12,13},{... | collective-permute-start | bytes 258056 | tf_op jit(solution)/shard_map/ppermute | solution.py:358

commit v10 on v9

--- a/solution.py
+++ b/solution.py
@@ -306,7 +306,7 @@
 
 
 def exchange_order(filts):
-    return sorted(range(filts), key=lambda f: (abs(f - filts // 2), f))
+    return list(range(filts))[::-1]
 
 
 def exchange(chunks):

time: 41.4 us -> 43.5 us (1.051)
  waiting for transfers between devices: 0.58 us -> 2.37 us
  starting transfers between devices: 11.7 us -> 12.7 us
  blocking collectives: 21.4 us -> 20.7 us
    all_to_all x1, waiting for transfers between devices: 0.26 us -> 2.37 us  [exchange(): lax.all_to_all(chunks, 'filt', 0, 0, axis_index_groups=groups, tiled=True)]
    all_to_all x1, starting transfers between devices: 6.76 us -> 7.77 us  [exchange(): lax.all_to_all(chunks, 'filt', 0, 0, axis_index_groups=groups, tiled=True)]
    all_gather x1, blocking collectives: 10.5 us -> 9.58 us  [body(): sums = lax.all_gather(sums, 'space')]
  transfers between devices with their start and end apart: 3 -> 3, of which waited for: 2 -> 1; matrix products, arithmetic and copies ran while one was open for 0% -> 0% of each run, Pallas kernels for 5% -> 5%
where the time goes in v10:
time: 43.5 us; the launch traced here: 43.1 us
  blocking collectives  20.7 us (48%)
  starting transfers between devices  12.7 us (29%)
  Pallas kernels  6.52 us (15%)
  waiting for transfers between devices  2.37 us (5%)
  between operations  0.73 us (2%)
    all_to_all x1, blocking collectives, exchange(): lax.all_to_all(chunks, 'filt', 0, 0, axis_index_groups=groups, tiled=True)  11.1 us
    all_gather x1, blocking collectives, body(): sums = lax.all_gather(sums, 'space')  9.58 us
    all_to_all x1, starting transfers between devices, exchange(): lax.all_to_all(chunks, 'filt', 0, 0, axis_index_groups=groups, tiled=True)  7.77 us
    ppermute x1, starting transfers between devices, body(): border = lax.ppermute(border, 'filt', [(f - 1, f) for f in range(1, filts)])  2.6 us
    all_to_all x1, waiting for transfers between devices, exchange(): lax.all_to_all(chunks, 'filt', 0, 0, axis_index_groups=groups, tiled=True)  2.37 us
    ppermute x1, starting transfers between devices, body(): lax.ppermute(slab_x, 'space', [(s - 1, s) for s in range(1, spaces)])  2.37 us
    pallas_call x1, Pallas kernels, body(): pl.pallas_call(regroup_kernel, out_shape=[jax.ShapeDtypeStruct((planes, 1...  1.9 us
    pallas_call x1, Pallas kernels, body(): pl.pallas_call(upper_kernel, out_shape=[jax.ShapeDtypeStruct((64, 3 * LAN...  1.44 us
  transfers between devices with their start and end apart: 3, of which 1 were waited for; matrix products, arithmetic and copies ran while one was open for 0% of the time, Pallas kernels for 5%

profile of v10, /device:TPU:0, one launch (start us, length us, event | category | flops | bytes accessed | tf_op | source)
XLA Modules:
  0.0 43.1 jit_solution(6434060383942342564)
XLA Ops:
  0.6 1.9 %regroup.1 = (bf16[4,256,128]{2,1,0:T(8,128)(2,1)S(1)}, bf16[3,256,128]{2,1,0:T(8,128)(2,1)S(1)}, bf16[4,11,16,128]{3,2,1,0:T(8,128)(2,1)}) custom-call(bf16[4,4,16,512]{3,2,1,0:T(8,128)(2,1)} %volume_in.1, bf16[27,16,32]{2,1,0:T(8,128)(2,1)} %bitcast.9, bf16[16,16,128]{2,1,0:T(8,128)(2,1)} %bitcast.10), custom_call_target="tpu_custom_call" | custom-call | tf_op jit(solution)/shard_map/regroup/pallas_call | solution.py:329
  2.5 2.4 %collective-permute-start = (bf16[3,256,128]{2,1,0:T(8,128)(2,1)S(1)}, bf16[3,256,128]{2,1,0:T(8,128)(2,1)S(1)}, u32[]{:S(2)}, u32[]{:S(2)}) collective-permute-start(bf16[3,256,128]{2,1,0:T(8,128)(2,1)S(1)} %get-tuple-element.20), channel_id=1, source_target_pairs={{0,4},{4,8},{8,12},{12,16},{16,20},{20,24},{24,28},{1,5},{5,9},{9,... | collective-permute-start | bytes 589832 | tf_op jit(solution)/shard_map/ppermute | solution.py:348
  4.9 7.8 %all-to-all-start = ((bf16[4,11,16,128]{3,2,1,0:T(8,128)(2,1)}), bf16[4,11,16,128]{3,2,1,0:T(8,128)(2,1)S(1)}, u32[]{:S(2)}, u32[]{:S(2)}) async-start(bf16[4,11,16,128]{3,2,1,0:T(8,128)(2,1)} %get-tuple-element.21), calls=%async_computation | async-start | bytes 360448 | tf_op jit(solution)/shard_map/all_to_all | solution.py:314
  12.7 0.0 collective-permute-done.slab_x
  12.7 0.0 copy-start.1
  12.7 0.0 copy-start
  12.7 2.6 %collective-permute-start.1 = (bf16[7,48,128]{2,1,0:T(8,128)(2,1)S(1)}, bf16[7,48,128]{2,1,0:T(8,128)(2,1)S(1)}, u32[]{:S(2)}, u32[]{:S(2)}) collective-permute-start(bf16[7,48,128]{2,1,0:T(8,128)(2,1)S(1)} %border.1), channel_id=1, source_target_pairs={{0,1},{1,2},{2,3},{4,5},{5,6},{6,7},{8,9},{9,10},{10,11},{12,13},{... | collective-permute-start | bytes 258056 | tf_op jit(solution)/shard_map/ppermute | solution.py:358
  15.3 0.0 copy-done.1
  15.4 0.1 copy.12
  15.5 0.0 copy-done
  15.5 0.8 %stem_inner.1 = (bf16[96,144]{1,0:T(8,128)(2,1)S(1)}, bf16[7,48,896]{2,1,0:T(8,128)(2,1)S(1)}, f32[3,64,896]{2,1,0:T(8,128)S(1)}, bf16[3,96,896]{2,1,0:T(8,128)(2,1)S(1)}) custom-call(bf16[4,256,128]{2,1,0:T(8,128)(2,1)S(1)} %get-tuple-element.19.own, bf16[3,256,128]{2,1,0:T(8,128)(2,1)S(1)} %collective-permute-done.slab_x, bf16[32,128]{1,0:T(8,128)(2,1)S(1)} %pad.4.stem_w, ...), custom_call_target="tpu_custom_call" | custom-call | flops 200000000 | bytes 4000000 | tf_op jit(solution)/shard_map/stem_inner/pallas_call | solution.py:362
  16.3 2.4 %all-to-all-done.gathered = bf16[4,11,16,128]{3,2,1,0:T(8,128)(2,1)S(1)} async-done(((bf16[4,11,16,128]{3,2,1,0:T(8,128)(2,1)}), bf16[4,11,16,128]{3,2,1,0:T(8,128)(2,1)S(1)}, u32[]{:S(2)}, u32[]{:S(2)}) %all-to-all-start) | async-done | bytes 180256 | tf_op jit(solution)/shard_map/all_to_all | solution.py:314
  18.7 1.4 %upper_cells.1 = (bf16[64,384]{1,0:T(8,128)(2,1)S(1)}, f32[64,864]{1,0:T(8,128)S(1)}, f32[96,144]{1,0:T(8,128)S(1)}, bf16[64,896]{1,0:T(8,128)(2,1)S(1)}, bf16[1...) custom-call(bf16[4,11,16,128]{3,2,1,0:T(8,128)(2,1)S(1)} %all-to-all-done.gathered, ...), custom_call_target="tpu_custom_call" | custom-call | tf_op jit(solution)/shard_map/upper_cells/pallas_call | solution.py:376
  20.1 0.0 collective-permute-done.1.border
  20.1 1.4 %lower_cells.1 = bf16[4,13,16,128]{3,2,1,0:T(8,128)(2,1)S(1)} custom-call(bf16[4,256,128]{2,1,0:T(8,128)(2,1)S(1)} %get-tuple-element.19.own, bf16[3,256,128]{2,1,0:T(8,128)(2,1)S(1)} %collective-permute-done.slab_x, bf16[7,48,128]{2,1,0:T(8,128)(2,1)S(1)} %collective-permute-done.1.border, bf16[3,128,144]{2,1,0:T(8,128)(2,1)S(1)} %copy-done, ...), custom_call_target="tpu_custom_call" | custom-call | flops 600000000 | bytes 8000000 | tf_op jit(solution)/shard_map/lower_cells/pallas_call | solution.py:395
  21.5 11.1 %all_to_all.10.parts = bf16[4,13,16,128]{3,2,1,0:T(8,128)(2,1)S(1)} all-to-all(bf16[4,13,16,128]{3,2,1,0:T(8,128)(2,1)S(1)} %lower_cells.1), channel_id=1, replica_groups={{3,2,1,0},{7,6,5,4},{11,10,9,8},{15,14,13,12},{19,18,17,16},{23,22,21,2..., dimensions={0} | all-to-all | bytes 425984 | tf_op jit(solution)/shard_map/all_to_all | solution.py:314
  32.6 9.6 %all-gather = bf16[72,16,128]{2,1,0:T(8,128)(2,1)S(1)} all-gather(bf16[9,16,128]{2,1,0:T(8,128)(2,1)S(1)} %sums.1), channel_id=2, replica_groups=mesh['space'=8,'filt'=4] {'space'}, dimensions={0}, use_global_device_ids=true | all-gather | bytes 331776 | tf_op jit(solution)/shard_map/all_gather | solution.py:419
  42.2 0.9 %unpack.1 = (bf16[16,16,128]{2,1,0:T(8,128)(2,1)}, f32[27,16,32]{2,1,0:T(8,128)}, f32[27,4,32]{2,1,0:T(4,128)}) custom-call(bf16[8,9,16,128]{3,2,1,0:T(8,128)(2,1)S(1)} %bitcast.8, bf16[4,13,16,128]{3,2,1,0:T(8,128)(2,1)S(1)} %all_to_all.10.parts), custom_call_target="tpu_custom_call" | custom-call | tf_op jit(solution)/shard_map/unpack/pallas_call | solution.py:420
  (4 shorter events, 0.1 us)
Async XLA Ops:
  2.5 10.2 %collective-permute-start = (bf16[3,256,128]{2,1,0:T(8,128)(2,1)S(1)}, bf16[3,256,128]{2,1,0:T(8,128)(2,1)S(1)}, u32[]{:S(2)}, u32[]{:S(2)}) collective-permute-start(bf16[3,256,128]{2,1,0:T(8,128)(2,1)S(1)} %get-tuple-element.20), channel_id=1, source_target_pairs={{0,4},{4,8},{8,12},{12,16},{16,20},{20,24},{24,28},{1,5},{5,9},{9,... | collective-permute-start | bytes 589832 | tf_op jit(solution)/shard_map/ppermute | solution.py:348
  4.9 13.7 %all-to-all-start = ((bf16[4,11,16,128]{3,2,1,0:T(8,128)(2,1)}), bf16[4,11,16,128]{3,2,1,0:T(8,128)(2,1)S(1)}, u32[]{:S(2)}, u32[]{:S(2)}) async-start(bf16[4,11,16,128]{3,2,1,0:T(8,128)(2,1)} %get-tuple-element.21), calls=%async_computation | async-start | bytes 360448 | tf_op jit(solution)/shard_map/all_to_all | solution.py:314
  12.7 2.6 %copy-start.1 = (bf16[27,4,32]{2,1,0:T(4,128)(2,1)S(1)}, bf16[27,4,32]{2,1,0:T(4,128)(2,1)}, u32[]{:S(2)}) copy-start(bf16[27,4,32]{2,1,0:T(4,128)(2,1)} %param.6) | copy-start | bytes 20740
  12.7 2.8 %copy-start = (bf16[3,128,144]{2,1,0:T(8,128)(2,1)S(1)}, bf16[3,128,144]{2,1,0:T(8,128)(2,1)}, u32[]{:S(2)}) copy-start(bf16[3,128,144]{2,1,0:T(8,128)(2,1)} %constant.5.clone.place) | copy-start | bytes 331780
  12.7 7.4 %collective-permute-start.1 = (bf16[7,48,128]{2,1,0:T(8,128)(2,1)S(1)}, bf16[7,48,128]{2,1,0:T(8,128)(2,1)S(1)}, u32[]{:S(2)}, u32[]{:S(2)}) collective-permute-start(bf16[7,48,128]{2,1,0:T(8,128)(2,1)S(1)} %border.1), channel_id=1, source_target_pairs={{0,1},{1,2},{2,3},{4,5},{5,6},{6,7},{8,9},{9,10},{10,11},{12,13},{... | collective-permute-start | bytes 258056 | tf_op jit(solution)/shard_map/ppermute | solution.py:358

commit v11 on v9

--- a/solution.py
+++ b/solution.py
@@ -46,18 +46,37 @@
     return (source == column).astype(F32).astype(BF16)
 
 
-def regroup_kernel(volume_in, weight_in, cotangent_in, own, slab_x, packed_out, volume, weight, cotangent, packed, sems):
+def depth_phases(rows):
+    count = rows.shape[0]
+    z, column = rows_lanes((256, 256))
+    source = lax.shift_left(column & 63, 2) + lax.shift_right_logical(column, 6)
+    select = (z == source).astype(F32).astype(BF16)
+    halves = jnp.concatenate([rows[:, 0:256], rows[:, 256:512]], axis=0)
+    picked = nn(halves, select)
+    return [
+        jnp.concatenate([picked[h * count : (h + 1) * count, 64 * p : 64 * p + 64] for h in range(2)], axis=1)
+        for p in range(4)
+    ]
+
+
+def grouped_planes(volume, chosen):
     channels, planes, width, depth = volume.shape
-    pairs = [(weight_in, weight), (cotangent_in, cotangent), (packed, packed_out)]
-    pairs += [(volume_in.at[c], volume.at[c]) for c in range(channels)]
+    phases = [part.astype(BF16) for part in depth_phases(volume[...].reshape(channels * planes * width, depth))]
+    grouped = []
+    for x in chosen:
+        starts = [(c * planes + x) * width for c in range(channels)]
+        grouped.append(
+            jnp.concatenate([part[start : start + width] for part in phases for start in starts], axis=0)
+        )
+    return grouped
+
+
+def regroup_kernel(volume_in, weight_in, cotangent_in, own, packed_out, volume, weight, cotangent, packed, sems):
+    pairs = [(weight_in, weight), (cotangent_in, cotangent), (volume_in, volume), (packed, packed_out)]
     copies = [pltpu.make_async_copy(*pair, sems.at[k]) for k, pair in enumerate(pairs)]
-    for copy in copies[:2] + copies[3:]:
+    for copy in copies[:3]:
         copy.start()
-    z, column = rows_lanes((depth, depth))
-    source = lax.shift_left(column & (LANES - 1), 2) + lax.shift_right_logical(column, 7)
-    select = (z == source).astype(F32).astype(BF16)
     turn = turn_matrix()
-
     blank = jnp.zeros((16, 32), BF16)
     copies[0].wait()
     taps = [weight[t] if t < 27 else blank for t in range(28)]
@@ -71,31 +90,31 @@
         for j in range(4):
             row = 16 * (4 * f + j)
             packed[k, 7 + j] = turned[row : row + 16]
-    copies[2].start()
-
-    for copy in copies[3:]:
-        copy.wait()
-    picked = nn(volume[...].reshape(channels * planes * width, depth), select).astype(BF16)
+    copies[3].start()
+    copies[2].wait()
+    turned = nn(turn, jnp.concatenate(grouped_planes(volume, range(4)), axis=1)).astype(BF16)
+    for x in range(4):
+        own[x] = turned[:, x * LANES : (x + 1) * LANES]
+    copies[3].wait()
+
+
+def border_kernel(raw, own, border):
+    channels, planes, width, depth = raw.shape
+    rows = [raw[c, x, 8:16].astype(F32) for c in range(channels) for x in range(1, planes)]
+    phases = depth_phases(jnp.concatenate(rows, axis=0).astype(BF16))
     grouped = []
-    for x in range(planes):
-        parts = []
-        for phase in range(4):
-            for c in range(channels):
-                start = (c * planes + x) * width
-                parts.append(picked[start : start + width, phase * LANES : (phase + 1) * LANES])
-        grouped.append(jnp.concatenate(parts, axis=0))
-    turned = nn(turn, jnp.concatenate(grouped, axis=1)).astype(BF16)
-    for x in range(planes):
-        plane = turned[:, x * LANES : (x + 1) * LANES]
-        own[x] = plane
-        if x > 0:
-            slab_x[x - 1] = plane
-    copies[2].wait()
-
-
-def border_kernel(slab_x, own, border):
     for x in range(3):
-        border[x] = slab_x[x, -48:]
+        starts = [8 * (3 * c + x) for c in range(channels)]
+        grouped.append(
+            jnp.concatenate([part[start : start + 8] for part in phases for start in starts], axis=0)
+        )
+    row, column = rows_lanes((64, LANES))
+    source = lax.shift_left(row & 15, 3) + 4 + lax.shift_right_logical(row, 4)
+    turned = nn(
+        (source == column).astype(F32).astype(BF16), jnp.concatenate(grouped, axis=1).astype(BF16)
+    ).astype(BF16)
+    for x in range(3):
+        border[x] = turned[16:64, x * LANES : (x + 1) * LANES]
     for x in range(4):
         border[3 + x] = own[x, -48:]
 
@@ -136,9 +155,12 @@
     return jnp.where(lax.axis_index("space") > 0, 1.0, 0.0).astype(F32)
 
 
-def inner_kernel(own, slab_x, stem_w, place, weights, cols, slope, taps):
+def inner_kernel(own, raw, stem_w, place, slab, weights, cols, slope, taps):
+    turned = nn(turn_matrix(), jnp.concatenate(grouped_planes(raw, range(1, 4)), axis=1)).astype(BF16)
+    for x in range(3):
+        slab[x] = turned[:, x * LANES : (x + 1) * LANES]
     weights[...] = jnp.concatenate([nn(stem_w[...], place[g]) for g in range(3)], axis=0).astype(BF16)
-    planes = [slab_x[x, 16:256] if x < 3 else own[x - 3, 16:256] for x in range(7)]
+    planes = [turned[16:256, x * LANES : (x + 1) * LANES] if x < 3 else own[x - 3, 16:256] for x in range(7)]
     fill_columns(cols, planes, 7)
     for i in range(3):
         slope[i], taps[i] = stem_forward(weights[...], cols, i, keep_space() if i == 0 else 1.0)
@@ -325,27 +347,26 @@
     middle_cells = stem_cells // 8
     limit = pltpu.CompilerParams(vmem_limit_bytes=48 * 1024 * 1024)
 
-    raw = (volume, middle_weight.transpose(0, 2, 1), cotangent.reshape(16, 16, LANES))
-    own, slab_x, packed = pl.pallas_call(
+    raw = lax.ppermute(volume, "space", [(s - 1, s) for s in range(1, spaces)])
+    inputs = (volume, middle_weight.transpose(0, 2, 1), cotangent.reshape(16, 16, LANES))
+    own, packed = pl.pallas_call(
         regroup_kernel,
         out_shape=[
             jax.ShapeDtypeStruct((planes, 16 * width, LANES), BF16),
-            jax.ShapeDtypeStruct((planes - 1, 16 * width, LANES), BF16),
             jax.ShapeDtypeStruct((filts, 11, 16, LANES), BF16),
         ],
         in_specs=[pl.BlockSpec(memory_space=pltpu.HBM)] * 3,
-        out_specs=whole(2) + [pl.BlockSpec(memory_space=pl.ANY)],
+        out_specs=whole(1) + [pl.BlockSpec(memory_space=pl.ANY)],
         scratch_shapes=[
             pltpu.VMEM(volume.shape, BF16),
             pltpu.VMEM((27, 16, 32), BF16),
             pltpu.VMEM((16, 16, LANES), BF16),
             pltpu.VMEM((filts, 11, 16, LANES), BF16),
-            pltpu.SemaphoreType.DMA((3 + channels,)),
+            pltpu.SemaphoreType.DMA((4,)),
         ],
         compiler_params=limit,
         name="regroup",
-    )(*[pltpu.with_memory_space_constraint(x, pltpu.HBM) for x in raw])
-    slab_x = lax.ppermute(slab_x, "space", [(s - 1, s) for s in range(1, spaces)])
+    )(*[pltpu.with_memory_space_constraint(x, pltpu.HBM) for x in inputs])
     gathered = exchange(packed)
     border = pl.pallas_call(
         border_kernel,
@@ -354,25 +375,26 @@
         out_specs=whole(1)[0],
         compiler_params=limit,
         name="border",
-    )(slab_x, own)
+    )(raw, own)
     border = lax.ppermute(border, "filt", [(f - 1, f) for f in range(1, filts)])
 
     stem_w = jnp.pad(stem_weight.reshape(108, 32).T, ((0, 0), (0, 20)))
     place = jnp.asarray(place_table(), BF16)
-    weights, cols, slope, taps = pl.pallas_call(
+    slab, weights, cols, slope, taps = pl.pallas_call(
         inner_kernel,
         out_shape=[
+            jax.ShapeDtypeStruct((planes - 1, 16 * width, LANES), BF16),
             jax.ShapeDtypeStruct((96, STEM_ROWS), BF16),
             jax.ShapeDtypeStruct((7, 48, 7 * LANES), BF16),
             jax.ShapeDtypeStruct((3, 64, 7 * LANES), F32),
             jax.ShapeDtypeStruct((3, 96, 7 * LANES), BF16),
         ],
         in_specs=whole(4),
-        out_specs=whole(4),
+        out_specs=whole(5),
         compiler_params=limit,
         cost_estimate=pl.CostEstimate(flops=200_000_000, bytes_accessed=4_000_000, transcendentals=500_000),
         name="stem_inner",
-    )(own, slab_x, stem_w, place)
+    )(own, raw, stem_w, place)
     upper = pl.pallas_call(
         upper_kernel,
         out_shape=[
@@ -405,7 +427,7 @@
         compiler_params=limit,
         cost_estimate=pl.CostEstimate(flops=600_000_000, bytes_accessed=8_000_000, transcendentals=500_000),
         name="lower_cells",
-    )(own, slab_x, border, place, gathered, weights, cols, slope, taps, *upper)
+    )(own, slab, border, place, gathered, weights, cols, slope, taps, *upper)
 
     parts = exchange(parts)
     sums = pl.pallas_call(

time: 41.4 us -> 41.7 us (level)
  Pallas kernels: 6.49 us -> 7.4 us
  waiting for transfers between devices: 0.58 us -> 0.01 us
    pallas_call x1, Pallas kernels: 0.8 us -> 1.32 us  [body(): pl.pallas_call(inner_kernel, out_shape=[jax.ShapeDtypeStruct((planes - 1,...]
    all_to_all x1, blocking collectives: 11 us -> 11.5 us  [exchange(): lax.all_to_all(chunks, 'filt', 0, 0, axis_index_groups=groups, tiled=True)]
  transfers between devices with their start and end apart: 3 -> 3, of which waited for: 2 -> 0; matrix products, arithmetic and copies ran while one was open for 0% -> 0% of each run, Pallas kernels for 5% -> 12%
where the time goes in v11:
time: 41.7 us; the launch traced here: 41.4 us
  blocking collectives  21.5 us (52%)
  starting transfers between devices  11.6 us (28%)
  Pallas kernels  7.4 us (18%)
  between operations  0.73 us (2%)
    all_to_all x1, blocking collectives, exchange(): lax.all_to_all(chunks, 'filt', 0, 0, axis_index_groups=groups, tiled=True)  11.5 us
    all_gather x1, blocking collectives, body(): sums = lax.all_gather(sums, 'space')  10.1 us
    all_to_all x1, starting transfers between devices, exchange(): lax.all_to_all(chunks, 'filt', 0, 0, axis_index_groups=groups, tiled=True)  6.76 us
    ppermute x1, starting transfers between devices, body(): border = lax.ppermute(border, 'filt', [(f - 1, f) for f in range(1, filts)])  2.47 us
    ppermute x1, starting transfers between devices, body(): raw = lax.ppermute(volume, 'space', [(s - 1, s) for s in range(1, spaces)])  2.37 us
    pallas_call x1, Pallas kernels, body(): pl.pallas_call(regroup_kernel, out_shape=[jax.ShapeDtypeStruct((planes, 1...  1.88 us
    pallas_call x1, Pallas kernels, body(): pl.pallas_call(upper_kernel, out_shape=[jax.ShapeDtypeStruct((64, 3 * LAN...  1.44 us
    pallas_call x1, Pallas kernels, body(): pl.pallas_call(lower_kernel, out_shape=jax.ShapeDtypeStruct((filts, 13, 1...  1.4 us
  transfers between devices with their start and end apart: 3, of which 0 were waited for; matrix products, arithmetic and copies ran while one was open for 0% of the time, Pallas kernels for 12%

profile of v11, /device:TPU:0, one launch (start us, length us, event | category | flops | bytes accessed | tf_op | source)
XLA Modules:
  0.0 41.4 jit_solution(10864959289822993857)
XLA Ops:
  0.6 2.4 %collective-permute-start = (bf16[4,4,16,512]{3,2,1,0:T(8,128)(2,1)}, bf16[4,4,16,512]{3,2,1,0:T(8,128)(2,1)S(1)}, u32[]{:S(2)}, u32[]{:S(2)}) collective-permute-start(bf16[4,4,16,512]{3,2,1,0:T(8,128)(2,1)} %volume_in.1), channel_id=1, source_target_pairs={{0,4},{4,8},{8,12},{12,16},{16,20},{20,24},{24,28},{1,5},{5,9},{9,... | collective-permute-start | bytes 786440 | tf_op jit(solution)/shard_map/ppermute | solution.py:350
  3.0 1.9 %regroup.1 = (bf16[4,256,128]{2,1,0:T(8,128)(2,1)S(1)}, bf16[4,11,16,128]{3,2,1,0:T(8,128)(2,1)}) custom-call(bf16[4,4,16,512]{3,2,1,0:T(8,128)(2,1)} %volume_in.1, bf16[27,16,32]{2,1,0:T(8,128)(2,1)} %bitcast.9, bf16[16,16,128]{2,1,0:T(8,128)(2,1)} %bitcast.10), custom_call_target="tpu_custom_call" | custom-call | tf_op jit(solution)/shard_map/regroup/pallas_call | solution.py:352
  4.9 6.8 %all-to-all-start = ((bf16[4,11,16,128]{3,2,1,0:T(8,128)(2,1)}), bf16[4,11,16,128]{3,2,1,0:T(8,128)(2,1)S(1)}, u32[]{:S(2)}, u32[]{:S(2)}) async-start(bf16[4,11,16,128]{3,2,1,0:T(8,128)(2,1)} %get-tuple-element.21), calls=%async_computation | async-start | bytes 360448 | tf_op jit(solution)/shard_map/all_to_all | solution.py:336
  11.7 0.0 collective-permute-done.raw
  11.7 0.0 copy-start.1
  11.7 0.0 copy-start
  11.7 0.4 %border.1 = bf16[7,48,128]{2,1,0:T(8,128)(2,1)S(1)} custom-call(bf16[4,4,16,512]{3,2,1,0:T(8,128)(2,1)S(1)} %collective-permute-done.raw, bf16[4,256,128]{2,1,0:T(8,128)(2,1)S(1)} %get-tuple-element.19.own), custom_call_target="tpu_custom_call" | custom-call | tf_op jit(solution)/shard_map/border/pallas_call | solution.py:371
  12.1 2.5 %collective-permute-start.1 = (bf16[7,48,128]{2,1,0:T(8,128)(2,1)S(1)}, bf16[7,48,128]{2,1,0:T(8,128)(2,1)S(1)}, u32[]{:S(2)}, u32[]{:S(2)}) collective-permute-start(bf16[7,48,128]{2,1,0:T(8,128)(2,1)S(1)} %border.1), channel_id=1, source_target_pairs={{0,1},{1,2},{2,3},{4,5},{5,6},{6,7},{8,9},{9,10},{10,11},{12,13},{... | collective-permute-start | bytes 258056 | tf_op jit(solution)/shard_map/ppermute | solution.py:379
  14.6 0.0 copy-done.1
  14.6 0.1 copy.12
  14.7 0.0 copy-done
  14.7 1.3 %stem_inner.1 = (bf16[3,256,128]{2,1,0:T(8,128)(2,1)S(1)}, bf16[96,144]{1,0:T(8,128)(2,1)S(1)}, bf16[7,48,896]{2,1,0:T(8,128)(2,1)S(1)}, f32[3,64,896]{2,1,0:T(8,128)S(1)}, bf16[3,96,896]{2,1,0:T(8,128)(2,1)S(1)}) custom-call(bf16[4,256,128]{2,1,0:T(8,128)(2,1)S(1)} %get-tuple-element.19.own, bf16[4,4,16,512]{3,2,1,0:T(8,128)(2,1)S(1)} %collective-permute-done.raw, ...), custom_call_target="tpu_custom_call" | custom-call | flops 200000000 | bytes 4000000 | tf_op jit(solution)/shard_map/stem_inner/pallas_call | solution.py:383
  16.0 0.0 all-to-all-done.gathered
  16.0 1.4 %upper_cells.1 = (bf16[64,384]{1,0:T(8,128)(2,1)S(1)}, f32[64,864]{1,0:T(8,128)S(1)}, f32[96,144]{1,0:T(8,128)S(1)}, bf16[64,896]{1,0:T(8,128)(2,1)S(1)}, bf16[1...) custom-call(bf16[4,11,16,128]{3,2,1,0:T(8,128)(2,1)S(1)} %all-to-all-done.gathered, ...), custom_call_target="tpu_custom_call" | custom-call | tf_op jit(solution)/shard_map/upper_cells/pallas_call | solution.py:398
  17.5 0.0 collective-permute-done.1.border
  17.5 1.4 %lower_cells.1 = bf16[4,13,16,128]{3,2,1,0:T(8,128)(2,1)S(1)} custom-call(bf16[4,256,128]{2,1,0:T(8,128)(2,1)S(1)} %get-tuple-element.19.own, bf16[3,256,128]{2,1,0:T(8,128)(2,1)S(1)} %get-tuple-element.20.slab_x, bf16[7,48,128]{2,1,0:T(8,128)(2,1)S(1)} %collective-permute-done.1.border, bf16[3,128,144]{2,1,0:T(8,128)(2,1)S(1)} %copy-done, ...), custom_call_target="tpu_custom_call" | custom-call | flops 600000000 | bytes 8000000 | tf_op jit(solution)/shard_map/lower_cells/pallas_call | solution.py:417
  18.9 11.5 %all_to_all.10.parts = bf16[4,13,16,128]{3,2,1,0:T(8,128)(2,1)S(1)} all-to-all(bf16[4,13,16,128]{3,2,1,0:T(8,128)(2,1)S(1)} %lower_cells.1), channel_id=1, replica_groups={{2,1,3,0},{6,5,7,4},{10,9,11,8},{14,13,15,12},{18,17,19,16},{22,21,23,2..., dimensions={0} | all-to-all | bytes 425984 | tf_op jit(solution)/shard_map/all_to_all | solution.py:336
  30.4 10.1 %all-gather = bf16[72,16,128]{2,1,0:T(8,128)(2,1)S(1)} all-gather(bf16[9,16,128]{2,1,0:T(8,128)(2,1)S(1)} %sums.1), channel_id=2, replica_groups=mesh['space'=8,'filt'=4] {'space'}, dimensions={0}, use_global_device_ids=true | all-gather | bytes 331776 | tf_op jit(solution)/shard_map/all_gather | solution.py:441
  40.5 0.9 %unpack.1 = (bf16[16,16,128]{2,1,0:T(8,128)(2,1)}, f32[27,16,32]{2,1,0:T(8,128)}, f32[27,4,32]{2,1,0:T(4,128)}) custom-call(bf16[8,9,16,128]{3,2,1,0:T(8,128)(2,1)S(1)} %bitcast.8, bf16[4,13,16,128]{3,2,1,0:T(8,128)(2,1)S(1)} %all_to_all.10.parts), custom_call_target="tpu_custom_call" | custom-call | tf_op jit(solution)/shard_map/unpack/pallas_call | solution.py:442
  (3 shorter events, 0.1 us)
Async XLA Ops:
  0.6 11.0 %collective-permute-start = (bf16[4,4,16,512]{3,2,1,0:T(8,128)(2,1)}, bf16[4,4,16,512]{3,2,1,0:T(8,128)(2,1)S(1)}, u32[]{:S(2)}, u32[]{:S(2)}) collective-permute-start(bf16[4,4,16,512]{3,2,1,0:T(8,128)(2,1)} %volume_in.1), channel_id=1, source_target_pairs={{0,4},{4,8},{8,12},{12,16},{16,20},{20,24},{24,28},{1,5},{5,9},{9,... | collective-permute-start | bytes 786440 | tf_op jit(solution)/shard_map/ppermute | solution.py:350
  4.9 11.1 %all-to-all-start = ((bf16[4,11,16,128]{3,2,1,0:T(8,128)(2,1)}), bf16[4,11,16,128]{3,2,1,0:T(8,128)(2,1)S(1)}, u32[]{:S(2)}, u32[]{:S(2)}) async-start(bf16[4,11,16,128]{3,2,1,0:T(8,128)(2,1)} %get-tuple-element.21), calls=%async_computation | async-start | bytes 360448 | tf_op jit(solution)/shard_map/all_to_all | solution.py:336
  11.7 2.9 %copy-start.1 = (bf16[27,4,32]{2,1,0:T(4,128)(2,1)S(1)}, bf16[27,4,32]{2,1,0:T(4,128)(2,1)}, u32[]{:S(2)}) copy-start(bf16[27,4,32]{2,1,0:T(4,128)(2,1)} %param.6) | copy-start | bytes 20740
  11.7 3.0 %copy-start = (bf16[3,128,144]{2,1,0:T(8,128)(2,1)S(1)}, bf16[3,128,144]{2,1,0:T(8,128)(2,1)}, u32[]{:S(2)}) copy-start(bf16[3,128,144]{2,1,0:T(8,128)(2,1)} %constant.5.clone.place) | copy-start | bytes 331780
  12.1 5.4 %collective-permute-start.1 = (bf16[7,48,128]{2,1,0:T(8,128)(2,1)S(1)}, bf16[7,48,128]{2,1,0:T(8,128)(2,1)S(1)}, u32[]{:S(2)}, u32[]{:S(2)}) collective-permute-start(bf16[7,48,128]{2,1,0:T(8,128)(2,1)S(1)} %border.1), channel_id=1, source_target_pairs={{0,1},{1,2},{2,3},{4,5},{5,6},{6,7},{8,9},{9,10},{10,11},{12,13},{... | collective-permute-start | bytes 258056 | tf_op jit(solution)/shard_map/ppermute | solution.py:379

commit v12 on v9

--- a/solution.py
+++ b/solution.py
@@ -136,19 +136,22 @@
     return jnp.where(lax.axis_index("space") > 0, 1.0, 0.0).astype(F32)
 
 
-def inner_kernel(own, slab_x, stem_w, place, weights, cols, slope, taps):
-    weights[...] = jnp.concatenate([nn(stem_w[...], place[g]) for g in range(3)], axis=0).astype(BF16)
-    planes = [slab_x[x, 16:256] if x < 3 else own[x - 3, 16:256] for x in range(7)]
-    fill_columns(cols, planes, 7)
-    for i in range(3):
-        slope[i], taps[i] = stem_forward(weights[...], cols, i, keep_space() if i == 0 else 1.0)
-
-
 def fill_taps(mid_cols, part, i, j, first, count):
     for b in range(3):
         if (j - b) % 2 == 0 and first <= (j - b) // 2 < first + count:
             row = 96 * (3 * i + b)
             mid_cols[row : row + 96, pl.ds(((j - b) // 2 - first) * LANES, LANES)] = part
+
+
+def inner_kernel(own, slab_x, stem_w, place, weights, cols, slope, mid_cols, near_taps):
+    weights[...] = jnp.concatenate([nn(stem_w[...], place[g]) for g in range(3)], axis=0).astype(BF16)
+    planes = [slab_x[x, 16:256] if x < 3 else own[x - 3, 16:256] for x in range(7)]
+    fill_columns(cols, planes, 7)
+    for i in range(3):
+        slope[i], taps = stem_forward(weights[...], cols, i, keep_space() if i == 0 else 1.0)
+        for j in range(2, 9):
+            fill_taps(mid_cols, taps[:, (j - 2) * LANES : (j - 1) * LANES], i, j, 1, 3)
+        near_taps[i] = taps[:, 0:LANES]
 
 
 def middle_cells_step(mid_w, mid_cols, cotangent):
@@ -168,16 +171,13 @@
 
 
 def upper_kernel(
-    gathered, cols, slope, taps, features, mid_grad, stem_grad, mid_w, odd_w, even_w, mid_cols, stem_back,
+    gathered, cols, slope, mid_cols, features, mid_grad, stem_grad, mid_w, odd_w, even_w, stem_back,
 ):
     blocks = gathered.shape[0]
     order = exchange_order(blocks)
     for k, f in enumerate(order):
         for t in range(7):
             mid_w[16 * f : 16 * f + 16, t * LANES : (t + 1) * LANES] = gathered[k, t]
-    for i in range(3):
-        for j in range(2, 9):
-            fill_taps(mid_cols, taps[i, :, pl.ds((j - 2) * LANES, LANES)], i, j, 1, 3)
     cotangent = jnp.concatenate(
         [jnp.concatenate([gathered[order.index(f), 7 + j] for j in range(1, 4)], axis=1) for f in range(blocks)],
         axis=0,
@@ -219,7 +219,7 @@
 
 
 def lower_kernel(
-    own, slab_x, border, place, gathered, weights, cols, slope, taps, upper_features, upper_mid, upper_stem,
+    own, slab_x, border, place, gathered, weights, cols, slope, near_taps, upper_features, upper_mid, upper_stem,
     mid_w, odd_w, even_w, parts, low_cols, mid_cols, low_back,
 ):
     blocks = gathered.shape[0]
@@ -238,7 +238,7 @@
         low_slope.append(one_slope)
         for j in range(2):
             fill_taps(mid_cols, low_taps[:, j * LANES : (j + 1) * LANES], i, j, 0, 1)
-        fill_taps(mid_cols, taps[i, :, 0:LANES], i, 2, 0, 1)
+        fill_taps(mid_cols, near_taps[i], i, 2, 0, 1)
     order = exchange_order(blocks)
     cotangent = jnp.concatenate([gathered[order.index(f), 7] for f in range(blocks)], axis=0)
     features, mid_grad, both = middle_cells_step(mid_w, mid_cols, cotangent)
@@ -359,16 +359,17 @@
 
     stem_w = jnp.pad(stem_weight.reshape(108, 32).T, ((0, 0), (0, 20)))
     place = jnp.asarray(place_table(), BF16)
-    weights, cols, slope, taps = pl.pallas_call(
+    weights, cols, slope, mid_cols, near_taps = pl.pallas_call(
         inner_kernel,
         out_shape=[
             jax.ShapeDtypeStruct((96, STEM_ROWS), BF16),
             jax.ShapeDtypeStruct((7, 48, 7 * LANES), BF16),
             jax.ShapeDtypeStruct((3, 64, 7 * LANES), F32),
-            jax.ShapeDtypeStruct((3, 96, 7 * LANES), BF16),
+            jax.ShapeDtypeStruct((864, 3 * LANES), BF16),
+            jax.ShapeDtypeStruct((3, 96, LANES), BF16),
         ],
         in_specs=whole(4),
-        out_specs=whole(4),
+        out_specs=whole(5),
         compiler_params=limit,
         cost_estimate=pl.CostEstimate(flops=200_000_000, bytes_accessed=4_000_000, transcendentals=500_000),
         name="stem_inner",
@@ -385,13 +386,10 @@
         ],
         in_specs=whole(4),
         out_specs=whole(6),
-        scratch_shapes=[
-            pltpu.VMEM((864, 3 * LANES), BF16),
-            pltpu.VMEM((3, 96, 7 * LANES), BF16),
-        ],
+        scratch_shapes=[pltpu.VMEM((3, 96, 7 * LANES), BF16)],
         compiler_params=limit,
         name="upper_cells",
-    )(gathered, cols, slope, taps)
+    )(gathered, cols, slope, mid_cols)
     parts = pl.pallas_call(
         lower_kernel,
         out_shape=jax.ShapeDtypeStruct((filts, 13, 16, LANES), BF16),
@@ -405,7 +403,7 @@
         compiler_params=limit,
         cost_estimate=pl.CostEstimate(flops=600_000_000, bytes_accessed=8_000_000, transcendentals=500_000),
         name="lower_cells",
-    )(own, slab_x, border, place, gathered, weights, cols, slope, taps, *upper)
+    )(own, slab_x, border, place, gathered, weights, cols, slope, near_taps, *upper)
 
     parts = exchange(parts)
     sums = pl.pallas_call(
@@ -416,7 +414,8 @@
         compiler_params=limit,
         name="sums",
     )(parts)
-    sums = lax.all_gather(sums, "space")
+    around = [(s + 2) % spaces for s in range(spaces)]
+    sums = lax.all_gather(sums, "space", axis_index_groups=[around])
     features, middle, stem = pl.pallas_call(
         functools.partial(unpack_kernel, middle_cells**-0.5, stem_cells**-0.5),
         out_shape=[

time: 41.4 us -> 44 us (1.063)
  blocking collectives: 21.4 us -> 24.1 us
    all_gather x1, blocking collectives: 10.5 us -> 13 us  [body(): sums = lax.all_gather(sums, 'space', axis_index_groups=[around])]
where the time goes in v12:
time: 44 us; the launch traced here: 43.7 us
  blocking collectives  24.1 us (55%)
  starting transfers between devices  11.7 us (27%)
  Pallas kernels  6.46 us (15%)
  between operations  0.72 us (2%)
  waiting for transfers between devices  0.61 us (1%)
    all_gather x1, blocking collectives, body(): sums = lax.all_gather(sums, 'space', axis_index_groups=[around])  13 us
    all_to_all x1, blocking collectives, exchange(): lax.all_to_all(chunks, 'filt', 0, 0, axis_index_groups=groups, tiled=True)  11.1 us
    all_to_all x1, starting transfers between devices, exchange(): lax.all_to_all(chunks, 'filt', 0, 0, axis_index_groups=groups, tiled=True)  6.76 us
    ppermute x1, starting transfers between devices, body(): border = lax.ppermute(border, 'filt', [(f - 1, f) for f in range(1, filts)])  2.6 us
    ppermute x1, starting transfers between devices, body(): lax.ppermute(slab_x, 'space', [(s - 1, s) for s in range(1, spaces)])  2.37 us
    pallas_call x1, Pallas kernels, body(): pl.pallas_call(regroup_kernel, out_shape=[jax.ShapeDtypeStruct((planes, 1...  1.9 us
    pallas_call x1, Pallas kernels, body(): pl.pallas_call(lower_kernel, out_shape=jax.ShapeDtypeStruct((filts, 13, 1...  1.41 us
    pallas_call x1, Pallas kernels, body(): pl.pallas_call(upper_kernel, out_shape=[jax.ShapeDtypeStruct((64, 3 * LAN...  1.36 us
  transfers between devices with their start and end apart: 3, of which 2 were waited for; matrix products, arithmetic and copies ran while one was open for 0% of the time, Pallas kernels for 5%

profile of v12, /device:TPU:0, one launch (start us, length us, event | category | flops | bytes accessed | tf_op | source)
XLA Modules:
  0.0 43.7 jit_solution(13200889076746025349)
XLA Ops:
  0.6 1.9 %regroup.1 = (bf16[4,256,128]{2,1,0:T(8,128)(2,1)S(1)}, bf16[3,256,128]{2,1,0:T(8,128)(2,1)S(1)}, bf16[4,11,16,128]{3,2,1,0:T(8,128)(2,1)}) custom-call(bf16[4,4,16,512]{3,2,1,0:T(8,128)(2,1)} %volume_in.1, bf16[27,16,32]{2,1,0:T(8,128)(2,1)} %bitcast.9, bf16[16,16,128]{2,1,0:T(8,128)(2,1)} %bitcast.10), custom_call_target="tpu_custom_call" | custom-call | tf_op jit(solution)/shard_map/regroup/pallas_call | solution.py:329
  2.5 2.4 %collective-permute-start = (bf16[3,256,128]{2,1,0:T(8,128)(2,1)S(1)}, bf16[3,256,128]{2,1,0:T(8,128)(2,1)S(1)}, u32[]{:S(2)}, u32[]{:S(2)}) collective-permute-start(bf16[3,256,128]{2,1,0:T(8,128)(2,1)S(1)} %get-tuple-element.21), channel_id=1, source_target_pairs={{0,4},{4,8},{8,12},{12,16},{16,20},{20,24},{24,28},{1,5},{5,9},{9,... | collective-permute-start | bytes 589832 | tf_op jit(solution)/shard_map/ppermute | solution.py:348
  4.9 6.8 %all-to-all-start = ((bf16[4,11,16,128]{3,2,1,0:T(8,128)(2,1)}), bf16[4,11,16,128]{3,2,1,0:T(8,128)(2,1)S(1)}, u32[]{:S(2)}, u32[]{:S(2)}) async-start(bf16[4,11,16,128]{3,2,1,0:T(8,128)(2,1)} %get-tuple-element.22), calls=%async_computation | async-start | bytes 360448 | tf_op jit(solution)/shard_map/all_to_all | solution.py:314
  11.7 0.0 collective-permute-done.slab_x
  11.7 0.0 copy-start.1
  11.7 0.0 copy-start
  11.7 2.6 %collective-permute-start.1 = (bf16[7,48,128]{2,1,0:T(8,128)(2,1)S(1)}, bf16[7,48,128]{2,1,0:T(8,128)(2,1)S(1)}, u32[]{:S(2)}, u32[]{:S(2)}) collective-permute-start(bf16[7,48,128]{2,1,0:T(8,128)(2,1)S(1)} %border.1), channel_id=1, source_target_pairs={{0,1},{1,2},{2,3},{4,5},{5,6},{6,7},{8,9},{9,10},{10,11},{12,13},{... | collective-permute-start | bytes 258056 | tf_op jit(solution)/shard_map/ppermute | solution.py:358
  14.3 0.0 copy-done.1
  14.3 0.1 copy.12
  14.4 0.0 copy-done
  14.5 0.8 %stem_inner.1 = (bf16[96,144]{1,0:T(8,128)(2,1)S(1)}, bf16[7,48,896]{2,1,0:T(8,128)(2,1)S(1)}, f32[3,64,896]{2,1,0:T(8,128)S(1)}, bf16[864,384]{1,0:T(8,128)(2,1)S(1)}, bf16[3,96,128]{2,1,0:T(8,128)(2,1)S(1)}) custom-call(bf16[4,256,128]{2,1,0:T(8,128)(2,1)S(1)} %get-tuple-element.20.own, bf16[3,256,128]{2,1,0:T(8,128)(2,1)S(1)} %collective-permute-done.slab_x, ...), custom_call_target="tpu_custom_call" | custom-call | flops 200000000 | bytes 4000000 | tf_op jit(solution)/shard_map/stem_inner/pallas_call | solution.py:362
  15.3 0.2 all-to-all-done.gathered
  15.5 1.4 %upper_cells.1 = (bf16[64,384]{1,0:T(8,128)(2,1)S(1)}, f32[64,864]{1,0:T(8,128)S(1)}, f32[96,144]{1,0:T(8,128)S(1)}, bf16[64,896]{1,0:T(8,128)(2,1)S(1)}, bf16[1...) custom-call(bf16[4,11,16,128]{3,2,1,0:T(8,128)(2,1)S(1)} %all-to-all-done.gathered, ...), custom_call_target="tpu_custom_call" | custom-call | tf_op jit(solution)/shard_map/upper_cells/pallas_call | solution.py:377
  16.9 0.4 collective-permute-done.1.border
  17.3 1.4 %lower_cells.1 = bf16[4,13,16,128]{3,2,1,0:T(8,128)(2,1)S(1)} custom-call(bf16[4,256,128]{2,1,0:T(8,128)(2,1)S(1)} %get-tuple-element.20.own, bf16[3,256,128]{2,1,0:T(8,128)(2,1)S(1)} %collective-permute-done.slab_x, bf16[7,48,128]{2,1,0:T(8,128)(2,1)S(1)} %collective-permute-done.1.border, bf16[3,128,144]{2,1,0:T(8,128)(2,1)S(1)} %copy-done, ...), custom_call_target="tpu_custom_call" | custom-call | flops 600000000 | bytes 8000000 | tf_op jit(solution)/shard_map/lower_cells/pallas_call | solution.py:393
  18.7 11.1 %all_to_all.10.parts = bf16[4,13,16,128]{3,2,1,0:T(8,128)(2,1)S(1)} all-to-all(bf16[4,13,16,128]{3,2,1,0:T(8,128)(2,1)S(1)} %lower_cells.1), channel_id=1, replica_groups={{2,1,3,0},{6,5,7,4},{10,9,11,8},{14,13,15,12},{18,17,19,16},{22,21,23,2..., dimensions={0} | all-to-all | bytes 425984 | tf_op jit(solution)/shard_map/all_to_all | solution.py:314
  29.8 13.0 %all-gather = bf16[72,16,128]{2,1,0:T(8,128)(2,1)S(1)} all-gather(bf16[9,16,128]{2,1,0:T(8,128)(2,1)S(1)} %sums.1), channel_id=2, replica_groups={{8,12,16,20,24,28,0,4},{9,13,17,21,25,29,1,5},{10,14,18,22,26,30,2,6},{..., dimensions={0}, use_global_device_ids=true | all-gather | bytes 331776 | tf_op jit(solution)/shard_map/all_gather | solution.py:418
  42.8 0.9 %unpack.1 = (bf16[16,16,128]{2,1,0:T(8,128)(2,1)}, f32[27,16,32]{2,1,0:T(8,128)}, f32[27,4,32]{2,1,0:T(4,128)}) custom-call(bf16[8,9,16,128]{3,2,1,0:T(8,128)(2,1)S(1)} %bitcast.8, bf16[4,13,16,128]{3,2,1,0:T(8,128)(2,1)S(1)} %all_to_all.10.parts), custom_call_target="tpu_custom_call" | custom-call | tf_op jit(solution)/shard_map/unpack/pallas_call | solution.py:419
  (4 shorter events, 0.1 us)
Async XLA Ops:
  2.5 9.1 %collective-permute-start = (bf16[3,256,128]{2,1,0:T(8,128)(2,1)S(1)}, bf16[3,256,128]{2,1,0:T(8,128)(2,1)S(1)}, u32[]{:S(2)}, u32[]{:S(2)}) collective-permute-start(bf16[3,256,128]{2,1,0:T(8,128)(2,1)S(1)} %get-tuple-element.21), channel_id=1, source_target_pairs={{0,4},{4,8},{8,12},{12,16},{16,20},{20,24},{24,28},{1,5},{5,9},{9,... | collective-permute-start | bytes 589832 | tf_op jit(solution)/shard_map/ppermute | solution.py:348
  4.9 10.6 %all-to-all-start = ((bf16[4,11,16,128]{3,2,1,0:T(8,128)(2,1)}), bf16[4,11,16,128]{3,2,1,0:T(8,128)(2,1)S(1)}, u32[]{:S(2)}, u32[]{:S(2)}) async-start(bf16[4,11,16,128]{3,2,1,0:T(8,128)(2,1)} %get-tuple-element.22), calls=%async_computation | async-start | bytes 360448 | tf_op jit(solution)/shard_map/all_to_all | solution.py:314
  11.7 2.6 %copy-start.1 = (bf16[27,4,32]{2,1,0:T(4,128)(2,1)S(1)}, bf16[27,4,32]{2,1,0:T(4,128)(2,1)}, u32[]{:S(2)}) copy-start(bf16[27,4,32]{2,1,0:T(4,128)(2,1)} %param.6) | copy-start | bytes 20740
  11.7 2.8 %copy-start = (bf16[3,128,144]{2,1,0:T(8,128)(2,1)S(1)}, bf16[3,128,144]{2,1,0:T(8,128)(2,1)}, u32[]{:S(2)}) copy-start(bf16[3,128,144]{2,1,0:T(8,128)(2,1)} %constant.5.clone.place) | copy-start | bytes 331780
  11.7 5.6 %collective-permute-start.1 = (bf16[7,48,128]{2,1,0:T(8,128)(2,1)S(1)}, bf16[7,48,128]{2,1,0:T(8,128)(2,1)S(1)}, u32[]{:S(2)}, u32[]{:S(2)}) collective-permute-start(bf16[7,48,128]{2,1,0:T(8,128)(2,1)S(1)} %border.1), channel_id=1, source_target_pairs={{0,1},{1,2},{2,3},{4,5},{5,6},{6,7},{8,9},{9,10},{10,11},{12,13},{... | collective-permute-start | bytes 258056 | tf_op jit(solution)/shard_map/ppermute | solution.py:358

commit v13 on v12

--- a/solution.py
+++ b/solution.py
@@ -414,8 +414,7 @@
         compiler_params=limit,
         name="sums",
     )(parts)
-    around = [(s + 2) % spaces for s in range(spaces)]
-    sums = lax.all_gather(sums, "space", axis_index_groups=[around])
+    sums = lax.all_gather(sums, "space")
     features, middle, stem = pl.pallas_call(
         functools.partial(unpack_kernel, middle_cells**-0.5, stem_cells**-0.5),
         out_shape=[

time: 44 us -> 41.3 us (0.939)
  blocking collectives: 24.1 us -> 21.4 us
    all_gather x1, blocking collectives: 13 us -> 10.3 us  [body(): sums = lax.all_gather(sums, 'space')]
where the time goes in v13:
time: 41.3 us; the launch traced here: 41 us
  blocking collectives  21.4 us (52%)
  starting transfers between devices  11.7 us (28%)
  Pallas kernels  6.46 us (16%)
  between operations  0.72 us (2%)
  waiting for transfers between devices  0.61 us (1%)
    all_to_all x1, blocking collectives, exchange(): lax.all_to_all(chunks, 'filt', 0, 0, axis_index_groups=groups, tiled=True)  11.1 us
    all_gather x1, blocking collectives, body(): sums = lax.all_gather(sums, 'space')  10.3 us
    all_to_all x1, starting transfers between devices, exchange(): lax.all_to_all(chunks, 'filt', 0, 0, axis_index_groups=groups, tiled=True)  6.76 us
    ppermute x1, starting transfers between devices, body(): border = lax.ppermute(border, 'filt', [(f - 1, f) for f in range(1, filts)])  2.6 us
    ppermute x1, starting transfers between devices, body(): lax.ppermute(slab_x, 'space', [(s - 1, s) for s in range(1, spaces)])  2.37 us
    pallas_call x1, Pallas kernels, body(): pl.pallas_call(regroup_kernel, out_shape=[jax.ShapeDtypeStruct((planes, 1...  1.9 us
    pallas_call x1, Pallas kernels, body(): pl.pallas_call(lower_kernel, out_shape=jax.ShapeDtypeStruct((filts, 13, 1...  1.41 us
    pallas_call x1, Pallas kernels, body(): pl.pallas_call(upper_kernel, out_shape=[jax.ShapeDtypeStruct((64, 3 * LAN...  1.36 us
  transfers between devices with their start and end apart: 3, of which 2 were waited for; matrix products, arithmetic and copies ran while one was open for 0% of the time, Pallas kernels for 5%

profile of v13, /device:TPU:0, one launch (start us, length us, event | category | flops | bytes accessed | tf_op | source)
XLA Modules:
  0.0 41.0 jit_solution(15983481112375303436)
XLA Ops:
  0.6 1.9 %regroup.1 = (bf16[4,256,128]{2,1,0:T(8,128)(2,1)S(1)}, bf16[3,256,128]{2,1,0:T(8,128)(2,1)S(1)}, bf16[4,11,16,128]{3,2,1,0:T(8,128)(2,1)}) custom-call(bf16[4,4,16,512]{3,2,1,0:T(8,128)(2,1)} %volume_in.1, bf16[27,16,32]{2,1,0:T(8,128)(2,1)} %bitcast.9, bf16[16,16,128]{2,1,0:T(8,128)(2,1)} %bitcast.10), custom_call_target="tpu_custom_call" | custom-call | tf_op jit(solution)/shard_map/regroup/pallas_call | solution.py:329
  2.5 2.4 %collective-permute-start = (bf16[3,256,128]{2,1,0:T(8,128)(2,1)S(1)}, bf16[3,256,128]{2,1,0:T(8,128)(2,1)S(1)}, u32[]{:S(2)}, u32[]{:S(2)}) collective-permute-start(bf16[3,256,128]{2,1,0:T(8,128)(2,1)S(1)} %get-tuple-element.21), channel_id=1, source_target_pairs={{0,4},{4,8},{8,12},{12,16},{16,20},{20,24},{24,28},{1,5},{5,9},{9,... | collective-permute-start | bytes 589832 | tf_op jit(solution)/shard_map/ppermute | solution.py:348
  4.9 6.8 %all-to-all-start = ((bf16[4,11,16,128]{3,2,1,0:T(8,128)(2,1)}), bf16[4,11,16,128]{3,2,1,0:T(8,128)(2,1)S(1)}, u32[]{:S(2)}, u32[]{:S(2)}) async-start(bf16[4,11,16,128]{3,2,1,0:T(8,128)(2,1)} %get-tuple-element.22), calls=%async_computation | async-start | bytes 360448 | tf_op jit(solution)/shard_map/all_to_all | solution.py:314
  11.7 0.0 collective-permute-done.slab_x
  11.7 0.0 copy-start.1
  11.7 0.0 copy-start
  11.7 2.6 %collective-permute-start.1 = (bf16[7,48,128]{2,1,0:T(8,128)(2,1)S(1)}, bf16[7,48,128]{2,1,0:T(8,128)(2,1)S(1)}, u32[]{:S(2)}, u32[]{:S(2)}) collective-permute-start(bf16[7,48,128]{2,1,0:T(8,128)(2,1)S(1)} %border.1), channel_id=1, source_target_pairs={{0,1},{1,2},{2,3},{4,5},{5,6},{6,7},{8,9},{9,10},{10,11},{12,13},{... | collective-permute-start | bytes 258056 | tf_op jit(solution)/shard_map/ppermute | solution.py:358
  14.3 0.0 copy-done.1
  14.3 0.1 copy.12
  14.4 0.0 copy-done
  14.5 0.8 %stem_inner.1 = (bf16[96,144]{1,0:T(8,128)(2,1)S(1)}, bf16[7,48,896]{2,1,0:T(8,128)(2,1)S(1)}, f32[3,64,896]{2,1,0:T(8,128)S(1)}, bf16[864,384]{1,0:T(8,128)(2,1)S(1)}, bf16[3,96,128]{2,1,0:T(8,128)(2,1)S(1)}) custom-call(bf16[4,256,128]{2,1,0:T(8,128)(2,1)S(1)} %get-tuple-element.20.own, bf16[3,256,128]{2,1,0:T(8,128)(2,1)S(1)} %collective-permute-done.slab_x, ...), custom_call_target="tpu_custom_call" | custom-call | flops 200000000 | bytes 4000000 | tf_op jit(solution)/shard_map/stem_inner/pallas_call | solution.py:362
  15.3 0.2 all-to-all-done.gathered
  15.5 1.4 %upper_cells.1 = (bf16[64,384]{1,0:T(8,128)(2,1)S(1)}, f32[64,864]{1,0:T(8,128)S(1)}, f32[96,144]{1,0:T(8,128)S(1)}, bf16[64,896]{1,0:T(8,128)(2,1)S(1)}, bf16[1...) custom-call(bf16[4,11,16,128]{3,2,1,0:T(8,128)(2,1)S(1)} %all-to-all-done.gathered, ...), custom_call_target="tpu_custom_call" | custom-call | tf_op jit(solution)/shard_map/upper_cells/pallas_call | solution.py:377
  16.9 0.4 collective-permute-done.1.border
  17.3 1.4 %lower_cells.1 = bf16[4,13,16,128]{3,2,1,0:T(8,128)(2,1)S(1)} custom-call(bf16[4,256,128]{2,1,0:T(8,128)(2,1)S(1)} %get-tuple-element.20.own, bf16[3,256,128]{2,1,0:T(8,128)(2,1)S(1)} %collective-permute-done.slab_x, bf16[7,48,128]{2,1,0:T(8,128)(2,1)S(1)} %collective-permute-done.1.border, bf16[3,128,144]{2,1,0:T(8,128)(2,1)S(1)} %copy-done, ...), custom_call_target="tpu_custom_call" | custom-call | flops 600000000 | bytes 8000000 | tf_op jit(solution)/shard_map/lower_cells/pallas_call | solution.py:393
  18.7 11.1 %all_to_all.10.parts = bf16[4,13,16,128]{3,2,1,0:T(8,128)(2,1)S(1)} all-to-all(bf16[4,13,16,128]{3,2,1,0:T(8,128)(2,1)S(1)} %lower_cells.1), channel_id=1, replica_groups={{2,1,3,0},{6,5,7,4},{10,9,11,8},{14,13,15,12},{18,17,19,16},{22,21,23,2..., dimensions={0} | all-to-all | bytes 425984 | tf_op jit(solution)/shard_map/all_to_all | solution.py:314
  29.8 10.3 %all-gather = bf16[72,16,128]{2,1,0:T(8,128)(2,1)S(1)} all-gather(bf16[9,16,128]{2,1,0:T(8,128)(2,1)S(1)} %sums.1), channel_id=2, replica_groups=mesh['space'=8,'filt'=4] {'space'}, dimensions={0}, use_global_device_ids=true | all-gather | bytes 331776 | tf_op jit(solution)/shard_map/all_gather | solution.py:417
  40.1 0.9 %unpack.1 = (bf16[16,16,128]{2,1,0:T(8,128)(2,1)}, f32[27,16,32]{2,1,0:T(8,128)}, f32[27,4,32]{2,1,0:T(4,128)}) custom-call(bf16[8,9,16,128]{3,2,1,0:T(8,128)(2,1)S(1)} %bitcast.8, bf16[4,13,16,128]{3,2,1,0:T(8,128)(2,1)S(1)} %all_to_all.10.parts), custom_call_target="tpu_custom_call" | custom-call | tf_op jit(solution)/shard_map/unpack/pallas_call | solution.py:418
  (4 shorter events, 0.1 us)
Async XLA Ops:
  2.5 9.1 %collective-permute-start = (bf16[3,256,128]{2,1,0:T(8,128)(2,1)S(1)}, bf16[3,256,128]{2,1,0:T(8,128)(2,1)S(1)}, u32[]{:S(2)}, u32[]{:S(2)}) collective-permute-start(bf16[3,256,128]{2,1,0:T(8,128)(2,1)S(1)} %get-tuple-element.21), channel_id=1, source_target_pairs={{0,4},{4,8},{8,12},{12,16},{16,20},{20,24},{24,28},{1,5},{5,9},{9,... | collective-permute-start | bytes 589832 | tf_op jit(solution)/shard_map/ppermute | solution.py:348
  4.9 10.6 %all-to-all-start = ((bf16[4,11,16,128]{3,2,1,0:T(8,128)(2,1)}), bf16[4,11,16,128]{3,2,1,0:T(8,128)(2,1)S(1)}, u32[]{:S(2)}, u32[]{:S(2)}) async-start(bf16[4,11,16,128]{3,2,1,0:T(8,128)(2,1)} %get-tuple-element.22), calls=%async_computation | async-start | bytes 360448 | tf_op jit(solution)/shard_map/all_to_all | solution.py:314
  11.7 2.6 %copy-start.1 = (bf16[27,4,32]{2,1,0:T(4,128)(2,1)S(1)}, bf16[27,4,32]{2,1,0:T(4,128)(2,1)}, u32[]{:S(2)}) copy-start(bf16[27,4,32]{2,1,0:T(4,128)(2,1)} %param.6) | copy-start | bytes 20740
  11.7 2.8 %copy-start = (bf16[3,128,144]{2,1,0:T(8,128)(2,1)S(1)}, bf16[3,128,144]{2,1,0:T(8,128)(2,1)}, u32[]{:S(2)}) copy-start(bf16[3,128,144]{2,1,0:T(8,128)(2,1)} %constant.5.clone.place) | copy-start | bytes 331780
  11.7 5.6 %collective-permute-start.1 = (bf16[7,48,128]{2,1,0:T(8,128)(2,1)S(1)}, bf16[7,48,128]{2,1,0:T(8,128)(2,1)S(1)}, u32[]{:S(2)}, u32[]{:S(2)}) collective-permute-start(bf16[7,48,128]{2,1,0:T(8,128)(2,1)S(1)} %border.1), channel_id=1, source_target_pairs={{0,1},{1,2},{2,3},{4,5},{5,6},{6,7},{8,9},{9,10},{10,11},{12,13},{... | collective-permute-start | bytes 258056 | tf_op jit(solution)/shard_map/ppermute | solution.py:358

commit v14 on v13

--- a/solution.py
+++ b/solution.py
@@ -46,12 +46,12 @@
     return (source == column).astype(F32).astype(BF16)
 
 
-def regroup_kernel(volume_in, weight_in, cotangent_in, own, slab_x, packed_out, volume, weight, cotangent, packed, sems):
+def regroup_kernel(volume_in, weight_in, cotangent_in, own, slab_x, packed, volume, weight, cotangent, sems):
     channels, planes, width, depth = volume.shape
-    pairs = [(weight_in, weight), (cotangent_in, cotangent), (packed, packed_out)]
+    pairs = [(weight_in, weight), (cotangent_in, cotangent)]
     pairs += [(volume_in.at[c], volume.at[c]) for c in range(channels)]
     copies = [pltpu.make_async_copy(*pair, sems.at[k]) for k, pair in enumerate(pairs)]
-    for copy in copies[:2] + copies[3:]:
+    for copy in copies:
         copy.start()
     z, column = rows_lanes((depth, depth))
     source = lax.shift_left(column & (LANES - 1), 2) + lax.shift_right_logical(column, 7)
@@ -71,9 +71,8 @@
         for j in range(4):
             row = 16 * (4 * f + j)
             packed[k, 7 + j] = turned[row : row + 16]
-    copies[2].start()
-
-    for copy in copies[3:]:
+
+    for copy in copies[2:]:
         copy.wait()
     picked = nn(volume[...].reshape(channels * planes * width, depth), select).astype(BF16)
     grouped = []
@@ -90,7 +89,6 @@
         own[x] = plane
         if x > 0:
             slab_x[x - 1] = plane
-    copies[2].wait()
 
 
 def border_kernel(slab_x, own, border):
@@ -331,16 +329,15 @@
         out_shape=[
             jax.ShapeDtypeStruct((planes, 16 * width, LANES), BF16),
             jax.ShapeDtypeStruct((planes - 1, 16 * width, LANES), BF16),
-            jax.ShapeDtypeStruct((filts, 11, 16, LANES), BF16),
+            pltpu.VMEM((filts, 11, 16, LANES), BF16),
         ],
         in_specs=[pl.BlockSpec(memory_space=pltpu.HBM)] * 3,
-        out_specs=whole(2) + [pl.BlockSpec(memory_space=pl.ANY)],
+        out_specs=whole(3),
         scratch_shapes=[
             pltpu.VMEM(volume.shape, BF16),
             pltpu.VMEM((27, 16, 32), BF16),
             pltpu.VMEM((16, 16, LANES), BF16),
-            pltpu.VMEM((filts, 11, 16, LANES), BF16),
-            pltpu.SemaphoreType.DMA((3 + channels,)),
+            pltpu.SemaphoreType.DMA((2 + channels,)),
         ],
         compiler_params=limit,
         name="regroup",

time: 41.3 us -> 41.4 us (level)
  no operation moved by 1% of the time
where the time goes in v14:
time: 41.4 us; the launch traced here: 41 us
  blocking collectives  21.4 us (52%)
  starting transfers between devices  11.7 us (28%)
  Pallas kernels  6.49 us (16%)
  between operations  0.72 us (2%)
  waiting for transfers between devices  0.6 us (1%)
    all_to_all x1, blocking collectives, exchange(): lax.all_to_all(chunks, 'filt', 0, 0, axis_index_groups=groups, tiled=True)  11.1 us
    all_gather x1, blocking collectives, body(): sums = lax.all_gather(sums, 'space')  10.3 us
    all_to_all x1, starting transfers between devices, exchange(): lax.all_to_all(chunks, 'filt', 0, 0, axis_index_groups=groups, tiled=True)  6.76 us
    ppermute x1, starting transfers between devices, body(): border = lax.ppermute(border, 'filt', [(f - 1, f) for f in range(1, filts)])  2.6 us
    ppermute x1, starting transfers between devices, body(): lax.ppermute(slab_x, 'space', [(s - 1, s) for s in range(1, spaces)])  2.37 us
    pallas_call x1, Pallas kernels, body(): pl.pallas_call(regroup_kernel, out_shape=[jax.ShapeDtypeStruct((planes, 1...  1.93 us
    pallas_call x1, Pallas kernels, body(): pl.pallas_call(lower_kernel, out_shape=jax.ShapeDtypeStruct((filts, 13, 1...  1.4 us
    pallas_call x1, Pallas kernels, body(): pl.pallas_call(upper_kernel, out_shape=[jax.ShapeDtypeStruct((64, 3 * LAN...  1.36 us
  transfers between devices with their start and end apart: 3, of which 2 were waited for; matrix products, arithmetic and copies ran while one was open for 0% of the time, Pallas kernels for 5%

profile of v14, /device:TPU:0, one launch (start us, length us, event | category | flops | bytes accessed | tf_op | source)
XLA Modules:
  0.0 41.0 jit_solution(3453146088298159123)
XLA Ops:
  0.6 1.9 %regroup.1 = (bf16[4,256,128]{2,1,0:T(8,128)(2,1)S(1)}, bf16[3,256,128]{2,1,0:T(8,128)(2,1)S(1)}, bf16[4,11,16,128]{3,2,1,0:T(8,128)(2,1)}) custom-call(bf16[4,4,16,512]{3,2,1,0:T(8,128)(2,1)} %volume_in.1, bf16[27,16,32]{2,1,0:T(8,128)(2,1)} %bitcast.9, bf16[16,16,128]{2,1,0:T(8,128)(2,1)} %bitcast.10), custom_call_target="tpu_custom_call" | custom-call | tf_op jit(solution)/shard_map/regroup/pallas_call | solution.py:327
  2.6 2.4 %collective-permute-start = (bf16[3,256,128]{2,1,0:T(8,128)(2,1)S(1)}, bf16[3,256,128]{2,1,0:T(8,128)(2,1)S(1)}, u32[]{:S(2)}, u32[]{:S(2)}) collective-permute-start(bf16[3,256,128]{2,1,0:T(8,128)(2,1)S(1)} %get-tuple-element.21), channel_id=1, source_target_pairs={{0,4},{4,8},{8,12},{12,16},{16,20},{20,24},{24,28},{1,5},{5,9},{9,... | collective-permute-start | bytes 589832 | tf_op jit(solution)/shard_map/ppermute | solution.py:345
  4.9 6.8 %all-to-all-start = ((bf16[4,11,16,128]{3,2,1,0:T(8,128)(2,1)}), bf16[4,11,16,128]{3,2,1,0:T(8,128)(2,1)S(1)}, u32[]{:S(2)}, u32[]{:S(2)}) async-start(bf16[4,11,16,128]{3,2,1,0:T(8,128)(2,1)} %get-tuple-element.22), calls=%async_computation | async-start | bytes 360448 | tf_op jit(solution)/shard_map/all_to_all | solution.py:312
  11.7 0.0 collective-permute-done.slab_x
  11.7 0.0 copy-start.1
  11.7 0.0 copy-start
  11.7 2.6 %collective-permute-start.1 = (bf16[7,48,128]{2,1,0:T(8,128)(2,1)S(1)}, bf16[7,48,128]{2,1,0:T(8,128)(2,1)S(1)}, u32[]{:S(2)}, u32[]{:S(2)}) collective-permute-start(bf16[7,48,128]{2,1,0:T(8,128)(2,1)S(1)} %border.1), channel_id=1, source_target_pairs={{0,1},{1,2},{2,3},{4,5},{5,6},{6,7},{8,9},{9,10},{10,11},{12,13},{... | collective-permute-start | bytes 258056 | tf_op jit(solution)/shard_map/ppermute | solution.py:355
  14.3 0.0 copy-done.1
  14.4 0.1 copy.12
  14.5 0.0 copy-done
  14.5 0.8 %stem_inner.1 = (bf16[96,144]{1,0:T(8,128)(2,1)S(1)}, bf16[7,48,896]{2,1,0:T(8,128)(2,1)S(1)}, f32[3,64,896]{2,1,0:T(8,128)S(1)}, bf16[864,384]{1,0:T(8,128)(2,1)S(1)}, bf16[3,96,128]{2,1,0:T(8,128)(2,1)S(1)}) custom-call(bf16[4,256,128]{2,1,0:T(8,128)(2,1)S(1)} %get-tuple-element.20.own, bf16[3,256,128]{2,1,0:T(8,128)(2,1)S(1)} %collective-permute-done.slab_x, ...), custom_call_target="tpu_custom_call" | custom-call | flops 200000000 | bytes 4000000 | tf_op jit(solution)/shard_map/stem_inner/pallas_call | solution.py:359
  15.3 0.2 all-to-all-done.gathered
  15.5 1.4 %upper_cells.1 = (bf16[64,384]{1,0:T(8,128)(2,1)S(1)}, f32[64,864]{1,0:T(8,128)S(1)}, f32[96,144]{1,0:T(8,128)S(1)}, bf16[64,896]{1,0:T(8,128)(2,1)S(1)}, bf16[1...) custom-call(bf16[4,11,16,128]{3,2,1,0:T(8,128)(2,1)S(1)} %all-to-all-done.gathered, ...), custom_call_target="tpu_custom_call" | custom-call | tf_op jit(solution)/shard_map/upper_cells/pallas_call | solution.py:374
  16.9 0.4 collective-permute-done.1.border
  17.3 1.4 %lower_cells.1 = bf16[4,13,16,128]{3,2,1,0:T(8,128)(2,1)S(1)} custom-call(bf16[4,256,128]{2,1,0:T(8,128)(2,1)S(1)} %get-tuple-element.20.own, bf16[3,256,128]{2,1,0:T(8,128)(2,1)S(1)} %collective-permute-done.slab_x, bf16[7,48,128]{2,1,0:T(8,128)(2,1)S(1)} %collective-permute-done.1.border, bf16[3,128,144]{2,1,0:T(8,128)(2,1)S(1)} %copy-done, ...), custom_call_target="tpu_custom_call" | custom-call | flops 600000000 | bytes 8000000 | tf_op jit(solution)/shard_map/lower_cells/pallas_call | solution.py:390
  18.7 11.1 %all_to_all.10.parts = bf16[4,13,16,128]{3,2,1,0:T(8,128)(2,1)S(1)} all-to-all(bf16[4,13,16,128]{3,2,1,0:T(8,128)(2,1)S(1)} %lower_cells.1), channel_id=1, replica_groups={{2,1,3,0},{6,5,7,4},{10,9,11,8},{14,13,15,12},{18,17,19,16},{22,21,23,2..., dimensions={0} | all-to-all | bytes 425984 | tf_op jit(solution)/shard_map/all_to_all | solution.py:312
  29.8 10.3 %all-gather = bf16[72,16,128]{2,1,0:T(8,128)(2,1)S(1)} all-gather(bf16[9,16,128]{2,1,0:T(8,128)(2,1)S(1)} %sums.1), channel_id=2, replica_groups=mesh['space'=8,'filt'=4] {'space'}, dimensions={0}, use_global_device_ids=true | all-gather | bytes 331776 | tf_op jit(solution)/shard_map/all_gather | solution.py:414
  40.1 0.9 %unpack.1 = (bf16[16,16,128]{2,1,0:T(8,128)(2,1)}, f32[27,16,32]{2,1,0:T(8,128)}, f32[27,4,32]{2,1,0:T(4,128)}) custom-call(bf16[8,9,16,128]{3,2,1,0:T(8,128)(2,1)S(1)} %bitcast.8, bf16[4,13,16,128]{3,2,1,0:T(8,128)(2,1)S(1)} %all_to_all.10.parts), custom_call_target="tpu_custom_call" | custom-call | tf_op jit(solution)/shard_map/unpack/pallas_call | solution.py:415
  (4 shorter events, 0.1 us)
Async XLA Ops:
  2.6 9.1 %collective-permute-start = (bf16[3,256,128]{2,1,0:T(8,128)(2,1)S(1)}, bf16[3,256,128]{2,1,0:T(8,128)(2,1)S(1)}, u32[]{:S(2)}, u32[]{:S(2)}) collective-permute-start(bf16[3,256,128]{2,1,0:T(8,128)(2,1)S(1)} %get-tuple-element.21), channel_id=1, source_target_pairs={{0,4},{4,8},{8,12},{12,16},{16,20},{20,24},{24,28},{1,5},{5,9},{9,... | collective-permute-start | bytes 589832 | tf_op jit(solution)/shard_map/ppermute | solution.py:345
  4.9 10.6 %all-to-all-start = ((bf16[4,11,16,128]{3,2,1,0:T(8,128)(2,1)}), bf16[4,11,16,128]{3,2,1,0:T(8,128)(2,1)S(1)}, u32[]{:S(2)}, u32[]{:S(2)}) async-start(bf16[4,11,16,128]{3,2,1,0:T(8,128)(2,1)} %get-tuple-element.22), calls=%async_computation | async-start | bytes 360448 | tf_op jit(solution)/shard_map/all_to_all | solution.py:312
  11.7 2.6 %copy-start.1 = (bf16[27,4,32]{2,1,0:T(4,128)(2,1)S(1)}, bf16[27,4,32]{2,1,0:T(4,128)(2,1)}, u32[]{:S(2)}) copy-start(bf16[27,4,32]{2,1,0:T(4,128)(2,1)} %param.6) | copy-start | bytes 20740
  11.7 2.8 %copy-start = (bf16[3,128,144]{2,1,0:T(8,128)(2,1)S(1)}, bf16[3,128,144]{2,1,0:T(8,128)(2,1)}, u32[]{:S(2)}) copy-start(bf16[3,128,144]{2,1,0:T(8,128)(2,1)} %constant.5.clone.place) | copy-start | bytes 331780
  11.7 5.6 %collective-permute-start.1 = (bf16[7,48,128]{2,1,0:T(8,128)(2,1)S(1)}, bf16[7,48,128]{2,1,0:T(8,128)(2,1)S(1)}, u32[]{:S(2)}, u32[]{:S(2)}) collective-permute-start(bf16[7,48,128]{2,1,0:T(8,128)(2,1)S(1)} %border.1), channel_id=1, source_target_pairs={{0,1},{1,2},{2,3},{4,5},{5,6},{6,7},{8,9},{9,10},{10,11},{12,13},{... | collective-permute-start | bytes 258056 | tf_op jit(solution)/shard_map/ppermute | solution.py:355

commit v15 on v14

--- a/solution.py
+++ b/solution.py
@@ -274,7 +274,9 @@
 
 
 def sum_kernel(parts, sums):
-    sums[...] = jnp.sum(parts[:, 0:9].astype(F32), axis=0).astype(BF16)
+    total = jnp.sum(parts[:, 0:9].astype(F32), axis=0).astype(BF16)
+    for s in range(sums.shape[0]):
+        sums[s] = total
 
 
 def unpack_kernel(
@@ -405,13 +407,14 @@
     parts = exchange(parts)
     sums = pl.pallas_call(
         sum_kernel,
-        out_shape=jax.ShapeDtypeStruct((9, 16, LANES), BF16),
+        out_shape=jax.ShapeDtypeStruct((spaces, 9, 16, LANES), BF16),
         in_specs=whole(1),
         out_specs=whole(1)[0],
         compiler_params=limit,
         name="sums",
     )(parts)
-    sums = lax.all_gather(sums, "space")
+    around = [(s + 2) % spaces for s in range(spaces)]
+    sums = lax.all_to_all(sums, "space", 0, 0, axis_index_groups=[around], tiled=True)
     features, middle, stem = pl.pallas_call(
         functools.partial(unpack_kernel, middle_cells**-0.5, stem_cells**-0.5),
         out_shape=[

time: 41.4 us -> 41.7 us (level)
    all_to_all x0 -> x1, blocking collectives: none -> 10.6 us  [body(): lax.all_to_all(sums, 'space', 0, 0, axis_index_groups=[around], tiled=True)]
    all_gather x1 -> x0, blocking collectives: 10.3 us -> none  [body(): sums = lax.all_gather(sums, 'space')]
where the time goes in v15:
time: 41.7 us; the launch traced here: 41.3 us
  blocking collectives  21.6 us (52%)
  starting transfers between devices  11.7 us (28%)
  Pallas kernels  6.5 us (16%)
  between operations  0.72 us (2%)
  waiting for transfers between devices  0.6 us (1%)
    all_to_all x1, blocking collectives, exchange(): lax.all_to_all(chunks, 'filt', 0, 0, axis_index_groups=groups, tiled=True)  11.1 us
    all_to_all x1, blocking collectives, body(): lax.all_to_all(sums, 'space', 0, 0, axis_index_groups=[around], tiled=True)  10.6 us
    all_to_all x1, starting transfers between devices, exchange(): lax.all_to_all(chunks, 'filt', 0, 0, axis_index_groups=groups, tiled=True)  6.76 us
    ppermute x1, starting transfers between devices, body(): border = lax.ppermute(border, 'filt', [(f - 1, f) for f in range(1, filts)])  2.6 us
    ppermute x1, starting transfers between devices, body(): lax.ppermute(slab_x, 'space', [(s - 1, s) for s in range(1, spaces)])  2.37 us
    pallas_call x1, Pallas kernels, body(): pl.pallas_call(regroup_kernel, out_shape=[jax.ShapeDtypeStruct((planes, 1...  1.93 us
    pallas_call x1, Pallas kernels, body(): pl.pallas_call(lower_kernel, out_shape=jax.ShapeDtypeStruct((filts, 13, 1...  1.4 us
    pallas_call x1, Pallas kernels, body(): pl.pallas_call(upper_kernel, out_shape=[jax.ShapeDtypeStruct((64, 3 * LAN...  1.36 us
  transfers between devices with their start and end apart: 3, of which 2 were waited for; matrix products, arithmetic and copies ran while one was open for 0% of the time, Pallas kernels for 5%

profile of v15, /device:TPU:0, one launch (start us, length us, event | category | flops | bytes accessed | tf_op | source)
XLA Modules:
  0.0 41.3 jit_solution(14590259980794271392)
XLA Ops:
  0.6 1.9 %regroup.1 = (bf16[4,256,128]{2,1,0:T(8,128)(2,1)S(1)}, bf16[3,256,128]{2,1,0:T(8,128)(2,1)S(1)}, bf16[4,11,16,128]{3,2,1,0:T(8,128)(2,1)}) custom-call(bf16[4,4,16,512]{3,2,1,0:T(8,128)(2,1)} %volume_in.1, bf16[27,16,32]{2,1,0:T(8,128)(2,1)} %bitcast.7, bf16[16,16,128]{2,1,0:T(8,128)(2,1)} %bitcast.8), custom_call_target="tpu_custom_call" | custom-call | tf_op jit(solution)/shard_map/regroup/pallas_call | solution.py:329
  2.6 2.4 %collective-permute-start = (bf16[3,256,128]{2,1,0:T(8,128)(2,1)S(1)}, bf16[3,256,128]{2,1,0:T(8,128)(2,1)S(1)}, u32[]{:S(2)}, u32[]{:S(2)}) collective-permute-start(bf16[3,256,128]{2,1,0:T(8,128)(2,1)S(1)} %get-tuple-element.21), channel_id=1, source_target_pairs={{0,4},{4,8},{8,12},{12,16},{16,20},{20,24},{24,28},{1,5},{5,9},{9,... | collective-permute-start | bytes 589832 | tf_op jit(solution)/shard_map/ppermute | solution.py:347
  4.9 6.8 %all-to-all-start = ((bf16[4,11,16,128]{3,2,1,0:T(8,128)(2,1)}), bf16[4,11,16,128]{3,2,1,0:T(8,128)(2,1)S(1)}, u32[]{:S(2)}, u32[]{:S(2)}) async-start(bf16[4,11,16,128]{3,2,1,0:T(8,128)(2,1)} %get-tuple-element.22), calls=%async_computation | async-start | bytes 360448 | tf_op jit(solution)/shard_map/all_to_all | solution.py:314
  11.7 0.0 collective-permute-done.slab_x
  11.7 0.0 copy-start.1
  11.7 0.0 copy-start
  11.7 2.6 %collective-permute-start.1 = (bf16[7,48,128]{2,1,0:T(8,128)(2,1)S(1)}, bf16[7,48,128]{2,1,0:T(8,128)(2,1)S(1)}, u32[]{:S(2)}, u32[]{:S(2)}) collective-permute-start(bf16[7,48,128]{2,1,0:T(8,128)(2,1)S(1)} %border.1), channel_id=1, source_target_pairs={{0,1},{1,2},{2,3},{4,5},{5,6},{6,7},{8,9},{9,10},{10,11},{12,13},{... | collective-permute-start | bytes 258056 | tf_op jit(solution)/shard_map/ppermute | solution.py:357
  14.3 0.0 copy-done.1
  14.4 0.1 copy.10
  14.5 0.0 copy-done
  14.5 0.8 %stem_inner.1 = (bf16[96,144]{1,0:T(8,128)(2,1)S(1)}, bf16[7,48,896]{2,1,0:T(8,128)(2,1)S(1)}, f32[3,64,896]{2,1,0:T(8,128)S(1)}, bf16[864,384]{1,0:T(8,128)(2,1)S(1)}, bf16[3,96,128]{2,1,0:T(8,128)(2,1)S(1)}) custom-call(bf16[4,256,128]{2,1,0:T(8,128)(2,1)S(1)} %get-tuple-element.20.own, bf16[3,256,128]{2,1,0:T(8,128)(2,1)S(1)} %collective-permute-done.slab_x, ...), custom_call_target="tpu_custom_call" | custom-call | flops 200000000 | bytes 4000000 | tf_op jit(solution)/shard_map/stem_inner/pallas_call | solution.py:361
  15.3 0.2 all-to-all-done.gathered
  15.5 1.4 %upper_cells.1 = (bf16[64,384]{1,0:T(8,128)(2,1)S(1)}, f32[64,864]{1,0:T(8,128)S(1)}, f32[96,144]{1,0:T(8,128)S(1)}, bf16[64,896]{1,0:T(8,128)(2,1)S(1)}, bf16[1...) custom-call(bf16[4,11,16,128]{3,2,1,0:T(8,128)(2,1)S(1)} %all-to-all-done.gathered, ...), custom_call_target="tpu_custom_call" | custom-call | tf_op jit(solution)/shard_map/upper_cells/pallas_call | solution.py:376
  16.9 0.4 collective-permute-done.1.border
  17.3 1.4 %lower_cells.1 = bf16[4,13,16,128]{3,2,1,0:T(8,128)(2,1)S(1)} custom-call(bf16[4,256,128]{2,1,0:T(8,128)(2,1)S(1)} %get-tuple-element.20.own, bf16[3,256,128]{2,1,0:T(8,128)(2,1)S(1)} %collective-permute-done.slab_x, bf16[7,48,128]{2,1,0:T(8,128)(2,1)S(1)} %collective-permute-done.1.border, bf16[3,128,144]{2,1,0:T(8,128)(2,1)S(1)} %copy-done, ...), custom_call_target="tpu_custom_call" | custom-call | flops 600000000 | bytes 8000000 | tf_op jit(solution)/shard_map/lower_cells/pallas_call | solution.py:392
  18.7 11.1 %all_to_all.15.parts = bf16[4,13,16,128]{3,2,1,0:T(8,128)(2,1)S(1)} all-to-all(bf16[4,13,16,128]{3,2,1,0:T(8,128)(2,1)S(1)} %lower_cells.1), channel_id=1, replica_groups={{2,1,3,0},{6,5,7,4},{10,9,11,8},{14,13,15,12},{18,17,19,16},{22,21,23,2..., dimensions={0} | all-to-all | bytes 425984 | tf_op jit(solution)/shard_map/all_to_all | solution.py:314
  29.8 10.6 %all_to_all.16.sums = bf16[8,9,16,128]{3,2,1,0:T(8,128)(2,1)S(1)} all-to-all(bf16[8,9,16,128]{3,2,1,0:T(8,128)(2,1)S(1)} %sums.1), channel_id=1, replica_groups={{8,12,16,20,24,28,0,4},{9,13,17,21,25,29,1,5},{10,14,18,22,26,30,2,6},{..., dimensions={0} | all-to-all | bytes 589824 | tf_op jit(solution)/shard_map/all_to_all | solution.py:417
  40.4 0.9 %unpack.1 = (bf16[16,16,128]{2,1,0:T(8,128)(2,1)}, f32[27,16,32]{2,1,0:T(8,128)}, f32[27,4,32]{2,1,0:T(4,128)}) custom-call(bf16[8,9,16,128]{3,2,1,0:T(8,128)(2,1)S(1)} %all_to_all.16.sums, bf16[4,13,16,128]{3,2,1,0:T(8,128)(2,1)S(1)} %all_to_all.15.parts), custom_call_target="tpu_custom_call" | custom-call | tf_op jit(solution)/shard_map/unpack/pallas_call | solution.py:418
  (4 shorter events, 0.1 us)
Async XLA Ops:
  2.6 9.1 %collective-permute-start = (bf16[3,256,128]{2,1,0:T(8,128)(2,1)S(1)}, bf16[3,256,128]{2,1,0:T(8,128)(2,1)S(1)}, u32[]{:S(2)}, u32[]{:S(2)}) collective-permute-start(bf16[3,256,128]{2,1,0:T(8,128)(2,1)S(1)} %get-tuple-element.21), channel_id=1, source_target_pairs={{0,4},{4,8},{8,12},{12,16},{16,20},{20,24},{24,28},{1,5},{5,9},{9,... | collective-permute-start | bytes 589832 | tf_op jit(solution)/shard_map/ppermute | solution.py:347
  4.9 10.6 %all-to-all-start = ((bf16[4,11,16,128]{3,2,1,0:T(8,128)(2,1)}), bf16[4,11,16,128]{3,2,1,0:T(8,128)(2,1)S(1)}, u32[]{:S(2)}, u32[]{:S(2)}) async-start(bf16[4,11,16,128]{3,2,1,0:T(8,128)(2,1)} %get-tuple-element.22), calls=%async_computation | async-start | bytes 360448 | tf_op jit(solution)/shard_map/all_to_all | solution.py:314
  11.7 2.6 %copy-start.1 = (bf16[27,4,32]{2,1,0:T(4,128)(2,1)S(1)}, bf16[27,4,32]{2,1,0:T(4,128)(2,1)}, u32[]{:S(2)}) copy-start(bf16[27,4,32]{2,1,0:T(4,128)(2,1)} %param.6) | copy-start | bytes 20740
  11.7 2.8 %copy-start = (bf16[3,128,144]{2,1,0:T(8,128)(2,1)S(1)}, bf16[3,128,144]{2,1,0:T(8,128)(2,1)}, u32[]{:S(2)}) copy-start(bf16[3,128,144]{2,1,0:T(8,128)(2,1)} %constant.5.clone.place) | copy-start | bytes 331780
  11.7 5.6 %collective-permute-start.1 = (bf16[7,48,128]{2,1,0:T(8,128)(2,1)S(1)}, bf16[7,48,128]{2,1,0:T(8,128)(2,1)S(1)}, u32[]{:S(2)}, u32[]{:S(2)}) collective-permute-start(bf16[7,48,128]{2,1,0:T(8,128)(2,1)S(1)} %border.1), channel_id=1, source_target_pairs={{0,1},{1,2},{2,3},{4,5},{5,6},{6,7},{8,9},{9,10},{10,11},{12,13},{... | collective-permute-start | bytes 258056 | tf_op jit(solution)/shard_map/ppermute | solution.py:357

commit v16 on v14

--- a/solution.py
+++ b/solution.py
@@ -262,7 +262,7 @@
 
     middle = (mid_grad + upper_mid[...]).astype(BF16)
     middle = jnp.concatenate([middle, jnp.zeros((blocks * 16, 32), BF16)], axis=1)
-    for k, f in enumerate(order):
+    for k, f in enumerate(return_order(blocks)):
         rows = slice(16 * f, 16 * f + 16)
         for t in range(7):
             parts[k, t] = middle[rows, t * LANES : (t + 1) * LANES]
@@ -291,7 +291,7 @@
         start = 32 * (t % 4)
         middle[t] = total[t // 4, :, start : start + 32] * middle_scale
     copies[0].start()
-    order = exchange_order(parts.shape[0])
+    order = return_order(parts.shape[0])
     rows = [parts[order.index(f), 9 + j] for f in range(parts.shape[0]) for j in range(4)]
     features[...] = nn(turn_matrix(), jnp.concatenate(rows, axis=0)).astype(BF16).reshape(16, 16, LANES)
     copies[2].start()
@@ -307,9 +307,13 @@
     return sorted(range(filts), key=lambda f: (abs(f - filts // 2), f))
 
 
-def exchange(chunks):
-    groups = [exchange_order(lax.axis_size("filt"))]
-    return lax.all_to_all(chunks, "filt", 0, 0, axis_index_groups=groups, tiled=True)
+def return_order(filts):
+    middle = filts // 2
+    return [middle] + [f for f in range(filts) if f != middle]
+
+
+def exchange(chunks, order):
+    return lax.all_to_all(chunks, "filt", 0, 0, axis_index_groups=[order], tiled=True)
 
 
 def whole(count):
@@ -343,7 +347,7 @@
         name="regroup",
     )(*[pltpu.with_memory_space_constraint(x, pltpu.HBM) for x in raw])
     slab_x = lax.ppermute(slab_x, "space", [(s - 1, s) for s in range(1, spaces)])
-    gathered = exchange(packed)
+    gathered = exchange(packed, exchange_order(filts))
     border = pl.pallas_call(
         border_kernel,
         out_shape=jax.ShapeDtypeStruct((7, 48, LANES), BF16),
@@ -402,7 +406,7 @@
         name="lower_cells",
     )(own, slab_x, border, place, gathered, weights, cols, slope, near_taps, *upper)
 
-    parts = exchange(parts)
+    parts = exchange(parts, return_order(filts))
     sums = pl.pallas_call(
         sum_kernel,
         out_shape=jax.ShapeDtypeStruct((9, 16, LANES), BF16),

time: 41.4 us -> 41.4 us (level)
    all_to_all x1, blocking collectives: 11.1 us -> 12 us  [exchange(): lax.all_to_all(chunks, 'filt', 0, 0, axis_index_groups=[order], tiled=True)]
    all_gather x1, blocking collectives: 10.3 us -> 9.44 us  [body(): sums = lax.all_gather(sums, 'space')]
where the time goes in v16:
time: 41.4 us; the launch traced here: 41.1 us
  blocking collectives  21.4 us (52%)
  starting transfers between devices  11.7 us (28%)
  Pallas kernels  6.49 us (16%)
  between operations  0.72 us (2%)
  waiting for transfers between devices  0.6 us (1%)
    all_to_all x1, blocking collectives, exchange(): lax.all_to_all(chunks, 'filt', 0, 0, axis_index_groups=[order], tiled=True)  12 us
    all_gather x1, blocking collectives, body(): sums = lax.all_gather(sums, 'space')  9.44 us
    all_to_all x1, starting transfers between devices, exchange(): lax.all_to_all(chunks, 'filt', 0, 0, axis_index_groups=[order], tiled=True)  6.76 us
    ppermute x1, starting transfers between devices, body(): border = lax.ppermute(border, 'filt', [(f - 1, f) for f in range(1, filts)])  2.6 us
    ppermute x1, starting transfers between devices, body(): lax.ppermute(slab_x, 'space', [(s - 1, s) for s in range(1, spaces)])  2.37 us
    pallas_call x1, Pallas kernels, body(): pl.pallas_call(regroup_kernel, out_shape=[jax.ShapeDtypeStruct((planes, 1...  1.93 us
    pallas_call x1, Pallas kernels, body(): pl.pallas_call(lower_kernel, out_shape=jax.ShapeDtypeStruct((filts, 13, 1...  1.4 us
    pallas_call x1, Pallas kernels, body(): pl.pallas_call(upper_kernel, out_shape=[jax.ShapeDtypeStruct((64, 3 * LAN...  1.36 us
  transfers between devices with their start and end apart: 3, of which 2 were waited for; matrix products, arithmetic and copies ran while one was open for 0% of the time, Pallas kernels for 5%

profile of v16, /device:TPU:0, one launch (start us, length us, event | category | flops | bytes accessed | tf_op | source)
XLA Modules:
  0.0 41.1 jit_solution(3259700181784905634)
XLA Ops:
  0.6 1.9 %regroup.1 = (bf16[4,256,128]{2,1,0:T(8,128)(2,1)S(1)}, bf16[3,256,128]{2,1,0:T(8,128)(2,1)S(1)}, bf16[4,11,16,128]{3,2,1,0:T(8,128)(2,1)}) custom-call(bf16[4,4,16,512]{3,2,1,0:T(8,128)(2,1)} %volume_in.1, bf16[27,16,32]{2,1,0:T(8,128)(2,1)} %bitcast.9, bf16[16,16,128]{2,1,0:T(8,128)(2,1)} %bitcast.10), custom_call_target="tpu_custom_call" | custom-call | tf_op jit(solution)/shard_map/regroup/pallas_call | solution.py:331
  2.6 2.4 %collective-permute-start = (bf16[3,256,128]{2,1,0:T(8,128)(2,1)S(1)}, bf16[3,256,128]{2,1,0:T(8,128)(2,1)S(1)}, u32[]{:S(2)}, u32[]{:S(2)}) collective-permute-start(bf16[3,256,128]{2,1,0:T(8,128)(2,1)S(1)} %get-tuple-element.21), channel_id=1, source_target_pairs={{0,4},{4,8},{8,12},{12,16},{16,20},{20,24},{24,28},{1,5},{5,9},{9,... | collective-permute-start | bytes 589832 | tf_op jit(solution)/shard_map/ppermute | solution.py:349
  4.9 6.8 %all-to-all-start = ((bf16[4,11,16,128]{3,2,1,0:T(8,128)(2,1)}), bf16[4,11,16,128]{3,2,1,0:T(8,128)(2,1)S(1)}, u32[]{:S(2)}, u32[]{:S(2)}) async-start(bf16[4,11,16,128]{3,2,1,0:T(8,128)(2,1)} %get-tuple-element.22), calls=%async_computation | async-start | bytes 360448 | tf_op jit(solution)/shard_map/all_to_all | solution.py:316
  11.7 0.0 collective-permute-done.slab_x
  11.7 0.0 copy-start.1
  11.7 0.0 copy-start
  11.7 2.6 %collective-permute-start.1 = (bf16[7,48,128]{2,1,0:T(8,128)(2,1)S(1)}, bf16[7,48,128]{2,1,0:T(8,128)(2,1)S(1)}, u32[]{:S(2)}, u32[]{:S(2)}) collective-permute-start(bf16[7,48,128]{2,1,0:T(8,128)(2,1)S(1)} %border.1), channel_id=1, source_target_pairs={{0,1},{1,2},{2,3},{4,5},{5,6},{6,7},{8,9},{9,10},{10,11},{12,13},{... | collective-permute-start | bytes 258056 | tf_op jit(solution)/shard_map/ppermute | solution.py:359
  14.3 0.0 copy-done.1
  14.4 0.1 copy.12
  14.5 0.0 copy-done
  14.5 0.8 %stem_inner.1 = (bf16[96,144]{1,0:T(8,128)(2,1)S(1)}, bf16[7,48,896]{2,1,0:T(8,128)(2,1)S(1)}, f32[3,64,896]{2,1,0:T(8,128)S(1)}, bf16[864,384]{1,0:T(8,128)(2,1)S(1)}, bf16[3,96,128]{2,1,0:T(8,128)(2,1)S(1)}) custom-call(bf16[4,256,128]{2,1,0:T(8,128)(2,1)S(1)} %get-tuple-element.20.own, bf16[3,256,128]{2,1,0:T(8,128)(2,1)S(1)} %collective-permute-done.slab_x, ...), custom_call_target="tpu_custom_call" | custom-call | flops 200000000 | bytes 4000000 | tf_op jit(solution)/shard_map/stem_inner/pallas_call | solution.py:363
  15.3 0.2 all-to-all-done.gathered
  15.5 1.4 %upper_cells.1 = (bf16[64,384]{1,0:T(8,128)(2,1)S(1)}, f32[64,864]{1,0:T(8,128)S(1)}, f32[96,144]{1,0:T(8,128)S(1)}, bf16[64,896]{1,0:T(8,128)(2,1)S(1)}, bf16[1...) custom-call(bf16[4,11,16,128]{3,2,1,0:T(8,128)(2,1)S(1)} %all-to-all-done.gathered, ...), custom_call_target="tpu_custom_call" | custom-call | tf_op jit(solution)/shard_map/upper_cells/pallas_call | solution.py:378
  16.9 0.4 collective-permute-done.1.border
  17.3 1.4 %lower_cells.1 = bf16[4,13,16,128]{3,2,1,0:T(8,128)(2,1)S(1)} custom-call(bf16[4,256,128]{2,1,0:T(8,128)(2,1)S(1)} %get-tuple-element.20.own, bf16[3,256,128]{2,1,0:T(8,128)(2,1)S(1)} %collective-permute-done.slab_x, bf16[7,48,128]{2,1,0:T(8,128)(2,1)S(1)} %collective-permute-done.1.border, bf16[3,128,144]{2,1,0:T(8,128)(2,1)S(1)} %copy-done, ...), custom_call_target="tpu_custom_call" | custom-call | flops 600000000 | bytes 8000000 | tf_op jit(solution)/shard_map/lower_cells/pallas_call | solution.py:394
  18.7 12.0 %all_to_all.10.parts = bf16[4,13,16,128]{3,2,1,0:T(8,128)(2,1)S(1)} all-to-all(bf16[4,13,16,128]{3,2,1,0:T(8,128)(2,1)S(1)} %lower_cells.1), channel_id=1, replica_groups={{2,0,1,3},{6,4,5,7},{10,8,9,11},{14,12,13,15},{18,16,17,19},{22,20,21,2..., dimensions={0} | all-to-all | bytes 425984 | tf_op jit(solution)/shard_map/all_to_all | solution.py:316
  30.7 9.4 %all-gather = bf16[72,16,128]{2,1,0:T(8,128)(2,1)S(1)} all-gather(bf16[9,16,128]{2,1,0:T(8,128)(2,1)S(1)} %sums.1), channel_id=2, replica_groups=mesh['space'=8,'filt'=4] {'space'}, dimensions={0}, use_global_device_ids=true | all-gather | bytes 331776 | tf_op jit(solution)/shard_map/all_gather | solution.py:418
  40.1 0.9 %unpack.1 = (bf16[16,16,128]{2,1,0:T(8,128)(2,1)}, f32[27,16,32]{2,1,0:T(8,128)}, f32[27,4,32]{2,1,0:T(4,128)}) custom-call(bf16[8,9,16,128]{3,2,1,0:T(8,128)(2,1)S(1)} %bitcast.8, bf16[4,13,16,128]{3,2,1,0:T(8,128)(2,1)S(1)} %all_to_all.10.parts), custom_call_target="tpu_custom_call" | custom-call | tf_op jit(solution)/shard_map/unpack/pallas_call | solution.py:419
  (4 shorter events, 0.1 us)
Async XLA Ops:
  2.6 9.1 %collective-permute-start = (bf16[3,256,128]{2,1,0:T(8,128)(2,1)S(1)}, bf16[3,256,128]{2,1,0:T(8,128)(2,1)S(1)}, u32[]{:S(2)}, u32[]{:S(2)}) collective-permute-start(bf16[3,256,128]{2,1,0:T(8,128)(2,1)S(1)} %get-tuple-element.21), channel_id=1, source_target_pairs={{0,4},{4,8},{8,12},{12,16},{16,20},{20,24},{24,28},{1,5},{5,9},{9,... | collective-permute-start | bytes 589832 | tf_op jit(solution)/shard_map/ppermute | solution.py:349
  4.9 10.6 %all-to-all-start = ((bf16[4,11,16,128]{3,2,1,0:T(8,128)(2,1)}), bf16[4,11,16,128]{3,2,1,0:T(8,128)(2,1)S(1)}, u32[]{:S(2)}, u32[]{:S(2)}) async-start(bf16[4,11,16,128]{3,2,1,0:T(8,128)(2,1)} %get-tuple-element.22), calls=%async_computation | async-start | bytes 360448 | tf_op jit(solution)/shard_map/all_to_all | solution.py:316
  11.7 2.6 %copy-start.1 = (bf16[27,4,32]{2,1,0:T(4,128)(2,1)S(1)}, bf16[27,4,32]{2,1,0:T(4,128)(2,1)}, u32[]{:S(2)}) copy-start(bf16[27,4,32]{2,1,0:T(4,128)(2,1)} %param.6) | copy-start | bytes 20740
  11.7 2.8 %copy-start = (bf16[3,128,144]{2,1,0:T(8,128)(2,1)S(1)}, bf16[3,128,144]{2,1,0:T(8,128)(2,1)}, u32[]{:S(2)}) copy-start(bf16[3,128,144]{2,1,0:T(8,128)(2,1)} %constant.5.clone.place) | copy-start | bytes 331780
  11.7 5.6 %collective-permute-start.1 = (bf16[7,48,128]{2,1,0:T(8,128)(2,1)S(1)}, bf16[7,48,128]{2,1,0:T(8,128)(2,1)S(1)}, u32[]{:S(2)}, u32[]{:S(2)}) collective-permute-start(bf16[7,48,128]{2,1,0:T(8,128)(2,1)S(1)} %border.1), channel_id=1, source_target_pairs={{0,1},{1,2},{2,3},{4,5},{5,6},{6,7},{8,9},{9,10},{10,11},{12,13},{... | collective-permute-start | bytes 258056 | tf_op jit(solution)/shard_map/ppermute | solution.py:359

commit v17 on v14

--- a/solution.py
+++ b/solution.py
@@ -58,22 +58,9 @@
     select = (z == source).astype(F32).astype(BF16)
     turn = turn_matrix()
 
-    blank = jnp.zeros((16, 32), BF16)
-    copies[0].wait()
-    taps = [weight[t] if t < 27 else blank for t in range(28)]
-    for t in range(7):
-        tile = jnp.concatenate(taps[4 * t : 4 * t + 4], axis=1)
-        for f in range(packed.shape[0]):
-            packed[f, t] = tile
-    copies[1].wait()
-    turned = nn(turn, cotangent[...].reshape(256, LANES)).astype(BF16)
-    for k, f in enumerate(exchange_order(packed.shape[0])):
-        for j in range(4):
-            row = 16 * (4 * f + j)
-            packed[k, 7 + j] = turned[row : row + 16]
-
-    for copy in copies[2:]:
+    for copy in copies:
         copy.wait()
+
     picked = nn(volume[...].reshape(channels * planes * width, depth), select).astype(BF16)
     grouped = []
     for x in range(planes):
@@ -83,12 +70,23 @@
                 start = (c * planes + x) * width
                 parts.append(picked[start : start + width, phase * LANES : (phase + 1) * LANES])
         grouped.append(jnp.concatenate(parts, axis=0))
+    grouped.append(cotangent[...].reshape(256, LANES))
     turned = nn(turn, jnp.concatenate(grouped, axis=1)).astype(BF16)
     for x in range(planes):
         plane = turned[:, x * LANES : (x + 1) * LANES]
         own[x] = plane
         if x > 0:
             slab_x[x - 1] = plane
+    blank = jnp.zeros((16, 32), BF16)
+    taps = [weight[t] if t < 27 else blank for t in range(28)]
+    for t in range(7):
+        tile = jnp.concatenate(taps[4 * t : 4 * t + 4], axis=1)
+        for f in range(packed.shape[0]):
+            packed[f, t] = tile
+    for k, f in enumerate(exchange_order(packed.shape[0])):
+        for j in range(4):
+            row = 16 * (4 * f + j)
+            packed[k, 7 + j] = turned[row : row + 16, planes * LANES :]
 
 
 def border_kernel(slab_x, own, border):

time: 41.4 us -> 41.8 us (level)
  no operation moved by 1% of the time
where the time goes in v17:
time: 41.8 us; the launch traced here: 41.4 us
  blocking collectives  21.4 us (51%)
  starting transfers between devices  11.7 us (28%)
  Pallas kernels  6.9 us (17%)
  between operations  0.72 us (2%)
  waiting for transfers between devices  0.6 us (1%)
    all_to_all x1, blocking collectives, exchange(): lax.all_to_all(chunks, 'filt', 0, 0, axis_index_groups=groups, tiled=True)  11 us
    all_gather x1, blocking collectives, body(): sums = lax.all_gather(sums, 'space')  10.4 us
    all_to_all x1, starting transfers between devices, exchange(): lax.all_to_all(chunks, 'filt', 0, 0, axis_index_groups=groups, tiled=True)  6.76 us
    ppermute x1, starting transfers between devices, body(): border = lax.ppermute(border, 'filt', [(f - 1, f) for f in range(1, filts)])  2.6 us
    ppermute x1, starting transfers between devices, body(): lax.ppermute(slab_x, 'space', [(s - 1, s) for s in range(1, spaces)])  2.37 us
    pallas_call x1, Pallas kernels, body(): pl.pallas_call(regroup_kernel, out_shape=[jax.ShapeDtypeStruct((planes, 1...  2.34 us
    pallas_call x1, Pallas kernels, body(): pl.pallas_call(lower_kernel, out_shape=jax.ShapeDtypeStruct((filts, 13, 1...  1.4 us
    pallas_call x1, Pallas kernels, body(): pl.pallas_call(upper_kernel, out_shape=[jax.ShapeDtypeStruct((64, 3 * LAN...  1.36 us
  transfers between devices with their start and end apart: 3, of which 2 were waited for; matrix products, arithmetic and copies ran while one was open for 0% of the time, Pallas kernels for 5%

profile of v17, /device:TPU:0, one launch (start us, length us, event | category | flops | bytes accessed | tf_op | source)
XLA Modules:
  0.0 41.4 jit_solution(5800803664670980263)
XLA Ops:
  0.6 2.3 %regroup.1 = (bf16[4,256,128]{2,1,0:T(8,128)(2,1)S(1)}, bf16[3,256,128]{2,1,0:T(8,128)(2,1)S(1)}, bf16[4,11,16,128]{3,2,1,0:T(8,128)(2,1)}) custom-call(bf16[4,4,16,512]{3,2,1,0:T(8,128)(2,1)} %volume_in.1, bf16[27,16,32]{2,1,0:T(8,128)(2,1)} %bitcast.9, bf16[16,16,128]{2,1,0:T(8,128)(2,1)} %bitcast.10), custom_call_target="tpu_custom_call" | custom-call | tf_op jit(solution)/shard_map/regroup/pallas_call | solution.py:325
  3.0 2.4 %collective-permute-start = (bf16[3,256,128]{2,1,0:T(8,128)(2,1)S(1)}, bf16[3,256,128]{2,1,0:T(8,128)(2,1)S(1)}, u32[]{:S(2)}, u32[]{:S(2)}) collective-permute-start(bf16[3,256,128]{2,1,0:T(8,128)(2,1)S(1)} %get-tuple-element.21), channel_id=1, source_target_pairs={{0,4},{4,8},{8,12},{12,16},{16,20},{20,24},{24,28},{1,5},{5,9},{9,... | collective-permute-start | bytes 589832 | tf_op jit(solution)/shard_map/ppermute | solution.py:343
  5.3 6.8 %all-to-all-start = ((bf16[4,11,16,128]{3,2,1,0:T(8,128)(2,1)}), bf16[4,11,16,128]{3,2,1,0:T(8,128)(2,1)S(1)}, u32[]{:S(2)}, u32[]{:S(2)}) async-start(bf16[4,11,16,128]{3,2,1,0:T(8,128)(2,1)} %get-tuple-element.22), calls=%async_computation | async-start | bytes 360448 | tf_op jit(solution)/shard_map/all_to_all | solution.py:310
  12.1 0.0 collective-permute-done.slab_x
  12.1 0.0 copy-start.1
  12.1 0.0 copy-start
  12.1 2.6 %collective-permute-start.1 = (bf16[7,48,128]{2,1,0:T(8,128)(2,1)S(1)}, bf16[7,48,128]{2,1,0:T(8,128)(2,1)S(1)}, u32[]{:S(2)}, u32[]{:S(2)}) collective-permute-start(bf16[7,48,128]{2,1,0:T(8,128)(2,1)S(1)} %border.1), channel_id=1, source_target_pairs={{0,1},{1,2},{2,3},{4,5},{5,6},{6,7},{8,9},{9,10},{10,11},{12,13},{... | collective-permute-start | bytes 258056 | tf_op jit(solution)/shard_map/ppermute | solution.py:353
  14.7 0.0 copy-done.1
  14.8 0.1 copy.12
  14.9 0.0 copy-done
  14.9 0.8 %stem_inner.1 = (bf16[96,144]{1,0:T(8,128)(2,1)S(1)}, bf16[7,48,896]{2,1,0:T(8,128)(2,1)S(1)}, f32[3,64,896]{2,1,0:T(8,128)S(1)}, bf16[864,384]{1,0:T(8,128)(2,1)S(1)}, bf16[3,96,128]{2,1,0:T(8,128)(2,1)S(1)}) custom-call(bf16[4,256,128]{2,1,0:T(8,128)(2,1)S(1)} %get-tuple-element.20.own, bf16[3,256,128]{2,1,0:T(8,128)(2,1)S(1)} %collective-permute-done.slab_x, ...), custom_call_target="tpu_custom_call" | custom-call | flops 200000000 | bytes 4000000 | tf_op jit(solution)/shard_map/stem_inner/pallas_call | solution.py:357
  15.7 0.2 all-to-all-done.gathered
  15.9 1.4 %upper_cells.1 = (bf16[64,384]{1,0:T(8,128)(2,1)S(1)}, f32[64,864]{1,0:T(8,128)S(1)}, f32[96,144]{1,0:T(8,128)S(1)}, bf16[64,896]{1,0:T(8,128)(2,1)S(1)}, bf16[1...) custom-call(bf16[4,11,16,128]{3,2,1,0:T(8,128)(2,1)S(1)} %all-to-all-done.gathered, ...), custom_call_target="tpu_custom_call" | custom-call | tf_op jit(solution)/shard_map/upper_cells/pallas_call | solution.py:372
  17.3 0.4 collective-permute-done.1.border
  17.7 1.4 %lower_cells.1 = bf16[4,13,16,128]{3,2,1,0:T(8,128)(2,1)S(1)} custom-call(bf16[4,256,128]{2,1,0:T(8,128)(2,1)S(1)} %get-tuple-element.20.own, bf16[3,256,128]{2,1,0:T(8,128)(2,1)S(1)} %collective-permute-done.slab_x, bf16[7,48,128]{2,1,0:T(8,128)(2,1)S(1)} %collective-permute-done.1.border, bf16[3,128,144]{2,1,0:T(8,128)(2,1)S(1)} %copy-done, ...), custom_call_target="tpu_custom_call" | custom-call | flops 600000000 | bytes 8000000 | tf_op jit(solution)/shard_map/lower_cells/pallas_call | solution.py:388
  19.1 11.0 %all_to_all.10.parts = bf16[4,13,16,128]{3,2,1,0:T(8,128)(2,1)S(1)} all-to-all(bf16[4,13,16,128]{3,2,1,0:T(8,128)(2,1)S(1)} %lower_cells.1), channel_id=1, replica_groups={{2,1,3,0},{6,5,7,4},{10,9,11,8},{14,13,15,12},{18,17,19,16},{22,21,23,2..., dimensions={0} | all-to-all | bytes 425984 | tf_op jit(solution)/shard_map/all_to_all | solution.py:310
  30.2 10.4 %all-gather = bf16[72,16,128]{2,1,0:T(8,128)(2,1)S(1)} all-gather(bf16[9,16,128]{2,1,0:T(8,128)(2,1)S(1)} %sums.1), channel_id=2, replica_groups=mesh['space'=8,'filt'=4] {'space'}, dimensions={0}, use_global_device_ids=true | all-gather | bytes 331776 | tf_op jit(solution)/shard_map/all_gather | solution.py:412
  40.5 0.9 %unpack.1 = (bf16[16,16,128]{2,1,0:T(8,128)(2,1)}, f32[27,16,32]{2,1,0:T(8,128)}, f32[27,4,32]{2,1,0:T(4,128)}) custom-call(bf16[8,9,16,128]{3,2,1,0:T(8,128)(2,1)S(1)} %bitcast.8, bf16[4,13,16,128]{3,2,1,0:T(8,128)(2,1)S(1)} %all_to_all.10.parts), custom_call_target="tpu_custom_call" | custom-call | tf_op jit(solution)/shard_map/unpack/pallas_call | solution.py:413
  (4 shorter events, 0.1 us)
Async XLA Ops:
  3.0 9.1 %collective-permute-start = (bf16[3,256,128]{2,1,0:T(8,128)(2,1)S(1)}, bf16[3,256,128]{2,1,0:T(8,128)(2,1)S(1)}, u32[]{:S(2)}, u32[]{:S(2)}) collective-permute-start(bf16[3,256,128]{2,1,0:T(8,128)(2,1)S(1)} %get-tuple-element.21), channel_id=1, source_target_pairs={{0,4},{4,8},{8,12},{12,16},{16,20},{20,24},{24,28},{1,5},{5,9},{9,... | collective-permute-start | bytes 589832 | tf_op jit(solution)/shard_map/ppermute | solution.py:343
  5.3 10.6 %all-to-all-start = ((bf16[4,11,16,128]{3,2,1,0:T(8,128)(2,1)}), bf16[4,11,16,128]{3,2,1,0:T(8,128)(2,1)S(1)}, u32[]{:S(2)}, u32[]{:S(2)}) async-start(bf16[4,11,16,128]{3,2,1,0:T(8,128)(2,1)} %get-tuple-element.22), calls=%async_computation | async-start | bytes 360448 | tf_op jit(solution)/shard_map/all_to_all | solution.py:310
  12.1 2.6 %copy-start.1 = (bf16[27,4,32]{2,1,0:T(4,128)(2,1)S(1)}, bf16[27,4,32]{2,1,0:T(4,128)(2,1)}, u32[]{:S(2)}) copy-start(bf16[27,4,32]{2,1,0:T(4,128)(2,1)} %param.6) | copy-start | bytes 20740
  12.1 2.8 %copy-start = (bf16[3,128,144]{2,1,0:T(8,128)(2,1)S(1)}, bf16[3,128,144]{2,1,0:T(8,128)(2,1)}, u32[]{:S(2)}) copy-start(bf16[3,128,144]{2,1,0:T(8,128)(2,1)} %constant.5.clone.place) | copy-start | bytes 331780
  12.1 5.6 %collective-permute-start.1 = (bf16[7,48,128]{2,1,0:T(8,128)(2,1)S(1)}, bf16[7,48,128]{2,1,0:T(8,128)(2,1)S(1)}, u32[]{:S(2)}, u32[]{:S(2)}) collective-permute-start(bf16[7,48,128]{2,1,0:T(8,128)(2,1)S(1)} %border.1), channel_id=1, source_target_pairs={{0,1},{1,2},{2,3},{4,5},{5,6},{6,7},{8,9},{9,10},{10,11},{12,13},{... | collective-permute-start | bytes 258056 | tf_op jit(solution)/shard_map/ppermute | solution.py:353

commit v18 on v14

--- a/solution.py
+++ b/solution.py
@@ -51,7 +51,7 @@
     pairs = [(weight_in, weight), (cotangent_in, cotangent)]
     pairs += [(volume_in.at[c], volume.at[c]) for c in range(channels)]
     copies = [pltpu.make_async_copy(*pair, sems.at[k]) for k, pair in enumerate(pairs)]
-    for copy in copies:
+    for copy in copies[2:] + copies[:2]:
         copy.start()
     z, column = rows_lanes((depth, depth))
     source = lax.shift_left(column & (LANES - 1), 2) + lax.shift_right_logical(column, 7)

time: 41.4 us -> 41.5 us (level)
  no operation moved by 1% of the time
where the time goes in v18:
time: 41.5 us; the launch traced here: 41.2 us
  blocking collectives  21.4 us (52%)
  starting transfers between devices  11.7 us (28%)
  Pallas kernels  6.63 us (16%)
  between operations  0.72 us (2%)
  waiting for transfers between devices  0.6 us (1%)
    all_to_all x1, blocking collectives, exchange(): lax.all_to_all(chunks, 'filt', 0, 0, axis_index_groups=groups, tiled=True)  11.1 us
    all_gather x1, blocking collectives, body(): sums = lax.all_gather(sums, 'space')  10.3 us
    all_to_all x1, starting transfers between devices, exchange(): lax.all_to_all(chunks, 'filt', 0, 0, axis_index_groups=groups, tiled=True)  6.76 us
    ppermute x1, starting transfers between devices, body(): border = lax.ppermute(border, 'filt', [(f - 1, f) for f in range(1, filts)])  2.6 us
    ppermute x1, starting transfers between devices, body(): lax.ppermute(slab_x, 'space', [(s - 1, s) for s in range(1, spaces)])  2.37 us
    pallas_call x1, Pallas kernels, body(): pl.pallas_call(regroup_kernel, out_shape=[jax.ShapeDtypeStruct((planes, 1...  2.07 us
    pallas_call x1, Pallas kernels, body(): pl.pallas_call(lower_kernel, out_shape=jax.ShapeDtypeStruct((filts, 13, 1...  1.4 us
    pallas_call x1, Pallas kernels, body(): pl.pallas_call(upper_kernel, out_shape=[jax.ShapeDtypeStruct((64, 3 * LAN...  1.36 us
  transfers between devices with their start and end apart: 3, of which 2 were waited for; matrix products, arithmetic and copies ran while one was open for 0% of the time, Pallas kernels for 5%

profile of v18, /device:TPU:0, one launch (start us, length us, event | category | flops | bytes accessed | tf_op | source)
XLA Modules:
  0.0 41.2 jit_solution(6727146042627452702)
XLA Ops:
  0.6 2.1 %regroup.1 = (bf16[4,256,128]{2,1,0:T(8,128)(2,1)S(1)}, bf16[3,256,128]{2,1,0:T(8,128)(2,1)S(1)}, bf16[4,11,16,128]{3,2,1,0:T(8,128)(2,1)}) custom-call(bf16[4,4,16,512]{3,2,1,0:T(8,128)(2,1)} %volume_in.1, bf16[27,16,32]{2,1,0:T(8,128)(2,1)} %bitcast.9, bf16[16,16,128]{2,1,0:T(8,128)(2,1)} %bitcast.10), custom_call_target="tpu_custom_call" | custom-call | tf_op jit(solution)/shard_map/regroup/pallas_call | solution.py:327
  2.7 2.4 %collective-permute-start = (bf16[3,256,128]{2,1,0:T(8,128)(2,1)S(1)}, bf16[3,256,128]{2,1,0:T(8,128)(2,1)S(1)}, u32[]{:S(2)}, u32[]{:S(2)}) collective-permute-start(bf16[3,256,128]{2,1,0:T(8,128)(2,1)S(1)} %get-tuple-element.21), channel_id=1, source_target_pairs={{0,4},{4,8},{8,12},{12,16},{16,20},{20,24},{24,28},{1,5},{5,9},{9,... | collective-permute-start | bytes 589832 | tf_op jit(solution)/shard_map/ppermute | solution.py:345
  5.1 6.8 %all-to-all-start = ((bf16[4,11,16,128]{3,2,1,0:T(8,128)(2,1)}), bf16[4,11,16,128]{3,2,1,0:T(8,128)(2,1)S(1)}, u32[]{:S(2)}, u32[]{:S(2)}) async-start(bf16[4,11,16,128]{3,2,1,0:T(8,128)(2,1)} %get-tuple-element.22), calls=%async_computation | async-start | bytes 360448 | tf_op jit(solution)/shard_map/all_to_all | solution.py:312
  11.8 0.0 collective-permute-done.slab_x
  11.8 0.0 copy-start.1
  11.8 0.0 copy-start
  11.9 2.6 %collective-permute-start.1 = (bf16[7,48,128]{2,1,0:T(8,128)(2,1)S(1)}, bf16[7,48,128]{2,1,0:T(8,128)(2,1)S(1)}, u32[]{:S(2)}, u32[]{:S(2)}) collective-permute-start(bf16[7,48,128]{2,1,0:T(8,128)(2,1)S(1)} %border.1), channel_id=1, source_target_pairs={{0,1},{1,2},{2,3},{4,5},{5,6},{6,7},{8,9},{9,10},{10,11},{12,13},{... | collective-permute-start | bytes 258056 | tf_op jit(solution)/shard_map/ppermute | solution.py:355
  14.5 0.0 copy-done.1
  14.5 0.1 copy.12
  14.6 0.0 copy-done
  14.6 0.8 %stem_inner.1 = (bf16[96,144]{1,0:T(8,128)(2,1)S(1)}, bf16[7,48,896]{2,1,0:T(8,128)(2,1)S(1)}, f32[3,64,896]{2,1,0:T(8,128)S(1)}, bf16[864,384]{1,0:T(8,128)(2,1)S(1)}, bf16[3,96,128]{2,1,0:T(8,128)(2,1)S(1)}) custom-call(bf16[4,256,128]{2,1,0:T(8,128)(2,1)S(1)} %get-tuple-element.20.own, bf16[3,256,128]{2,1,0:T(8,128)(2,1)S(1)} %collective-permute-done.slab_x, ...), custom_call_target="tpu_custom_call" | custom-call | flops 200000000 | bytes 4000000 | tf_op jit(solution)/shard_map/stem_inner/pallas_call | solution.py:359
  15.5 0.2 all-to-all-done.gathered
  15.7 1.4 %upper_cells.1 = (bf16[64,384]{1,0:T(8,128)(2,1)S(1)}, f32[64,864]{1,0:T(8,128)S(1)}, f32[96,144]{1,0:T(8,128)S(1)}, bf16[64,896]{1,0:T(8,128)(2,1)S(1)}, bf16[1...) custom-call(bf16[4,11,16,128]{3,2,1,0:T(8,128)(2,1)S(1)} %all-to-all-done.gathered, ...), custom_call_target="tpu_custom_call" | custom-call | tf_op jit(solution)/shard_map/upper_cells/pallas_call | solution.py:374
  17.0 0.4 collective-permute-done.1.border
  17.4 1.4 %lower_cells.1 = bf16[4,13,16,128]{3,2,1,0:T(8,128)(2,1)S(1)} custom-call(bf16[4,256,128]{2,1,0:T(8,128)(2,1)S(1)} %get-tuple-element.20.own, bf16[3,256,128]{2,1,0:T(8,128)(2,1)S(1)} %collective-permute-done.slab_x, bf16[7,48,128]{2,1,0:T(8,128)(2,1)S(1)} %collective-permute-done.1.border, bf16[3,128,144]{2,1,0:T(8,128)(2,1)S(1)} %copy-done, ...), custom_call_target="tpu_custom_call" | custom-call | flops 600000000 | bytes 8000000 | tf_op jit(solution)/shard_map/lower_cells/pallas_call | solution.py:390
  18.8 11.1 %all_to_all.10.parts = bf16[4,13,16,128]{3,2,1,0:T(8,128)(2,1)S(1)} all-to-all(bf16[4,13,16,128]{3,2,1,0:T(8,128)(2,1)S(1)} %lower_cells.1), channel_id=1, replica_groups={{2,1,3,0},{6,5,7,4},{10,9,11,8},{14,13,15,12},{18,17,19,16},{22,21,23,2..., dimensions={0} | all-to-all | bytes 425984 | tf_op jit(solution)/shard_map/all_to_all | solution.py:312
  29.9 10.3 %all-gather = bf16[72,16,128]{2,1,0:T(8,128)(2,1)S(1)} all-gather(bf16[9,16,128]{2,1,0:T(8,128)(2,1)S(1)} %sums.1), channel_id=2, replica_groups=mesh['space'=8,'filt'=4] {'space'}, dimensions={0}, use_global_device_ids=true | all-gather | bytes 331776 | tf_op jit(solution)/shard_map/all_gather | solution.py:414
  40.2 0.9 %unpack.1 = (bf16[16,16,128]{2,1,0:T(8,128)(2,1)}, f32[27,16,32]{2,1,0:T(8,128)}, f32[27,4,32]{2,1,0:T(4,128)}) custom-call(bf16[8,9,16,128]{3,2,1,0:T(8,128)(2,1)S(1)} %bitcast.8, bf16[4,13,16,128]{3,2,1,0:T(8,128)(2,1)S(1)} %all_to_all.10.parts), custom_call_target="tpu_custom_call" | custom-call | tf_op jit(solution)/shard_map/unpack/pallas_call | solution.py:415
  (4 shorter events, 0.1 us)
Async XLA Ops:
  2.7 9.1 %collective-permute-start = (bf16[3,256,128]{2,1,0:T(8,128)(2,1)S(1)}, bf16[3,256,128]{2,1,0:T(8,128)(2,1)S(1)}, u32[]{:S(2)}, u32[]{:S(2)}) collective-permute-start(bf16[3,256,128]{2,1,0:T(8,128)(2,1)S(1)} %get-tuple-element.21), channel_id=1, source_target_pairs={{0,4},{4,8},{8,12},{12,16},{16,20},{20,24},{24,28},{1,5},{5,9},{9,... | collective-permute-start | bytes 589832 | tf_op jit(solution)/shard_map/ppermute | solution.py:345
  5.1 10.6 %all-to-all-start = ((bf16[4,11,16,128]{3,2,1,0:T(8,128)(2,1)}), bf16[4,11,16,128]{3,2,1,0:T(8,128)(2,1)S(1)}, u32[]{:S(2)}, u32[]{:S(2)}) async-start(bf16[4,11,16,128]{3,2,1,0:T(8,128)(2,1)} %get-tuple-element.22), calls=%async_computation | async-start | bytes 360448 | tf_op jit(solution)/shard_map/all_to_all | solution.py:312
  11.8 2.6 %copy-start.1 = (bf16[27,4,32]{2,1,0:T(4,128)(2,1)S(1)}, bf16[27,4,32]{2,1,0:T(4,128)(2,1)}, u32[]{:S(2)}) copy-start(bf16[27,4,32]{2,1,0:T(4,128)(2,1)} %param.6) | copy-start | bytes 20740
  11.8 2.8 %copy-start = (bf16[3,128,144]{2,1,0:T(8,128)(2,1)S(1)}, bf16[3,128,144]{2,1,0:T(8,128)(2,1)}, u32[]{:S(2)}) copy-start(bf16[3,128,144]{2,1,0:T(8,128)(2,1)} %constant.5.clone.place) | copy-start | bytes 331780
  11.9 5.6 %collective-permute-start.1 = (bf16[7,48,128]{2,1,0:T(8,128)(2,1)S(1)}, bf16[7,48,128]{2,1,0:T(8,128)(2,1)S(1)}, u32[]{:S(2)}, u32[]{:S(2)}) collective-permute-start(bf16[7,48,128]{2,1,0:T(8,128)(2,1)S(1)} %border.1), channel_id=1, source_target_pairs={{0,1},{1,2},{2,3},{4,5},{5,6},{6,7},{8,9},{9,10},{10,11},{12,13},{... | collective-permute-start | bytes 258056 | tf_op jit(solution)/shard_map/ppermute | solution.py:355

commit v19 on v14

--- a/solution.py
+++ b/solution.py
@@ -46,6 +46,19 @@
     return (source == column).astype(F32).astype(BF16)
 
 
+def depth_phases(rows):
+    count = rows.shape[0]
+    z, column = rows_lanes((256, 256))
+    source = lax.shift_left(column & 63, 2) + lax.shift_right_logical(column, 6)
+    select = (z == source).astype(F32).astype(BF16)
+    halves = jnp.concatenate([rows[:, 0:256], rows[:, 256:512]], axis=0)
+    picked = nn(halves, select)
+    return [
+        jnp.concatenate([picked[h * count : (h + 1) * count, 64 * p : 64 * p + 64] for h in range(2)], axis=1)
+        for p in range(4)
+    ]
+
+
 def regroup_kernel(volume_in, weight_in, cotangent_in, own, slab_x, packed, volume, weight, cotangent, sems):
     channels, planes, width, depth = volume.shape
     pairs = [(weight_in, weight), (cotangent_in, cotangent)]
@@ -53,9 +66,6 @@
     copies = [pltpu.make_async_copy(*pair, sems.at[k]) for k, pair in enumerate(pairs)]
     for copy in copies:
         copy.start()
-    z, column = rows_lanes((depth, depth))
-    source = lax.shift_left(column & (LANES - 1), 2) + lax.shift_right_logical(column, 7)
-    select = (z == source).astype(F32).astype(BF16)
     turn = turn_matrix()
 
     blank = jnp.zeros((16, 32), BF16)
@@ -74,14 +84,14 @@
 
     for copy in copies[2:]:
         copy.wait()
-    picked = nn(volume[...].reshape(channels * planes * width, depth), select).astype(BF16)
+    phases = [part.astype(BF16) for part in depth_phases(volume[...].reshape(channels * planes * width, depth))]
     grouped = []
     for x in range(planes):
         parts = []
-        for phase in range(4):
+        for phase in phases:
             for c in range(channels):
                 start = (c * planes + x) * width
-                parts.append(picked[start : start + width, phase * LANES : (phase + 1) * LANES])
+                parts.append(phase[start : start + width])
         grouped.append(jnp.concatenate(parts, axis=0))
     turned = nn(turn, jnp.concatenate(grouped, axis=1)).astype(BF16)
     for x in range(planes):

time: 41.4 us -> 41.3 us (level)
  no operation moved by 1% of the time
where the time goes in v19:
time: 41.3 us; the launch traced here: 41 us
  blocking collectives  21.4 us (52%)
  starting transfers between devices  11.7 us (28%)
  Pallas kernels  6.46 us (16%)
  between operations  0.72 us (2%)
  waiting for transfers between devices  0.61 us (1%)
    all_to_all x1, blocking collectives, exchange(): lax.all_to_all(chunks, 'filt', 0, 0, axis_index_groups=groups, tiled=True)  11.1 us
    all_gather x1, blocking collectives, body(): sums = lax.all_gather(sums, 'space')  10.3 us
    all_to_all x1, starting transfers between devices, exchange(): lax.all_to_all(chunks, 'filt', 0, 0, axis_index_groups=groups, tiled=True)  6.76 us
    ppermute x1, starting transfers between devices, body(): border = lax.ppermute(border, 'filt', [(f - 1, f) for f in range(1, filts)])  2.6 us
    ppermute x1, starting transfers between devices, body(): lax.ppermute(slab_x, 'space', [(s - 1, s) for s in range(1, spaces)])  2.37 us
    pallas_call x1, Pallas kernels, body(): pl.pallas_call(regroup_kernel, out_shape=[jax.ShapeDtypeStruct((planes, 1...  1.9 us
    pallas_call x1, Pallas kernels, body(): pl.pallas_call(lower_kernel, out_shape=jax.ShapeDtypeStruct((filts, 13, 1...  1.4 us
    pallas_call x1, Pallas kernels, body(): pl.pallas_call(upper_kernel, out_shape=[jax.ShapeDtypeStruct((64, 3 * LAN...  1.36 us
  transfers between devices with their start and end apart: 3, of which 2 were waited for; matrix products, arithmetic and copies ran while one was open for 0% of the time, Pallas kernels for 5%

profile of v19, /device:TPU:0, one launch (start us, length us, event | category | flops | bytes accessed | tf_op | source)
XLA Modules:
  0.0 41.0 jit_solution(11128691204517483271)
XLA Ops:
  0.6 1.9 %regroup.1 = (bf16[4,256,128]{2,1,0:T(8,128)(2,1)S(1)}, bf16[3,256,128]{2,1,0:T(8,128)(2,1)S(1)}, bf16[4,11,16,128]{3,2,1,0:T(8,128)(2,1)}) custom-call(bf16[4,4,16,512]{3,2,1,0:T(8,128)(2,1)} %volume_in.1, bf16[27,16,32]{2,1,0:T(8,128)(2,1)} %bitcast.9, bf16[16,16,128]{2,1,0:T(8,128)(2,1)} %bitcast.10), custom_call_target="tpu_custom_call" | custom-call | tf_op jit(solution)/shard_map/regroup/pallas_call | solution.py:337
  2.5 2.4 %collective-permute-start = (bf16[3,256,128]{2,1,0:T(8,128)(2,1)S(1)}, bf16[3,256,128]{2,1,0:T(8,128)(2,1)S(1)}, u32[]{:S(2)}, u32[]{:S(2)}) collective-permute-start(bf16[3,256,128]{2,1,0:T(8,128)(2,1)S(1)} %get-tuple-element.21), channel_id=1, source_target_pairs={{0,4},{4,8},{8,12},{12,16},{16,20},{20,24},{24,28},{1,5},{5,9},{9,... | collective-permute-start | bytes 589832 | tf_op jit(solution)/shard_map/ppermute | solution.py:355
  4.9 6.8 %all-to-all-start = ((bf16[4,11,16,128]{3,2,1,0:T(8,128)(2,1)}), bf16[4,11,16,128]{3,2,1,0:T(8,128)(2,1)S(1)}, u32[]{:S(2)}, u32[]{:S(2)}) async-start(bf16[4,11,16,128]{3,2,1,0:T(8,128)(2,1)} %get-tuple-element.22), calls=%async_computation | async-start | bytes 360448 | tf_op jit(solution)/shard_map/all_to_all | solution.py:322
  11.7 0.0 collective-permute-done.slab_x
  11.7 0.0 copy-start.1
  11.7 0.0 copy-start
  11.7 2.6 %collective-permute-start.1 = (bf16[7,48,128]{2,1,0:T(8,128)(2,1)S(1)}, bf16[7,48,128]{2,1,0:T(8,128)(2,1)S(1)}, u32[]{:S(2)}, u32[]{:S(2)}) collective-permute-start(bf16[7,48,128]{2,1,0:T(8,128)(2,1)S(1)} %border.1), channel_id=1, source_target_pairs={{0,1},{1,2},{2,3},{4,5},{5,6},{6,7},{8,9},{9,10},{10,11},{12,13},{... | collective-permute-start | bytes 258056 | tf_op jit(solution)/shard_map/ppermute | solution.py:365
  14.3 0.0 copy-done.1
  14.3 0.1 copy.12
  14.4 0.0 copy-done
  14.5 0.8 %stem_inner.1 = (bf16[96,144]{1,0:T(8,128)(2,1)S(1)}, bf16[7,48,896]{2,1,0:T(8,128)(2,1)S(1)}, f32[3,64,896]{2,1,0:T(8,128)S(1)}, bf16[864,384]{1,0:T(8,128)(2,1)S(1)}, bf16[3,96,128]{2,1,0:T(8,128)(2,1)S(1)}) custom-call(bf16[4,256,128]{2,1,0:T(8,128)(2,1)S(1)} %get-tuple-element.20.own, bf16[3,256,128]{2,1,0:T(8,128)(2,1)S(1)} %collective-permute-done.slab_x, ...), custom_call_target="tpu_custom_call" | custom-call | flops 200000000 | bytes 4000000 | tf_op jit(solution)/shard_map/stem_inner/pallas_call | solution.py:369
  15.3 0.2 all-to-all-done.gathered
  15.5 1.4 %upper_cells.1 = (bf16[64,384]{1,0:T(8,128)(2,1)S(1)}, f32[64,864]{1,0:T(8,128)S(1)}, f32[96,144]{1,0:T(8,128)S(1)}, bf16[64,896]{1,0:T(8,128)(2,1)S(1)}, bf16[1...) custom-call(bf16[4,11,16,128]{3,2,1,0:T(8,128)(2,1)S(1)} %all-to-all-done.gathered, ...), custom_call_target="tpu_custom_call" | custom-call | tf_op jit(solution)/shard_map/upper_cells/pallas_call | solution.py:384
  16.9 0.4 collective-permute-done.1.border
  17.3 1.4 %lower_cells.1 = bf16[4,13,16,128]{3,2,1,0:T(8,128)(2,1)S(1)} custom-call(bf16[4,256,128]{2,1,0:T(8,128)(2,1)S(1)} %get-tuple-element.20.own, bf16[3,256,128]{2,1,0:T(8,128)(2,1)S(1)} %collective-permute-done.slab_x, bf16[7,48,128]{2,1,0:T(8,128)(2,1)S(1)} %collective-permute-done.1.border, bf16[3,128,144]{2,1,0:T(8,128)(2,1)S(1)} %copy-done, ...), custom_call_target="tpu_custom_call" | custom-call | flops 600000000 | bytes 8000000 | tf_op jit(solution)/shard_map/lower_cells/pallas_call | solution.py:400
  18.7 11.1 %all_to_all.10.parts = bf16[4,13,16,128]{3,2,1,0:T(8,128)(2,1)S(1)} all-to-all(bf16[4,13,16,128]{3,2,1,0:T(8,128)(2,1)S(1)} %lower_cells.1), channel_id=1, replica_groups={{2,1,3,0},{6,5,7,4},{10,9,11,8},{14,13,15,12},{18,17,19,16},{22,21,23,2..., dimensions={0} | all-to-all | bytes 425984 | tf_op jit(solution)/shard_map/all_to_all | solution.py:322
  29.8 10.3 %all-gather = bf16[72,16,128]{2,1,0:T(8,128)(2,1)S(1)} all-gather(bf16[9,16,128]{2,1,0:T(8,128)(2,1)S(1)} %sums.1), channel_id=2, replica_groups=mesh['space'=8,'filt'=4] {'space'}, dimensions={0}, use_global_device_ids=true | all-gather | bytes 331776 | tf_op jit(solution)/shard_map/all_gather | solution.py:424
  40.1 0.9 %unpack.1 = (bf16[16,16,128]{2,1,0:T(8,128)(2,1)}, f32[27,16,32]{2,1,0:T(8,128)}, f32[27,4,32]{2,1,0:T(4,128)}) custom-call(bf16[8,9,16,128]{3,2,1,0:T(8,128)(2,1)S(1)} %bitcast.8, bf16[4,13,16,128]{3,2,1,0:T(8,128)(2,1)S(1)} %all_to_all.10.parts), custom_call_target="tpu_custom_call" | custom-call | tf_op jit(solution)/shard_map/unpack/pallas_call | solution.py:425
  (4 shorter events, 0.1 us)
Async XLA Ops:
  2.5 9.1 %collective-permute-start = (bf16[3,256,128]{2,1,0:T(8,128)(2,1)S(1)}, bf16[3,256,128]{2,1,0:T(8,128)(2,1)S(1)}, u32[]{:S(2)}, u32[]{:S(2)}) collective-permute-start(bf16[3,256,128]{2,1,0:T(8,128)(2,1)S(1)} %get-tuple-element.21), channel_id=1, source_target_pairs={{0,4},{4,8},{8,12},{12,16},{16,20},{20,24},{24,28},{1,5},{5,9},{9,... | collective-permute-start | bytes 589832 | tf_op jit(solution)/shard_map/ppermute | solution.py:355
  4.9 10.6 %all-to-all-start = ((bf16[4,11,16,128]{3,2,1,0:T(8,128)(2,1)}), bf16[4,11,16,128]{3,2,1,0:T(8,128)(2,1)S(1)}, u32[]{:S(2)}, u32[]{:S(2)}) async-start(bf16[4,11,16,128]{3,2,1,0:T(8,128)(2,1)} %get-tuple-element.22), calls=%async_computation | async-start | bytes 360448 | tf_op jit(solution)/shard_map/all_to_all | solution.py:322
  11.7 2.6 %copy-start.1 = (bf16[27,4,32]{2,1,0:T(4,128)(2,1)S(1)}, bf16[27,4,32]{2,1,0:T(4,128)(2,1)}, u32[]{:S(2)}) copy-start(bf16[27,4,32]{2,1,0:T(4,128)(2,1)} %param.6) | copy-start | bytes 20740
  11.7 2.8 %copy-start = (bf16[3,128,144]{2,1,0:T(8,128)(2,1)S(1)}, bf16[3,128,144]{2,1,0:T(8,128)(2,1)}, u32[]{:S(2)}) copy-start(bf16[3,128,144]{2,1,0:T(8,128)(2,1)} %constant.5.clone.place) | copy-start | bytes 331780
  11.7 5.6 %collective-permute-start.1 = (bf16[7,48,128]{2,1,0:T(8,128)(2,1)S(1)}, bf16[7,48,128]{2,1,0:T(8,128)(2,1)S(1)}, u32[]{:S(2)}, u32[]{:S(2)}) collective-permute-start(bf16[7,48,128]{2,1,0:T(8,128)(2,1)S(1)} %border.1), channel_id=1, source_target_pairs={{0,1},{1,2},{2,3},{4,5},{5,6},{6,7},{8,9},{9,10},{10,11},{12,13},{... | collective-permute-start | bytes 258056 | tf_op jit(solution)/shard_map/ppermute | solution.py:365
